TPU v7x, 768 devices: a whole 4x8x12 slice. The times are simulated.
768 devices in a mesh: col: 96 (over z, y_hi, x), row: 8 (over y_lo, core).
Axes of the slice: x: 4, y: 8 (y_hi: 2, y_lo: 4; y = y_hi * 4 + y_lo), z: 12, core: 2. Of those that a mesh axis runs over, the one named last changes fastest.
Arguments:
- picture_vectors: bfloat16 [147456, 1152], P(('col', 'row')), may hold values from -0.19921875 to 0.19921875
- caption_features: bfloat16 [147456, 1152], P(('col', 'row')), may hold values from -0.19921875 to 0.19921875
- matched_caption_slot: int32 [768, 192], P(('col', 'row')), may hold values from 0 to 191, each once within a row
- caption_mapper_matrix: bfloat16 [1152, 1152], replicated, may hold values from -0.1875 to 0.1875
- mapper_intercept: float32 [1152], replicated, may hold values from -0.2 to 0.2
- sharpness_factor: float32 [1], replicated, may hold values from 2 to 6
- score_shift_vector: float32 [1], replicated, may hold values from -2 to 0
Outputs:
- image_grad: float32 [147456, 1152], P(('col', 'row'))
- text_grad: float32 [147456, 1152], P(('col', 'row'))
- head_grad: float32 [1152, 1152], P('row')
- bias_grad: float32 [1152], P('row')
Inputs may be any that keep to these rules, and one draw needn't show every extreme that they name: `matched_caption_slot`: each row of 192 entries holds every number of 0 to 191 once.
All inputs are finite; a program needn't handle non-finite values.
Results may differ from a plain program's by a relative error of at most 0.025.
Values may be sent and summed in bfloat16 or wider, within the bound.
No kernel may reach another device: no remote copies, remote signals or barrier semaphores. Data moves between devices by JAX's collectives and lax.ppermute only.
A program may use at most 64 MiB of HBM per device.

v0:
```python
import jax
import jax.numpy as jnp
from jax import lax
from jax.sharding import PartitionSpec as P

eps = 1e-06


def shifted(block, axis, distance):
    devices = range(lax.axis_size(axis))
    route = [((i - distance) % len(devices), i) for i in devices]
    return lax.ppermute(block, axis, route)


def unit_rows(values):
    scale = lax.rsqrt(jnp.sum(values * values, -1, keepdims=True) + eps)
    return (values * scale, scale)


def unit_back(grad, unit, scale):
    return (grad - unit * jnp.sum(unit * grad, -1, keepdims=True)) * scale


def per_device(
    picture_vectors,
    caption_features,
    matched_caption_slot,
    caption_mapper_matrix,
    mapper_intercept,
    sharpness_factor,
    score_shift_vector,
):
    score_sharpness = sharpness_factor[0]
    cyclic_displacement = score_shift_vector[0]
    rows = picture_vectors.shape[0]
    mine = lax.axis_index("row")
    paired_texts = shifted(caption_features, "col", 1)
    projected = (
        jnp.dot(paired_texts, caption_mapper_matrix, preferred_element_type=jnp.float32)
        + mapper_intercept
    )
    text_unit_embedding, text_scale = unit_rows(projected)
    image_unit, image_scale = unit_rows(picture_vectors.astype(jnp.float32))
    caption_reduced = text_unit_embedding.astype(jnp.bfloat16)
    picture_reduced = image_unit.astype(jnp.bfloat16)
    target = mine * rows + matched_caption_slot[0]
    every_caption = lax.all_gather(caption_reduced, "row", axis=0, tiled=True)
    similarity_grid = (
        score_sharpness
        * lax.dot_general(
            picture_reduced,
            every_caption,
            (((1,), (1,)), ((), ())),
            preferred_element_type=jnp.float32,
        )
        + cyclic_displacement
    )
    columns = jnp.arange(every_caption.shape[0], dtype=jnp.int32)
    positive = target[:, None] == columns[None, :]
    sign = jnp.where(positive, 1.0, -1.0).astype(jnp.float32)
    coefficient_entry = (-sign * jax.nn.sigmoid(-sign * similarity_grid)).astype(jnp.bfloat16)
    picture_direction = score_sharpness * jnp.dot(
        coefficient_entry, every_caption, preferred_element_type=jnp.float32
    )
    text_dir = lax.psum_scatter(
        (
            score_sharpness
            * lax.dot_general(
                coefficient_entry,
                picture_reduced,
                (((0,), (0,)), ((), ())),
                preferred_element_type=jnp.float32,
            )
        ).astype(jnp.bfloat16),
        "row",
        scatter_dimension=0,
        tiled=True,
    ).astype(jnp.float32)
    image_grad = unit_back(picture_direction, image_unit, image_scale)
    projected_text_gradient = unit_back(text_dir, text_unit_embedding, text_scale).astype(
        jnp.bfloat16
    )
    text_grad = lax.dot_general(
        projected_text_gradient,
        caption_mapper_matrix,
        (((1,), (1,)), ((), ())),
        preferred_element_type=jnp.float32,
    )
    head_term = lax.dot_general(
        paired_texts,
        projected_text_gradient,
        (((0,), (0,)), ((), ())),
        preferred_element_type=jnp.float32,
    )
    bias_term = jnp.sum(projected_text_gradient.astype(jnp.float32), 0)
    head_part, bias_part = (
        lax.psum_scatter(
            head_term.astype(jnp.bfloat16), "row", scatter_dimension=0, tiled=True
        ).astype(jnp.float32),
        lax.psum_scatter(
            bias_term.astype(jnp.bfloat16), "row", scatter_dimension=0, tiled=True
        ).astype(jnp.float32),
    )
    head_grad, bias_grad = lax.psum((head_part, bias_part), "col")
    return (image_grad, text_grad, head_grad, bias_grad)


def solution(mesh):
    in_specs = (
        P(("col", "row"), None),
        P(("col", "row"), None),
        P(("col", "row"), None),
        P(),
        P(),
        P(),
        P(),
    )
    out_specs = (P(("col", "row"), None), P(("col", "row"), None), P("row", None), P("row"))
    return jax.shard_map(
        per_device, mesh=mesh, in_specs=in_specs, out_specs=out_specs, check_vma=False
    )
```

profile of v0, /device:TPU:56, one launch (start us, length us, event | category | flops | bytes accessed | tf_op | source)
XLA Modules:
  0.0 879.1 jit_solution(11543004793291168587)
XLA Ops:
  7.2 0.0 all-gather.2.cloned.1.call-start
  7.2 3.5 collective-permute-start
  10.8 16.7 %collective-permute-done = bf16[192,1152]{1,0:T(8,128)(2,1)S(1)} collective-permute-done((bf16[192,1152]{1,0:T(8,128)(2,1)}, bf16[192,1152]{1,0:T(8,128)(2,1)S(1)}, u32[]{:S(2)}, u32[]{:S(2)}) %collective-permute-start) | collective-permute-done | bytes 442400 | tf_op jit(solution)/shard_map/ppermute | solution.py:12
  27.5 0.8 copy-done.5
  28.3 1.6 multiply_reduce_fusion
  29.9 0.9 multiply_convert_fusion
  30.8 0.0 all-gather.2.cloned.1.call-update
  30.8 0.0 reduce-scatter.5.cloned.1.call-start
  32.1 1.2 fusion.16
  33.4 61.6 %all-gather.2.cloned.1.call-done = bf16[1536,1152]{1,0:T(8,128)(2,1)} async-done(((bf16[192,1152]{1,0:T(8,128)(2,1)}), bf16[1536,1152]{1,0:T(8,128)(2,1)}) %all-gather.2.cloned.1.call-update) | async-done | bytes 3538960 | tf_op jit(solution)/shard_map/all_gather | solution.py:47
  95.0 3.7 fusion.9
  98.7 0.8 copy-done.8
  99.5 3.1 fusion
  102.6 0.0 reduce-scatter.5.cloned.1.call-update
  102.6 0.0 reduce-scatter.7.cloned.1.call-start
  102.7 53.5 %reduce-scatter.5.cloned.1.call-done = bf16[192,1152]{1,0:T(8,128)(2,1)} async-done(((bf16[1536,1152]{1,0:T(8,128)(2,1)}), bf16[192,1152]{1,0:T(8,128)(2,1)}) %reduce-scatter.5.cloned.1.call-update) | async-done | bytes 442384 | tf_op jit(solution)/shard_map/reduce_scatter | solution.py:65
  156.2 1.3 fusion.17
  157.5 1.3 fusion.22
  158.8 0.8 copy-done.1
  159.6 2.6 fusion.1
  162.2 5.2 copy.13
  167.4 0.0 reduce-scatter.7.cloned.1.call-update
  167.4 1.3 dynamic-slice
  169.4 3.3 fusion.13
  172.7 1.1 fusion.15
  173.8 14.3 %all-reduce = bf16[1152]{0:T(1024)(128)(2,1)S(1)} all-reduce(bf16[1152]{0:T(1024)(128)(2,1)S(1)} %get-tuple-element.14), channel_id=4, replica_groups=mesh['col'=96,'row'=8] {'row'}, use_global_device_ids=true, to_apply=%region_8.9.clone | all-reduce | flops 1152 | bytes 4608
  188.1 0.1 dynamic-slice_convert_fusion
  188.2 1.9 fusion.24
  190.1 25.4 %reduce-scatter.7.cloned.1.call-done = bf16[144,1152]{1,0:T(8,128)(2,1)} async-done(((bf16[1152,1152]{1,0:T(8,128)(2,1)}), bf16[144,1152]{1,0:T(8,128)(2,1)}) %reduce-scatter.7.cloned.1.call-update) | async-done | bytes 331792
  215.5 1.2 copy.14
  216.7 653.4 %all-reduce.3 = (f32[144,1152]{0,1:T(8,128)}, f32[144]{0:T(256)}) all-reduce(bf16[144,1152]{0,1:T(8,128)(2,1)S(1)} %copy.14, f32[144]{0:T(256)S(1)} %dynamic-slice_convert_fusion), channel_id=1, replica_groups=mesh['col'=96,'row'=8] {'col'}, use_global_device_ids=true, to_apply=%region_6.7 | all-reduce | flops 166032 | bytes 996480 | tf_op jit(solution)/shard_map/psum | solution.py:104
  870.1 2.4 copy.12
  (18 shorter events, 0.1 us)
Async XLA Ops:
  7.2 21.1 %copy-start = (bf16[1152,1152]{1,0:T(8,128)(2,1)S(1)}, bf16[1152,1152]{1,0:T(8,128)(2,1)}, u32[]{:S(2)}) copy-start(bf16[1152,1152]{1,0:T(8,128)(2,1)} %param.10) | copy-start | bytes 7962628
  7.2 26.2 %copy-start.7 = (s32[1,192]{1,0:T(1,128)S(1)}, s32[1,192]{1,0:T(1,128)}, u32[]{:S(2)}) copy-start(s32[1,192]{1,0:T(1,128)} %param.9) | copy-start | bytes 2308
  7.2 87.8 %all-gather.2.cloned.1.call-start = ((), (), s32[]{:S(2)}) async-start(), calls=%async_computation.2 | async-start | bytes 3981312 | tf_op jit(solution)/shard_map/all_gather | solution.py:47
  7.2 20.3 %collective-permute-start = (bf16[192,1152]{1,0:T(8,128)(2,1)}, bf16[192,1152]{1,0:T(8,128)(2,1)S(1)}, u32[]{:S(2)}, u32[]{:S(2)}) collective-permute-start(bf16[192,1152]{1,0:T(8,128)(2,1)} %param.8), channel_id=1, source_target_pairs={{760,0},{0,8},{8,16},{16,24},{24,32},{32,40},{40,48},{48,56},{56,6... | collective-permute-start | bytes 1327112 | tf_op jit(solution)/shard_map/ppermute | solution.py:12
  27.5 0.8 copy-start.5
  30.8 125.4 %reduce-scatter.5.cloned.1.call-start = ((), (), s32[]{:S(2)}) async-start(), calls=%async_computation.3 | async-start | bytes 3981312 | tf_op jit(solution)/shard_map/reduce_scatter | solution.py:65
  95.0 4.5 copy-start.3
  98.7 0.8 copy-start.8
  102.6 112.9 %reduce-scatter.7.cloned.1.call-start = ((), (), s32[]{:S(2)}) async-start(), calls=%async_computation.4 | async-start | bytes 2985984
  156.2 3.4 copy-start.6
  158.8 0.8 copy-start.1
  167.4 2.0 copy-start.4
  169.4 18.8 %copy-start.2 = (bf16[192,1152]{1,0:T(8,128)(2,1)S(1)}, bf16[192,1152]{1,0:T(8,128)(2,1)}, u32[]{:S(2)}) copy-start(bf16[192,1152]{1,0:T(8,128)(2,1)} %copy-done.1) | copy-start | bytes 1327108
Sparse Core Ops, SparseCore 0:
  30.9 64.0 all-gather.1
  102.8 53.3 reduce-scatter.4
  167.5 47.9 reduce-scatter.6
where the time goes:
time: 893 us; the launch traced here: 879 us
  blocking collectives  668 us (75%)
  waiting for transfers between devices  157 us (18%)
  matrix products  16.2 us (2%)
  between operations  15.8 us (2%)
  local copies, waits for them, and re-layouts  12.6 us (1%)
    psum x1, blocking collectives, per_device(): head_grad, bias_grad = lax.psum((head_part, bias_part), 'col')  653 us
    all_gather x1, waiting for transfers between devices, per_device(): every_caption = lax.all_gather(caption_reduced, 'row', axis=0, tiled=True)  61.6 us
    reduce_scatter x1, waiting for transfers between devices, per_device(): lax.psum_scatter((score_sharpness * lax.dot_general(coefficient_entry, pi...  53.5 us
    unnamed x4, waiting for transfers between devices  25.4 us
  transfers between devices with their start and end apart: 4, of which 4 were waited for; matrix products, arithmetic and copies ran while one was open for 1% of the time, Pallas kernels for 0%

commit v1 on v0

v1 whole, which is shorter than its diff:
```python
import jax
import jax.numpy as jnp
from jax import lax
from jax.sharding import PartitionSpec as P

eps = 1e-06
AXES = ("z", "h", "x", "y", "k")
COL = AXES[:3]
SIZES = (12, 2, 4, 4, 2)
D = 1152
PART = 36
PAD = 40
f32, bf16 = jnp.float32, jnp.bfloat16


def swap(block, axis, mask):
    n = lax.axis_size(axis)
    return lax.ppermute(block, axis, [(i, i ^ mask) for i in range(n)])


def turn(block, axis, distance):
    n = lax.axis_size(axis)
    return lax.ppermute(block, axis, [(i, (i + distance) % n) for i in range(n)])


def low(values):
    return lax.reduce_precision(values, 8, 7).astype(bf16)


def dot(a, b, ca, cb):
    return lax.dot_general(a, b, (((ca,), (cb,)), ((), ())), preferred_element_type=f32)


def halve(both, bit, axis, mask):
    sent = lax.dynamic_index_in_dim(both, 1 - bit, 0, keepdims=False)
    kept = lax.dynamic_index_in_dim(both, bit, 0, keepdims=False)
    return low(kept.astype(f32) + swap(sent, axis, mask).astype(f32))


def join(own, bit, axis, mask):
    other = swap(own, axis, mask)
    first = jnp.where(bit == 0, own, other)
    second = jnp.where(bit == 0, other, own)
    return jnp.stack([first, second])


def spread_matrix():
    place = jnp.arange(32 * PAD, dtype=jnp.int32)
    part, i = place // PAD, place % PAD
    k, q, b, a = part // 16, part // 4 % 4, part // 2 % 2, part % 2
    feature = jnp.where(i < PART, ((2 * a + b) * 2 + k) * 144 + q * PART + i, -1)
    matrix = (jnp.arange(D, dtype=jnp.int32)[:, None] == feature[None, :]).astype(bf16)
    return matrix, (i == PART).astype(f32)


def per_device(pictures, captions, slot, matrix, intercept, sharpness, score_shift):
    sharp, moved = sharpness[0], score_shift[0]
    rows = pictures.shape[0]
    z, x, y, k = (lax.axis_index(a) for a in ("z", "x", "y", "k"))

    paired = turn_col(captions)
    picture = pictures.astype(f32)
    image_scale = lax.rsqrt(jnp.sum(picture * picture, -1, keepdims=True) + eps)
    image_unit = picture * image_scale
    image_low = image_unit.astype(bf16)
    pair = jnp.concatenate([image_low, swap(image_low, "y", 2)])
    images = jnp.concatenate([pair, swap(pair, "k", 1)])
    texts = jnp.concatenate([paired, swap(paired, "y", 1)])

    projected = dot(texts, matrix, 1, 0) + intercept
    text_scale = lax.rsqrt(jnp.sum(projected * projected, -1, keepdims=True) + eps)
    text_unit = projected * text_scale
    text_low = text_unit.astype(bf16)
    spread, ones = spread_matrix()
    texts_spread = (dot(texts, spread, 1, 0) + ones).astype(bf16)

    scores = sharp * dot(images, text_low, 1, 1) + moved
    wanted = jnp.concatenate([slot[0], jnp.full((3 * rows,), -1, jnp.int32)])
    positive = wanted[:, None] == jnp.arange(2 * rows, dtype=jnp.int32)[None, :]
    sign = jnp.where(positive, 1.0, -1.0).astype(f32)
    weight = (-sign * jax.nn.sigmoid(-sign * scores)).astype(bf16)

    text_dir = sharp * dot(weight, images, 0, 0)
    along = jnp.sum(text_unit * text_dir, -1, keepdims=True)
    grad = (text_dir - text_unit * along) * text_scale
    grad_low = low(grad)

    head = dot(texts_spread, grad_low, 0, 0).astype(bf16).reshape(2, 2, 2, 2, 2, PAD, D)
    head = halve(head, k, "k", 1)
    head = halve(head, (x // 2) ^ (x % 2), "x", 1)
    head = halve(head, x // 2, "x", 3)
    head = halve(head, y % 2, "y", 1)
    head = halve(head, y // 2, "y", 2)
    head = low(head.astype(f32) + swap(head, "h", 1).astype(f32))
    head = low(head.astype(f32) + swap(head, "z", 1).astype(f32))
    head = low(head.astype(f32) + swap(head, "z", 2).astype(f32))
    ring = [head, turn(head, "z", 8), turn(head, "z", 4)]
    u = z // 4
    total = 0.0
    for j in range(3):
        at = (j - u) % 3
        total = total + jnp.where(at == 0, ring[0], jnp.where(at == 1, ring[1], ring[2])).astype(f32)
    head = low(total)
    head = join(head, x // 2, "x", 3)
    head = join(head, (x // 2) ^ (x % 2), "x", 1).reshape(4, PAD, D)
    head_grad = head[:, :PART].reshape(4 * PART, D).astype(f32)
    bias_grad = lax.dynamic_slice(head[0, PART].astype(f32), ((2 * y + k) * 144,), (144,))

    projected_grad = grad_low[:rows].astype(f32) + swap(grad_low[rows:], "y", 1).astype(f32)
    text_grad = dot(projected_grad.astype(bf16), matrix, 1, 1)

    image_dir = sharp * dot(weight, text_low, 1, 0)
    mine = image_dir[: 2 * rows] + swap(image_dir[2 * rows :].astype(bf16), "k", 1).astype(f32)
    own = mine[:rows] + swap(mine[rows:].astype(bf16), "y", 2).astype(f32)
    along = jnp.sum(image_unit * own, -1, keepdims=True)
    image_grad = (own - image_unit * along) * image_scale
    return (image_grad, text_grad, head_grad, bias_grad)


def turn_col(block):
    return lax.ppermute(block, COL, [((i - 1) % 96, i) for i in range(96)])


def solution(mesh):
    fine = jax.sharding.Mesh(mesh.devices.reshape(SIZES), AXES)
    rows = P(AXES, None)
    in_specs = (rows, rows, rows, P(), P(), P(), P())
    out_specs = (rows, rows, P(("y", "k"), None), P(("y", "k")))
    return jax.shard_map(
        per_device, mesh=fine, in_specs=in_specs, out_specs=out_specs, check_vma=False
    )
```

time: 893 us -> 219 us (0.25); the launches traced: 879 us -> 216 us
  blocking collectives: 668 us -> 0 us
  starting transfers between devices: 3.65 us -> 84.8 us
  waiting for transfers between devices: 157 us -> 85.9 us
  between operations: 15.8 us -> 2.62 us
    psum x1 -> x0, blocking collectives: 653 us -> none  [per_device(): head_grad, bias_grad = lax.psum((head_part, bias_part), 'col')]
    ppermute x1 -> x19, starting transfers between devices: 3.53 us -> 84.8 us  [the longest x16 67.3 us: swap(): return lax.ppermute(block, axis, [(i, i ^ mask) for i in range(n)])]
    ppermute x1 -> x19, waiting for transfers between devices: 16.7 us -> 85.9 us  [the longest x16 71.4 us: swap(): return lax.ppermute(block, axis, [(i, i ^ mask) for i in range(n)])]
    all_gather x1 -> x0, waiting for transfers between devices: 61.6 us -> none  [per_device(): every_caption = lax.all_gather(caption_reduced, 'row', axis=0, tiled=True)]
    reduce_scatter x1 -> x0, waiting for transfers between devices: 53.5 us -> none  [per_device(): lax.psum_scatter((score_sharpness * lax.dot_general(coefficient_entry, pi...]
    unnamed x4 -> x0, waiting for transfers between devices: 25.4 us -> none
    unnamed x1 -> x0, blocking collectives: 14.3 us -> none
    convert_element_type x2 -> x14, other arithmetic: 0.97 us -> 11.4 us  [the longest x10 8.94 us: low(): return lax.reduce_precision(values, 8, 7).astype(bf16)]
  transfers between devices with their start and end apart: 4 -> 19, of which waited for: 4 -> 12; matrix products, arithmetic and copies ran while one was open for 1% -> 7% of each run, Pallas kernels for 0% -> 0%
where the time goes in v1:
time: 219 us; the launch traced here: 216 us
  waiting for transfers between devices  85.9 us (39%)
  starting transfers between devices  84.8 us (39%)
  matrix products  15.4 us (7%)
  other arithmetic  14.5 us (7%)
  local copies, waits for them, and re-layouts  12.5 us (6%)
  between operations  2.62 us (1%)
    ppermute x16, waiting for transfers between devices, swap(): return lax.ppermute(block, axis, [(i, i ^ mask) for i in range(n)])  71.4 us
    ppermute x16, starting transfers between devices, swap(): return lax.ppermute(block, axis, [(i, i ^ mask) for i in range(n)])  67.3 us
    dot_general x6, matrix products, dot(): lax.dot_general(a, b, (((ca,), (cb,)), ((), ())), preferred_element_type=...  15.4 us
    ppermute x2, starting transfers between devices, turn(): lax.ppermute(block, axis, [(i, (i + distance) % n) for i in range(n)])  13.9 us
    convert_element_type x10, other arithmetic, low(): return lax.reduce_precision(values, 8, 7).astype(bf16)  8.94 us
    ppermute x1, waiting for transfers between devices, turn_col(): return lax.ppermute(block, COL, [((i - 1) % 96, i) for i in range(96)])  8.39 us
    ppermute x2, waiting for transfers between devices, turn(): lax.ppermute(block, axis, [(i, (i + distance) % n) for i in range(n)])  6.09 us
    squeeze x5, local copies, waits for them, and re-layouts, halve(): sent = lax.dynamic_index_in_dim(both, 1 - bit, 0, keepdims=False)  5.63 us
  transfers between devices with their start and end apart: 19, of which 12 were waited for; matrix products, arithmetic and copies ran while one was open for 7% of the time, Pallas kernels for 0%

profile of v1, /device:TPU:56, one launch (start us, length us, event | category | flops | bytes accessed | tf_op | source)
XLA Modules:
  0.0 215.7 jit_solution(12513182390991456657)
XLA Ops:
  0.6 3.7 %collective-permute-start.2 = (bf16[192,1152]{1,0:T(8,128)(2,1)}, bf16[192,1152]{1,0:T(8,128)(2,1)}, u32[]{:S(2)}, u32[]{:S(2)}) collective-permute-start(bf16[192,1152]{1,0:T(8,128)(2,1)} %param.8), channel_id=1, source_target_pairs={{760,0},{0,8},{8,16},{16,24},{24,32},{32,40},{40,48},{48,56},{56,6... | collective-permute-start | bytes 1327112 | tf_op jit(solution)/shard_map/ppermute | solution.py:121
  6.7 4.0 %collective-permute-start = (bf16[192,1152]{1,0:T(8,128)(2,1)S(1)}, bf16[192,1152]{1,0:T(8,128)(2,1)S(1)}, u32[]{:S(2)}, u32[]{:S(2)}) collective-permute-start(bf16[192,1152]{1,0:T(8,128)(2,1)S(1)} %fusion.18), channel_id=1, source_target_pairs={{0,4},{2,6},{4,0},{6,2},{1,5},{3,7},{5,1},{7,3},{8,12},{10,14},{12... | collective-permute-start | bytes 1327112 | tf_op jit(solution)/shard_map/ppermute | solution.py:18
  13.9 8.4 %collective-permute-done.2 = bf16[192,1152]{1,0:T(8,128)(2,1)} collective-permute-done((bf16[192,1152]{1,0:T(8,128)(2,1)}, bf16[192,1152]{1,0:T(8,128)(2,1)}, u32[]{:S(2)}, u32[]{:S(2)}) %collective-permute-start.2) | collective-permute-done | bytes 442400 | tf_op jit(solution)/shard_map/ppermute | solution.py:121
  22.3 18.6 %collective-permute-start.3 = (bf16[192,1152]{1,0:T(8,128)(2,1)}, bf16[192,1152]{1,0:T(8,128)(2,1)S(1)}, u32[]{:S(2)}, u32[]{:S(2)}) collective-permute-start(bf16[192,1152]{1,0:T(8,128)(2,1)} %collective-permute-done.2), channel_id=1, source_target_pairs={{0,2},{2,0},{4,6},{6,4},{1,3},{3,1},{5,7},{7,5},{8,10},{10,8},{12,... | collective-permute-start | bytes 1327112 | tf_op jit(solution)/shard_map/ppermute | solution.py:18
  41.1 1.9 collective-permute-start.1
  44.0 5.1 %collective-permute-done.3 = bf16[192,1152]{1,0:T(8,128)(2,1)S(1)} collective-permute-done((bf16[192,1152]{1,0:T(8,128)(2,1)}, bf16[192,1152]{1,0:T(8,128)(2,1)S(1)}, u32[]{:S(2)}, u32[]{:S(2)}) %collective-permute-start.3) | collective-permute-done | bytes 442400 | tf_op jit(solution)/shard_map/ppermute | solution.py:18
  53.8 6.4 %convolution_convert_fusion = bf16[1280,1152]{1,0:T(8,128)(2,1)} fusion(bf16[384,1152]{1,0:T(8,128)(2,1)S(1)} %reduce-precision_convert_fusion, bf16[384,1152]{1,0:T(8,128)(2,1)} %copy-done.8, s32[1280]{0:T(1024)S(1)} %fusion.44, f32[1280]{0:T(1024)} %fusion.55), kind=kOutput, calls=%fused_computation | convolution fusion | flops 2268856320 | bytes 4728832 | tf_op jit(solution)/shard_map/dot_general | solution.py:31
  60.2 2.6 %dynamic-slice_bitcast_fusion = bf16[2,2,2,2,40,1152]{5,4,3,2,1,0:T(8,128)(2,1)} fusion(bf16[2,2,2,2,2,40,1152]{6,5,4,3,2,1,0:T(8,128)(2,1)} %bitcast.50, s32[]{:T(128)S(6)} %select_n.235), kind=kLoop, calls=%fused_computation.22 | loop fusion | bytes 2949124 | tf_op jit(solution)/shard_map/jit(dynamic_index_in_dim)/squeeze | solution.py:35
  64.7 3.6 %collective-permute-done.7 = bf16[2,2,2,2,40,1152]{5,4,3,2,1,0:T(8,128)(2,1)} collective-permute-done((bf16[2,2,2,2,40,1152]{5,4,3,2,1,0:T(8,128)(2,1)}, bf16[2,2,2,2,40,1152]{5,4,3,2,1,0:T(8,128)(2,1)}, u32[]{:S(2)}, u32[]{:S(2)}) %collective-permute-start.7) | collective-permute-done | bytes 1474592 | tf_op jit(solution)/shard_map/ppermute | solution.py:18
  68.3 2.2 %fusion.3 = bf16[2,2,2,2,40,1152]{5,4,3,2,1,0:T(8,128)(2,1)S(1)} fusion(bf16[2,2,2,2,40,1152]{5,4,3,2,1,0:T(8,128)(2,1)} %collective-permute-done.7, bf16[2,2,2,2,2,40,1152]{6,5,4,3,2,1,0:T(8,128)(2,1)} %bitcast.51, s32[]{:T(128)S(6)} %select_n.234), kind=kLoop, calls=%fused_computation.9 | loop fusion | flops 3686400 | bytes 4423684 | tf_op jit(solution)/shard_map/convert_element_type | solution.py:27
  74.4 18.8 %collective-permute-done.8 = bf16[2,2,2,40,1152]{4,3,2,1,0:T(8,128)(2,1)} collective-permute-done((bf16[2,2,2,40,1152]{4,3,2,1,0:T(8,128)(2,1)}, bf16[2,2,2,40,1152]{4,3,2,1,0:T(8,128)(2,1)}, u32[]{:S(2)}, u32[]{:S(2)}) %collective-permute-start.8) | collective-permute-done | bytes 737312 | tf_op jit(solution)/shard_map/ppermute | solution.py:18
  96.4 10.5 %collective-permute-start.9 = (bf16[2,2,40,1152]{3,2,1,0:T(8,128)(2,1)}, bf16[2,2,40,1152]{3,2,1,0:T(8,128)(2,1)}, u32[]{:S(2)}, u32[]{:S(2)}) collective-permute-start(bf16[2,2,40,1152]{3,2,1,0:T(8,128)(2,1)} %dynamic-slice_bitcast_fusion.2), channel_id=1, source_target_pairs={{0,24},{8,16},{16,8},{24,0},{1,25},{9,17},{17,9},{25,1},{2,26},{10... | collective-permute-start | bytes 1105928 | tf_op jit(solution)/shard_map/ppermute | solution.py:18
  107.0 8.3 %collective-permute-done.9 = bf16[2,2,40,1152]{3,2,1,0:T(8,128)(2,1)} collective-permute-done((bf16[2,2,40,1152]{3,2,1,0:T(8,128)(2,1)}, bf16[2,2,40,1152]{3,2,1,0:T(8,128)(2,1)}, u32[]{:S(2)}, u32[]{:S(2)}) %collective-permute-start.9) | collective-permute-done | bytes 368672 | tf_op jit(solution)/shard_map/ppermute | solution.py:18
  119.9 5.8 %collective-permute-done.10 = bf16[2,40,1152]{2,1,0:T(8,128)(2,1)} collective-permute-done((bf16[2,40,1152]{2,1,0:T(8,128)(2,1)}, bf16[2,40,1152]{2,1,0:T(8,128)(2,1)}, u32[]{:S(2)}, u32[]{:S(2)}) %collective-permute-start.10) | collective-permute-done | bytes 184352 | tf_op jit(solution)/shard_map/ppermute | solution.py:18
  128.0 3.6 %collective-permute-start.11 = (bf16[40,1152]{1,0:T(8,128)(2,1)}, bf16[40,1152]{1,0:T(8,128)(2,1)}, u32[]{:S(2)}, u32[]{:S(2)}) collective-permute-start(bf16[40,1152]{1,0:T(8,128)(2,1)} %dynamic-slice_bitcast_fusion.4), channel_id=1, source_target_pairs={{0,4},{2,6},{4,0},{6,2},{1,5},{3,7},{5,1},{7,3},{8,12},{10,14},{12... | collective-permute-start | bytes 276488 | tf_op jit(solution)/shard_map/ppermute | solution.py:18
  131.7 5.0 %collective-permute-done.11 = bf16[40,1152]{1,0:T(8,128)(2,1)} collective-permute-done((bf16[40,1152]{1,0:T(8,128)(2,1)}, bf16[40,1152]{1,0:T(8,128)(2,1)}, u32[]{:S(2)}, u32[]{:S(2)}) %collective-permute-start.11) | collective-permute-done | bytes 92192 | tf_op jit(solution)/shard_map/ppermute | solution.py:18
  138.3 3.0 %collective-permute-start.12 = (bf16[40,1152]{1,0:T(8,128)(2,1)}, bf16[40,1152]{1,0:T(8,128)(2,1)}, u32[]{:S(2)}, u32[]{:S(2)}) collective-permute-start(bf16[40,1152]{1,0:T(8,128)(2,1)} %fusion.30), channel_id=1, source_target_pairs={{0,32},{32,0},{1,33},{33,1},{2,34},{34,2},{3,35},{35,3},{4,36},{36... | collective-permute-start | bytes 276488 | tf_op jit(solution)/shard_map/ppermute | solution.py:18
  141.4 1.9 collective-permute-start.6
  143.3 7.0 %collective-permute-done.12 = bf16[40,1152]{1,0:T(8,128)(2,1)} collective-permute-done((bf16[40,1152]{1,0:T(8,128)(2,1)}, bf16[40,1152]{1,0:T(8,128)(2,1)}, u32[]{:S(2)}, u32[]{:S(2)}) %collective-permute-start.12) | collective-permute-done | bytes 92192 | tf_op jit(solution)/shard_map/ppermute | solution.py:18
  151.3 1.9 collective-permute-start.13
  153.2 2.9 %convolution_multiply_fusion = f32[768,1152]{1,0:T(8,128)S(1)} fusion(bf16[768,384]{1,0:T(8,128)(2,1)} %copy-done.7, f32[]{:T(128)} %bitcast.46, f32[384,1152]{1,0:T(8,128)} %copy-done.1, f32[384]{0:T(512)S(1)} %add_rsqrt_fusion), kind=kOutput, calls=%fused_computation.3 | convolution fusion | flops 681246720 | bytes 5899780 | tf_op jit(solution)/shard_map/dot_general | solution.py:31
  156.2 1.9 collective-permute-start.4
  158.2 2.3 %collective-permute-start.14 = (bf16[40,1152]{1,0:T(8,128)(2,1)S(1)}, bf16[40,1152]{1,0:T(8,128)(2,1)S(1)}, u32[]{:S(2)}, u32[]{:S(2)}) collective-permute-start(bf16[40,1152]{1,0:T(8,128)(2,1)S(1)} %reduce-precision_convert_fusion.3), channel_id=1, source_target_pairs={{0,128},{64,192},{128,0},{192,64},{256,384},{320,448},{384,256},{4... | collective-permute-start | bytes 276488 | tf_op jit(solution)/shard_map/ppermute | solution.py:18
  160.4 2.0 fusion.25
  162.4 5.6 %collective-permute-done.14 = bf16[40,1152]{1,0:T(8,128)(2,1)S(1)} collective-permute-done((bf16[40,1152]{1,0:T(8,128)(2,1)S(1)}, bf16[40,1152]{1,0:T(8,128)(2,1)S(1)}, u32[]{:S(2)}, u32[]{:S(2)}) %collective-permute-start.14) | collective-permute-done | bytes 92192 | tf_op jit(solution)/shard_map/ppermute | solution.py:18
  168.0 12.0 %collective-permute-start.15 = (bf16[40,1152]{1,0:T(8,128)(2,1)S(1)}, bf16[40,1152]{1,0:T(8,128)(2,1)S(1)}, u32[]{:S(2)}, u32[]{:S(2)}) collective-permute-start(bf16[40,1152]{1,0:T(8,128)(2,1)S(1)} %reduce-precision_convert_fusion.2), channel_id=1, source_target_pairs={{0,512},{64,576},{128,640},{192,704},{256,0},{320,64},{384,128},{4... | collective-permute-start | bytes 276488 | tf_op jit(solution)/shard_map/ppermute | solution.py:23
  180.0 1.9 collective-permute-start.16
  182.2 4.8 %collective-permute-start.5 = (bf16[192,1152]{1,0:T(8,128)(2,1)S(1)}, bf16[192,1152]{1,0:T(8,128)(2,1)S(1)}, u32[]{:S(2)}, u32[]{:S(2)}) collective-permute-start(bf16[192,1152]{1,0:T(8,128)(2,1)S(1)} %slice.56), channel_id=1, source_target_pairs={{0,4},{2,6},{4,0},{6,2},{1,5},{3,7},{5,1},{7,3},{8,12},{10,14},{12... | collective-permute-start | bytes 1327112 | tf_op jit(solution)/shard_map/ppermute | solution.py:18
  187.0 6.1 %collective-permute-done.16 = bf16[40,1152]{1,0:T(8,128)(2,1)S(1)} collective-permute-done((bf16[40,1152]{1,0:T(8,128)(2,1)S(1)}, bf16[40,1152]{1,0:T(8,128)(2,1)S(1)}, u32[]{:S(2)}, u32[]{:S(2)}) %collective-permute-start.16) | collective-permute-done | bytes 92192 | tf_op jit(solution)/shard_map/ppermute | solution.py:23
  193.1 5.1 %collective-permute-start.17 = (bf16[40,1152]{1,0:T(8,128)(2,1)S(1)}, bf16[40,1152]{1,0:T(8,128)(2,1)S(1)}, u32[]{:S(2)}, u32[]{:S(2)}) collective-permute-start(bf16[40,1152]{1,0:T(8,128)(2,1)S(1)} %reduce-precision_convert_fusion.1), channel_id=1, source_target_pairs={{0,24},{8,16},{16,8},{24,0},{1,25},{9,17},{17,9},{25,1},{2,26},{10... | collective-permute-start | bytes 276488 | tf_op jit(solution)/shard_map/ppermute | solution.py:18
  198.2 8.0 %collective-permute-done.5 = bf16[192,1152]{1,0:T(8,128)(2,1)S(1)} collective-permute-done((bf16[192,1152]{1,0:T(8,128)(2,1)S(1)}, bf16[192,1152]{1,0:T(8,128)(2,1)S(1)}, u32[]{:S(2)}, u32[]{:S(2)}) %collective-permute-start.5) | collective-permute-done | bytes 442400 | tf_op jit(solution)/shard_map/ppermute | solution.py:18
  209.7 4.3 %collective-permute-done.18 = bf16[2,40,1152]{2,1,0:T(8,128)(2,1)S(1)} collective-permute-done((bf16[2,40,1152]{2,1,0:T(8,128)(2,1)S(1)}, bf16[2,40,1152]{2,1,0:T(8,128)(2,1)S(1)}, u32[]{:S(2)}, u32[]{:S(2)}) %collective-permute-start.18) | collective-permute-done | bytes 184352 | tf_op jit(solution)/shard_map/ppermute | solution.py:18
  (73 shorter events, 34.0 us)
Async XLA Ops:
  0.6 48.5 %copy-start = (bf16[1152,1152]{1,0:T(8,128)(2,1)S(1)}, bf16[1152,1152]{1,0:T(8,128)(2,1)}, u32[]{:S(2)}) copy-start(bf16[1152,1152]{1,0:T(8,128)(2,1)} %param.10) | copy-start | bytes 7962628
  0.6 21.7 %collective-permute-start.2 = (bf16[192,1152]{1,0:T(8,128)(2,1)}, bf16[192,1152]{1,0:T(8,128)(2,1)}, u32[]{:S(2)}, u32[]{:S(2)}) collective-permute-start(bf16[192,1152]{1,0:T(8,128)(2,1)} %param.8), channel_id=1, source_target_pairs={{760,0},{0,8},{8,16},{16,24},{24,32},{32,40},{40,48},{48,56},{56,6... | collective-permute-start | bytes 1327112 | tf_op jit(solution)/shard_map/ppermute | solution.py:121
  6.7 34.3 %collective-permute-start = (bf16[192,1152]{1,0:T(8,128)(2,1)S(1)}, bf16[192,1152]{1,0:T(8,128)(2,1)S(1)}, u32[]{:S(2)}, u32[]{:S(2)}) collective-permute-start(bf16[192,1152]{1,0:T(8,128)(2,1)S(1)} %fusion.18), channel_id=1, source_target_pairs={{0,4},{2,6},{4,0},{6,2},{1,5},{3,7},{5,1},{7,3},{8,12},{10,14},{12... | collective-permute-start | bytes 1327112 | tf_op jit(solution)/shard_map/ppermute | solution.py:18
  13.9 35.2 %copy-start.10 = (f32[1152]{0:T(1024)S(1)}, f32[1152]{0:T(1024)}, u32[]{:S(2)}) copy-start(f32[1152]{0:T(1024)} %param.11) | copy-start | bytes 13828
  22.3 26.8 %collective-permute-start.3 = (bf16[192,1152]{1,0:T(8,128)(2,1)}, bf16[192,1152]{1,0:T(8,128)(2,1)S(1)}, u32[]{:S(2)}, u32[]{:S(2)}) collective-permute-start(bf16[192,1152]{1,0:T(8,128)(2,1)} %collective-permute-done.2), channel_id=1, source_target_pairs={{0,2},{2,0},{4,6},{6,4},{1,3},{3,1},{5,7},{7,5},{8,10},{10,8},{12,... | collective-permute-start | bytes 1327112 | tf_op jit(solution)/shard_map/ppermute | solution.py:18
  41.1 9.7 %collective-permute-start.1 = (bf16[384,1152]{1,0:T(8,128)(2,1)S(1)}, bf16[384,1152]{1,0:T(8,128)(2,1)S(1)}, u32[]{:S(2)}, u32[]{:S(2)}) collective-permute-start(bf16[384,1152]{1,0:T(8,128)(2,1)S(1)} %pad_maximum_fusion.1), channel_id=1, source_target_pairs={{0,1},{1,0},{2,3},{3,2},{4,5},{5,4},{6,7},{7,6},{8,9},{9,8},{10,11... | collective-permute-start | bytes 2654216 | tf_op jit(solution)/shard_map/ppermute | solution.py:18
  49.2 1.6 copy-start.8
  49.2 1.6 copy-start.9
  50.8 2.7 %copy-start.1 = (f32[384,1152]{1,0:T(8,128)}, f32[384,1152]{1,0:T(8,128)S(1)}, u32[]{:S(2)}) copy-start(f32[384,1152]{1,0:T(8,128)S(1)} %get-tuple-element.9) | copy-start | bytes 5308420
  52.3 1.1 copy-start.7
  62.8 5.5 %collective-permute-start.7 = (bf16[2,2,2,2,40,1152]{5,4,3,2,1,0:T(8,128)(2,1)}, bf16[2,2,2,2,40,1152]{5,4,3,2,1,0:T(8,128)(2,1)}, u32[]{:S(2)}, u32[]{:S(2)}) collective-permute-start(bf16[2,2,2,2,40,1152]{5,4,3,2,1,0:T(8,128)(2,1)} %dynamic-slice_bitcast_fusion), channel_id=1, source_target_pairs={{0,1},{1,0},{2,3},{3,2},{4,5},{5,4},{6,7},{7,6},{8,9},{9,8},{10,11... | collective-permute-start | bytes 4423688 | tf_op jit(solution)/shard_map/ppermute | solution.py:18
  70.4 1.1 copy-start.3
  72.5 20.7 %collective-permute-start.8 = (bf16[2,2,2,40,1152]{4,3,2,1,0:T(8,128)(2,1)}, bf16[2,2,2,40,1152]{4,3,2,1,0:T(8,128)(2,1)}, u32[]{:S(2)}, u32[]{:S(2)}) collective-permute-start(bf16[2,2,2,40,1152]{4,3,2,1,0:T(8,128)(2,1)} %dynamic-slice_bitcast_fusion.1), channel_id=1, source_target_pairs={{0,8},{8,0},{16,24},{24,16},{1,9},{9,1},{17,25},{25,17},{2,10},{10... | collective-permute-start | bytes 2211848 | tf_op jit(solution)/shard_map/ppermute | solution.py:18
  94.7 0.9 copy-start.4
  96.4 18.9 %collective-permute-start.9 = (bf16[2,2,40,1152]{3,2,1,0:T(8,128)(2,1)}, bf16[2,2,40,1152]{3,2,1,0:T(8,128)(2,1)}, u32[]{:S(2)}, u32[]{:S(2)}) collective-permute-start(bf16[2,2,40,1152]{3,2,1,0:T(8,128)(2,1)} %dynamic-slice_bitcast_fusion.2), channel_id=1, source_target_pairs={{0,24},{8,16},{16,8},{24,0},{1,25},{9,17},{17,9},{25,1},{2,26},{10... | collective-permute-start | bytes 1105928 | tf_op jit(solution)/shard_map/ppermute | solution.py:18
  116.5 0.7 copy-start.5
  117.9 7.7 %collective-permute-start.10 = (bf16[2,40,1152]{2,1,0:T(8,128)(2,1)}, bf16[2,40,1152]{2,1,0:T(8,128)(2,1)}, u32[]{:S(2)}, u32[]{:S(2)}) collective-permute-start(bf16[2,40,1152]{2,1,0:T(8,128)(2,1)} %dynamic-slice_bitcast_fusion.3), channel_id=1, source_target_pairs={{0,2},{2,0},{4,6},{6,4},{1,3},{3,1},{5,7},{7,5},{8,10},{10,8},{12,... | collective-permute-start | bytes 552968 | tf_op jit(solution)/shard_map/ppermute | solution.py:18
  126.7 0.7 copy-start.6
  128.0 8.6 %collective-permute-start.11 = (bf16[40,1152]{1,0:T(8,128)(2,1)}, bf16[40,1152]{1,0:T(8,128)(2,1)}, u32[]{:S(2)}, u32[]{:S(2)}) collective-permute-start(bf16[40,1152]{1,0:T(8,128)(2,1)} %dynamic-slice_bitcast_fusion.4), channel_id=1, source_target_pairs={{0,4},{2,6},{4,0},{6,2},{1,5},{3,7},{5,1},{7,3},{8,12},{10,14},{12... | collective-permute-start | bytes 276488 | tf_op jit(solution)/shard_map/ppermute | solution.py:18
  138.3 12.0 %collective-permute-start.12 = (bf16[40,1152]{1,0:T(8,128)(2,1)}, bf16[40,1152]{1,0:T(8,128)(2,1)}, u32[]{:S(2)}, u32[]{:S(2)}) collective-permute-start(bf16[40,1152]{1,0:T(8,128)(2,1)} %fusion.30), channel_id=1, source_target_pairs={{0,32},{32,0},{1,33},{33,1},{2,34},{34,2},{3,35},{35,3},{4,36},{36... | collective-permute-start | bytes 276488 | tf_op jit(solution)/shard_map/ppermute | solution.py:18
  141.4 19.0 %collective-permute-start.6 = (bf16[192,1152]{1,0:T(8,128)(2,1)S(1)}, bf16[192,1152]{1,0:T(8,128)(2,1)S(1)}, u32[]{:S(2)}, u32[]{:S(2)}) collective-permute-start(bf16[192,1152]{1,0:T(8,128)(2,1)S(1)} %slice.39), channel_id=1, source_target_pairs={{0,2},{2,0},{4,6},{6,4},{1,3},{3,1},{5,7},{7,5},{8,10},{10,8},{12,... | collective-permute-start | bytes 1327112 | tf_op jit(solution)/shard_map/ppermute | solution.py:18
  151.3 6.8 %collective-permute-start.13 = (bf16[40,1152]{1,0:T(8,128)(2,1)S(1)}, bf16[40,1152]{1,0:T(8,128)(2,1)S(1)}, u32[]{:S(2)}, u32[]{:S(2)}) collective-permute-start(bf16[40,1152]{1,0:T(8,128)(2,1)S(1)} %reduce-precision_convert_fusion.4), channel_id=1, source_target_pairs={{0,64},{64,0},{128,192},{192,128},{256,320},{320,256},{384,448},{4... | collective-permute-start | bytes 276488 | tf_op jit(solution)/shard_map/ppermute | solution.py:18
  156.2 25.8 %collective-permute-start.4 = (bf16[384,1152]{1,0:T(8,128)(2,1)S(1)}, bf16[384,1152]{1,0:T(8,128)(2,1)S(1)}, u32[]{:S(2)}, u32[]{:S(2)}) collective-permute-start(bf16[384,1152]{1,0:T(8,128)(2,1)S(1)} %slice.55), channel_id=1, source_target_pairs={{0,1},{1,0},{2,3},{3,2},{4,5},{5,4},{6,7},{7,6},{8,9},{9,8},{10,11... | collective-permute-start | bytes 2654216 | tf_op jit(solution)/shard_map/ppermute | solution.py:18
  158.2 9.8 %collective-permute-start.14 = (bf16[40,1152]{1,0:T(8,128)(2,1)S(1)}, bf16[40,1152]{1,0:T(8,128)(2,1)S(1)}, u32[]{:S(2)}, u32[]{:S(2)}) collective-permute-start(bf16[40,1152]{1,0:T(8,128)(2,1)S(1)} %reduce-precision_convert_fusion.3), channel_id=1, source_target_pairs={{0,128},{64,192},{128,0},{192,64},{256,384},{320,448},{384,256},{4... | collective-permute-start | bytes 276488 | tf_op jit(solution)/shard_map/ppermute | solution.py:18
  168.0 38.2 %copy-start.2 = (bf16[192,1152]{1,0:T(8,128)(2,1)S(1)}, bf16[192,1152]{1,0:T(8,128)(2,1)}, u32[]{:S(2)}) copy-start(bf16[192,1152]{1,0:T(8,128)(2,1)} %param.7) | copy-start | bytes 1327108
  168.0 18.9 %collective-permute-start.15 = (bf16[40,1152]{1,0:T(8,128)(2,1)S(1)}, bf16[40,1152]{1,0:T(8,128)(2,1)S(1)}, u32[]{:S(2)}, u32[]{:S(2)}) collective-permute-start(bf16[40,1152]{1,0:T(8,128)(2,1)S(1)} %reduce-precision_convert_fusion.2), channel_id=1, source_target_pairs={{0,512},{64,576},{128,640},{192,704},{256,0},{320,64},{384,128},{4... | collective-permute-start | bytes 276488 | tf_op jit(solution)/shard_map/ppermute | solution.py:23
  180.0 13.0 %collective-permute-start.16 = (bf16[40,1152]{1,0:T(8,128)(2,1)S(1)}, bf16[40,1152]{1,0:T(8,128)(2,1)S(1)}, u32[]{:S(2)}, u32[]{:S(2)}) collective-permute-start(bf16[40,1152]{1,0:T(8,128)(2,1)S(1)} %reduce-precision_convert_fusion.2), channel_id=1, source_target_pairs={{0,256},{64,320},{128,384},{192,448},{256,512},{320,576},{384,640}... | collective-permute-start | bytes 276488 | tf_op jit(solution)/shard_map/ppermute | solution.py:23
  182.2 24.0 %collective-permute-start.5 = (bf16[192,1152]{1,0:T(8,128)(2,1)S(1)}, bf16[192,1152]{1,0:T(8,128)(2,1)S(1)}, u32[]{:S(2)}, u32[]{:S(2)}) collective-permute-start(bf16[192,1152]{1,0:T(8,128)(2,1)S(1)} %slice.56), channel_id=1, source_target_pairs={{0,4},{2,6},{4,0},{6,2},{1,5},{3,7},{5,1},{7,3},{8,12},{10,14},{12... | collective-permute-start | bytes 1327112 | tf_op jit(solution)/shard_map/ppermute | solution.py:18
  193.1 13.4 %collective-permute-start.17 = (bf16[40,1152]{1,0:T(8,128)(2,1)S(1)}, bf16[40,1152]{1,0:T(8,128)(2,1)S(1)}, u32[]{:S(2)}, u32[]{:S(2)}) collective-permute-start(bf16[40,1152]{1,0:T(8,128)(2,1)S(1)} %reduce-precision_convert_fusion.1), channel_id=1, source_target_pairs={{0,24},{8,16},{16,8},{24,0},{1,25},{9,17},{17,9},{25,1},{2,26},{10... | collective-permute-start | bytes 276488 | tf_op jit(solution)/shard_map/ppermute | solution.py:18
  206.5 7.4 %collective-permute-start.18 = (bf16[2,40,1152]{2,1,0:T(8,128)(2,1)S(1)}, bf16[2,40,1152]{2,1,0:T(8,128)(2,1)S(1)}, u32[]{:S(2)}, u32[]{:S(2)}) collective-permute-start(bf16[2,40,1152]{2,1,0:T(8,128)(2,1)S(1)} %pad_maximum_fusion.5), channel_id=1, source_target_pairs={{0,8},{8,0},{16,24},{24,16},{1,9},{9,1},{17,25},{25,17},{2,10},{10... | collective-permute-start | bytes 552968 | tf_op jit(solution)/shard_map/ppermute | solution.py:18

commit v2 on v1

v2 whole, which is shorter than its diff:
```python
import jax
import jax.numpy as jnp
from jax import lax
from jax.sharding import PartitionSpec as P

eps = 1e-06
AXES = ("z", "h", "x", "y", "k")
COL = AXES[:3]
SIZES = (12, 2, 4, 4, 2)
D = 1152
PART = 36
PAD = 40
f32, bf16 = jnp.float32, jnp.bfloat16


def swap(block, axis, mask):
    n = lax.axis_size(axis)
    return lax.ppermute(block, axis, [(i, i ^ mask) for i in range(n)])


def turn(block, axis, distance):
    n = lax.axis_size(axis)
    return lax.ppermute(block, axis, [(i, (i + distance) % n) for i in range(n)])


def low(values):
    return lax.reduce_precision(values, 8, 7).astype(bf16)


def dot(a, b, ca, cb):
    return lax.dot_general(a, b, (((ca,), (cb,)), ((), ())), preferred_element_type=f32)


def pick(parts, at):
    total = 0.0
    for part in parts:
        total = total + lax.dynamic_index_in_dim(part, at, 0, keepdims=False).astype(f32)
    return total


def tie(*values):
    return lax.optimization_barrier(values)


def spread_matrix(core):
    place = jnp.arange(16 * PAD, dtype=jnp.int32)
    part, i = place // PAD, place % PAD
    x, y = part // 4, part % 4
    feature = jnp.where(i < PART, (2 * y + core) * 144 + x * PART + i, -1)
    matrix = (jnp.arange(D, dtype=jnp.int32)[:, None] == feature[None, :]).astype(bf16)
    return matrix, (i == PART).astype(f32)


def head_rows(texts, core):
    spread, ones = spread_matrix(core)
    (spread,) = tie(spread)
    return (dot(texts, spread, 1, 0) + ones).astype(bf16)


def per_device(pictures, captions, slot, matrix, intercept, sharpness, score_shift):
    sharp, moved = sharpness[0], score_shift[0]
    rows = pictures.shape[0]
    z, x, y, k = (lax.axis_index(a) for a in ("z", "x", "y", "k"))

    paired = turn_col(captions)
    picture = pictures.astype(f32)
    image_scale = lax.rsqrt(jnp.sum(picture * picture, -1, keepdims=True) + eps)
    image_unit = picture * image_scale
    image_low = image_unit.astype(bf16)
    pair = jnp.concatenate([image_low, swap(image_low, "y", 2)])
    images = jnp.concatenate([pair, swap(pair, "k", 1)])
    texts = jnp.concatenate([paired, swap(paired, "y", 1)])

    projected = dot(texts, matrix, 1, 0) + intercept
    text_scale = lax.rsqrt(jnp.sum(projected * projected, -1, keepdims=True) + eps)
    text_unit = projected * text_scale
    text_low = text_unit.astype(bf16)
    texts_sent, texts_kept = tie(head_rows(texts, 1 - k), head_rows(texts, k))

    scores = sharp * dot(images, text_low, 1, 1) + moved
    wanted = jnp.concatenate([slot[0], jnp.full((3 * rows,), -1, jnp.int32)])
    positive = wanted[:, None] == jnp.arange(2 * rows, dtype=jnp.int32)[None, :]
    sign = jnp.where(positive, 1.0, -1.0).astype(f32)
    weight = (-sign * jax.nn.sigmoid(-sign * scores)).astype(bf16)

    text_dir = sharp * dot(weight, images, 0, 0)
    along = jnp.sum(text_unit * text_dir, -1, keepdims=True)
    grad = (text_dir - text_unit * along) * text_scale
    grad_low = low(grad)

    sent = dot(texts_sent, grad_low, 0, 0).astype(bf16)
    arrived = swap(sent, "k", 1)
    kept = dot(texts_kept, grad_low, 0, 0).astype(bf16)
    parts = [p.reshape(4, 4 * PAD, D) for p in (kept, arrived)]

    over_x = {d: turn(low(pick(parts, (x + d) % 4)), "x", d) for d in (2, 1, 3)}
    grad_far = swap(grad_low[rows:], "y", 1)
    image_dir = sharp * dot(weight, text_low, 1, 0)
    image_sent = image_dir[2 * rows :].astype(bf16)
    *over_x, image_sent, grad_far = tie(*over_x.values(), image_sent, grad_far)
    projected_grad = grad_low[:rows].astype(f32) + grad_far.astype(f32)
    text_grad = dot(projected_grad.astype(bf16), matrix, 1, 1)

    parts = [lax.dynamic_index_in_dim(p, x, 0, keepdims=False) for p in parts] + over_x
    parts = [p.reshape(4, PAD, D) for p in parts]
    over_y = {m: swap(low(pick(parts, y ^ m)), "y", m) for m in (2, 3, 1)}
    total = pick(parts, y)
    for other in over_y.values():
        total = total + other.astype(f32)
    head = low(total)
    head = low(head.astype(f32) + swap(head, "h", 1).astype(f32))

    mine = image_dir[: 2 * rows] + swap(image_sent, "k", 1).astype(f32)
    image_far = mine[rows:].astype(bf16)
    head, image_far = tie(head, image_far)

    over_z = {m: swap(head, "z", m).astype(f32) for m in (2, 3, 1)}
    head = low((head.astype(f32) + over_z[1]) + (over_z[2] + over_z[3]))
    far_one = swap(image_far[: rows // 2], "y", 2)
    head, far_one = tie(head, far_one)
    ring = [head, turn(head, "z", 8), turn(head, "z", 4)]
    u = z // 4
    total = 0.0
    for j in range(3):
        at = (j - u) % 3
        total = total + jnp.where(at == 0, ring[0], jnp.where(at == 1, ring[1], ring[2])).astype(f32)
    far_two = swap(image_far[rows // 2 :], "y", 2)
    head, far_two = tie(low(total), far_two)
    own = mine[:rows] + jnp.concatenate([far_one, far_two]).astype(f32)
    around = [head] + [turn(head, "x", d) for d in (2, 1, 3)]
    ordered = []
    for q in range(4):
        d = (x - q) % 4
        one = jnp.where(d == 0, around[0], jnp.where(d == 2, around[1], jnp.where(d == 1, around[2], around[3])))
        ordered.append(one)
    head_grad = jnp.concatenate([one[:PART] for one in ordered]).astype(f32)
    bias_grad = lax.dynamic_slice(ordered[0][PART].astype(f32), ((2 * y + k) * 144,), (144,))

    along = jnp.sum(image_unit * own, -1, keepdims=True)
    image_grad = (own - image_unit * along) * image_scale
    return (image_grad, text_grad, head_grad, bias_grad)


def turn_col(block):
    return lax.ppermute(block, COL, [((i - 1) % 96, i) for i in range(96)])


def solution(mesh):
    fine = jax.sharding.Mesh(mesh.devices.reshape(SIZES), AXES)
    rows = P(AXES, None)
    in_specs = (rows, rows, rows, P(), P(), P(), P())
    out_specs = (rows, rows, P(("y", "k"), None), P(("y", "k")))
    return jax.shard_map(
        per_device, mesh=fine, in_specs=in_specs, out_specs=out_specs, check_vma=False
    )
```

time: 219 us -> 200 us (0.913)
  waiting for transfers between devices: 85.9 us -> 72.7 us
  local copies, waits for them, and re-layouts: 12.5 us -> 3.87 us
  starting transfers between devices: 84.8 us -> 88 us
    ppermute x16 -> x15, waiting for transfers between devices: 71.4 us -> 24.7 us  [swap(): return lax.ppermute(block, axis, [(i, i ^ mask) for i in range(n)])]
    ppermute x2 -> x8, starting transfers between devices: 13.9 us -> 34.2 us  [turn(): lax.ppermute(block, axis, [(i, (i + distance) % n) for i in range(n)])]
    ppermute x2 -> x8, waiting for transfers between devices: 6.09 us -> 25.9 us  [turn(): lax.ppermute(block, axis, [(i, (i + distance) % n) for i in range(n)])]
    ppermute x16 -> x15, starting transfers between devices: 67.3 us -> 50.4 us  [swap(): return lax.ppermute(block, axis, [(i, i ^ mask) for i in range(n)])]
    ppermute x1, waiting for transfers between devices: 8.39 us -> 22.1 us  [turn_col(): return lax.ppermute(block, COL, [((i - 1) % 96, i) for i in range(96)])]
    squeeze x5 -> x0, local copies, waits for them, and re-layouts: 5.63 us -> none  [halve(): sent = lax.dynamic_index_in_dim(both, 1 - bit, 0, keepdims=False)]
    convert_element_type x10 -> x7, other arithmetic: 8.94 us -> 5.78 us  [low(): return lax.reduce_precision(values, 8, 7).astype(bf16)]
    unnamed x23 -> x31, local copies, waits for them, and re-layouts: 4.48 us -> 1.49 us
  transfers between devices with their start and end apart: 19 -> 24, of which waited for: 12 -> 10; matrix products, arithmetic and copies ran while one was open for 7% -> 10% of each run, Pallas kernels for 0% -> 0%
where the time goes in v2:
time: 200 us; the launch traced here: 197 us
  starting transfers between devices  88 us (44%)
  waiting for transfers between devices  72.7 us (36%)
  matrix products  14.8 us (7%)
  other arithmetic  14.5 us (7%)
  local copies, waits for them, and re-layouts  3.87 us (2%)
  between operations  2.77 us (1%)
    ppermute x15, starting transfers between devices, swap(): return lax.ppermute(block, axis, [(i, i ^ mask) for i in range(n)])  50.4 us
    ppermute x8, starting transfers between devices, turn(): lax.ppermute(block, axis, [(i, (i + distance) % n) for i in range(n)])  34.2 us
    ppermute x8, waiting for transfers between devices, turn(): lax.ppermute(block, axis, [(i, (i + distance) % n) for i in range(n)])  25.9 us
    ppermute x15, waiting for transfers between devices, swap(): return lax.ppermute(block, axis, [(i, i ^ mask) for i in range(n)])  24.7 us
    ppermute x1, waiting for transfers between devices, turn_col(): return lax.ppermute(block, COL, [((i - 1) % 96, i) for i in range(96)])  22.1 us
    dot_general x9, matrix products, dot(): lax.dot_general(a, b, (((ca,), (cb,)), ((), ())), preferred_element_type=...  14.8 us
    convert_element_type x7, other arithmetic, low(): return lax.reduce_precision(values, 8, 7).astype(bf16)  5.78 us
  transfers between devices with their start and end apart: 24, of which 10 were waited for; matrix products, arithmetic and copies ran while one was open for 10% of the time, Pallas kernels for 0%

profile of v2, /device:TPU:56, one launch (start us, length us, event | category | flops | bytes accessed | tf_op | source)
XLA Modules:
  0.0 196.6 jit_solution(7782522117111127945)
XLA Ops:
  3.2 4.0 %collective-permute-start = (bf16[192,1152]{1,0:T(8,128)(2,1)S(1)}, bf16[192,1152]{1,0:T(8,128)(2,1)S(1)}, u32[]{:S(2)}, u32[]{:S(2)}) collective-permute-start(bf16[192,1152]{1,0:T(8,128)(2,1)S(1)} %fusion.14), channel_id=1, source_target_pairs={{0,4},{2,6},{4,0},{6,2},{1,5},{3,7},{5,1},{7,3},{8,12},{10,14},{12... | collective-permute-start | bytes 1327112 | tf_op jit(solution)/shard_map/ppermute | solution.py:18
  7.2 3.4 %collective-permute-start.2 = (bf16[192,1152]{1,0:T(8,128)(2,1)}, bf16[192,1152]{1,0:T(8,128)(2,1)}, u32[]{:S(2)}, u32[]{:S(2)}) collective-permute-start(bf16[192,1152]{1,0:T(8,128)(2,1)} %param.8), channel_id=1, source_target_pairs={{760,0},{0,8},{8,16},{16,24},{24,32},{32,40},{40,48},{48,56},{56,6... | collective-permute-start | bytes 1327112 | tf_op jit(solution)/shard_map/ppermute | solution.py:145
  13.1 22.1 %collective-permute-done.2 = bf16[192,1152]{1,0:T(8,128)(2,1)} collective-permute-done((bf16[192,1152]{1,0:T(8,128)(2,1)}, bf16[192,1152]{1,0:T(8,128)(2,1)}, u32[]{:S(2)}, u32[]{:S(2)}) %collective-permute-start.2) | collective-permute-done | bytes 442400 | tf_op jit(solution)/shard_map/ppermute | solution.py:145
  35.2 9.4 %collective-permute-start.3 = (bf16[192,1152]{1,0:T(8,128)(2,1)}, bf16[192,1152]{1,0:T(8,128)(2,1)S(1)}, u32[]{:S(2)}, u32[]{:S(2)}) collective-permute-start(bf16[192,1152]{1,0:T(8,128)(2,1)} %collective-permute-done.2), channel_id=1, source_target_pairs={{0,2},{2,0},{4,6},{6,4},{1,3},{3,1},{5,7},{7,5},{8,10},{10,8},{12,... | collective-permute-start | bytes 1327112 | tf_op jit(solution)/shard_map/ppermute | solution.py:18
  44.7 1.9 collective-permute-start.1
  47.7 4.1 %collective-permute-done.3 = bf16[192,1152]{1,0:T(8,128)(2,1)S(1)} collective-permute-done((bf16[192,1152]{1,0:T(8,128)(2,1)}, bf16[192,1152]{1,0:T(8,128)(2,1)S(1)}, u32[]{:S(2)}, u32[]{:S(2)}) %collective-permute-start.3) | collective-permute-done | bytes 442400 | tf_op jit(solution)/shard_map/ppermute | solution.py:18
  59.1 2.2 %convolution_convert_fusion = bf16[640,1152]{1,0:T(8,128)(2,1)} fusion(bf16[384,640]{1,0:T(8,128)(2,1)S(1)} %fusion.7, bf16[384,1152]{1,0:T(8,128)(2,1)S(1)} %reduce-precision_convert_fusion), kind=kOutput, calls=%fused_computation.1 | convolution fusion | flops 566968320 | bytes 2850816 | tf_op jit(solution)/shard_map/dot_general | solution.py:31
  63.3 3.6 %collective-permute-start.8 = (bf16[192,1152]{1,0:T(8,128)(2,1)S(1)}, bf16[192,1152]{1,0:T(8,128)(2,1)S(1)}, u32[]{:S(2)}, u32[]{:S(2)}) collective-permute-start(bf16[192,1152]{1,0:T(8,128)(2,1)S(1)} %slice.56), channel_id=1, source_target_pairs={{0,2},{2,0},{4,6},{6,4},{1,3},{3,1},{5,7},{7,5},{8,10},{10,8},{12,... | collective-permute-start | bytes 1327112 | tf_op jit(solution)/shard_map/ppermute | solution.py:18
  67.0 2.9 %convolution_multiply_fusion = f32[768,1152]{1,0:T(8,128)S(1)} fusion(bf16[768,384]{1,0:T(8,128)(2,1)} %copy-done.6, f32[]{:T(128)} %bitcast.47, f32[384,1152]{1,0:T(8,128)} %copy-done.2, f32[384]{0:T(512)S(1)} %add_rsqrt_fusion), kind=kOutput, calls=%fused_computation | convolution fusion | flops 681246720 | bytes 5899780 | tf_op jit(solution)/shard_map/dot_general | solution.py:31
  73.8 11.0 %collective-permute-start.7 = (bf16[160,1152]{1,0:T(8,128)(2,1)S(1)}, bf16[160,1152]{1,0:T(8,128)(2,1)S(1)}, u32[]{:S(2)}, u32[]{:S(2)}) collective-permute-start(bf16[160,1152]{1,0:T(8,128)(2,1)S(1)} %get-tuple-element.30), channel_id=1, source_target_pairs={{0,24},{8,0},{16,8},{24,16},{1,25},{9,1},{17,9},{25,17},{2,26},{10... | collective-permute-start | bytes 1105928 | tf_op jit(solution)/shard_map/ppermute | solution.py:23
  86.7 3.4 %collective-permute-start.5 = (bf16[160,1152]{1,0:T(8,128)(2,1)S(1)}, bf16[160,1152]{1,0:T(8,128)(2,1)S(1)}, u32[]{:S(2)}, u32[]{:S(2)}) collective-permute-start(bf16[160,1152]{1,0:T(8,128)(2,1)S(1)} %get-tuple-element.32), channel_id=1, source_target_pairs={{0,16},{8,24},{16,0},{24,8},{1,17},{9,25},{17,1},{25,9},{2,18},{10... | collective-permute-start | bytes 1105928 | tf_op jit(solution)/shard_map/ppermute | solution.py:23
  91.4 9.9 %collective-permute-done.7 = bf16[160,1152]{1,0:T(8,128)(2,1)S(1)} collective-permute-done((bf16[160,1152]{1,0:T(8,128)(2,1)S(1)}, bf16[160,1152]{1,0:T(8,128)(2,1)S(1)}, u32[]{:S(2)}, u32[]{:S(2)}) %collective-permute-start.7) | collective-permute-done | bytes 368672 | tf_op jit(solution)/shard_map/ppermute | solution.py:23
  101.2 5.3 %collective-permute-done.6 = bf16[160,1152]{1,0:T(8,128)(2,1)S(1)} collective-permute-done((bf16[160,1152]{1,0:T(8,128)(2,1)S(1)}, bf16[160,1152]{1,0:T(8,128)(2,1)S(1)}, u32[]{:S(2)}, u32[]{:S(2)}) %collective-permute-start.6) | collective-permute-done | bytes 368672 | tf_op jit(solution)/shard_map/ppermute | solution.py:23
  107.5 4.1 %collective-permute-start.10 = (bf16[40,1152]{1,0:T(8,128)(2,1)}, bf16[40,1152]{1,0:T(8,128)(2,1)}, u32[]{:S(2)}, u32[]{:S(2)}) collective-permute-start(bf16[40,1152]{1,0:T(8,128)(2,1)} %get-tuple-element.33), channel_id=1, source_target_pairs={{0,4},{2,6},{4,0},{6,2},{1,5},{3,7},{5,1},{7,3},{8,12},{10,14},{12... | collective-permute-start | bytes 276488 | tf_op jit(solution)/shard_map/ppermute | solution.py:18
  111.6 2.2 %collective-permute-start.12 = (bf16[40,1152]{1,0:T(8,128)(2,1)}, bf16[40,1152]{1,0:T(8,128)(2,1)}, u32[]{:S(2)}, u32[]{:S(2)}) collective-permute-start(bf16[40,1152]{1,0:T(8,128)(2,1)} %get-tuple-element.34), channel_id=1, source_target_pairs={{0,2},{2,0},{4,6},{6,4},{1,3},{3,1},{5,7},{7,5},{8,10},{10,8},{12,... | collective-permute-start | bytes 276488 | tf_op jit(solution)/shard_map/ppermute | solution.py:18
  113.8 3.8 %collective-permute-start.11 = (bf16[40,1152]{1,0:T(8,128)(2,1)}, bf16[40,1152]{1,0:T(8,128)(2,1)}, u32[]{:S(2)}, u32[]{:S(2)}) collective-permute-start(bf16[40,1152]{1,0:T(8,128)(2,1)} %get-tuple-element.35), channel_id=1, source_target_pairs={{0,6},{2,4},{4,2},{6,0},{1,7},{3,5},{5,3},{7,1},{8,14},{10,12},{12... | collective-permute-start | bytes 276488 | tf_op jit(solution)/shard_map/ppermute | solution.py:18
  117.7 1.9 collective-permute-start.9
  119.6 2.9 %collective-permute-done.11 = bf16[40,1152]{1,0:T(8,128)(2,1)} collective-permute-done((bf16[40,1152]{1,0:T(8,128)(2,1)}, bf16[40,1152]{1,0:T(8,128)(2,1)}, u32[]{:S(2)}, u32[]{:S(2)}) %collective-permute-start.11) | collective-permute-done | bytes 92192 | tf_op jit(solution)/shard_map/ppermute | solution.py:18
  124.4 2.1 %collective-permute-start.13 = (bf16[40,1152]{1,0:T(8,128)(2,1)}, bf16[40,1152]{1,0:T(8,128)(2,1)}, u32[]{:S(2)}, u32[]{:S(2)}) collective-permute-start(bf16[40,1152]{1,0:T(8,128)(2,1)} %fusion.27), channel_id=1, source_target_pairs={{0,32},{32,0},{1,33},{33,1},{2,34},{34,2},{3,35},{35,3},{4,36},{36... | collective-permute-start | bytes 276488 | tf_op jit(solution)/shard_map/ppermute | solution.py:18
  126.7 8.4 %collective-permute-done.13 = bf16[40,1152]{1,0:T(8,128)(2,1)} collective-permute-done((bf16[40,1152]{1,0:T(8,128)(2,1)}, bf16[40,1152]{1,0:T(8,128)(2,1)}, u32[]{:S(2)}, u32[]{:S(2)}) %collective-permute-start.13) | collective-permute-done | bytes 92192 | tf_op jit(solution)/shard_map/ppermute | solution.py:18
  138.0 2.1 %collective-permute-start.16 = (bf16[40,1152]{1,0:T(8,128)(2,1)S(1)}, bf16[40,1152]{1,0:T(8,128)(2,1)S(1)}, u32[]{:S(2)}, u32[]{:S(2)}) collective-permute-start(bf16[40,1152]{1,0:T(8,128)(2,1)S(1)} %reduce-precision_convert_fusion.9), channel_id=1, source_target_pairs={{0,192},{64,128},{128,64},{192,0},{256,448},{320,384},{384,320},{4... | collective-permute-start | bytes 276488 | tf_op jit(solution)/shard_map/ppermute | solution.py:18
  140.0 1.9 collective-permute-start.15
  141.9 6.3 %collective-permute-start.14 = (bf16[40,1152]{1,0:T(8,128)(2,1)S(1)}, bf16[40,1152]{1,0:T(8,128)(2,1)S(1)}, u32[]{:S(2)}, u32[]{:S(2)}) collective-permute-start(bf16[40,1152]{1,0:T(8,128)(2,1)S(1)} %reduce-precision_convert_fusion.9), channel_id=1, source_target_pairs={{0,64},{64,0},{128,192},{192,128},{256,320},{320,256},{384,448},{4... | collective-permute-start | bytes 276488 | tf_op jit(solution)/shard_map/ppermute | solution.py:18
  148.3 3.2 %collective-permute-start.17 = (bf16[96,1152]{1,0:T(8,128)(2,1)S(1)}, bf16[96,1152]{1,0:T(8,128)(2,1)S(1)}, u32[]{:S(2)}, u32[]{:S(2)}) collective-permute-start(bf16[96,1152]{1,0:T(8,128)(2,1)S(1)} %get-tuple-element.37), channel_id=1, source_target_pairs={{0,4},{2,6},{4,0},{6,2},{1,5},{3,7},{5,1},{7,3},{8,12},{10,14},{12... | collective-permute-start | bytes 663560 | tf_op jit(solution)/shard_map/ppermute | solution.py:18
  151.6 7.8 %collective-permute-done.17 = bf16[96,1152]{1,0:T(8,128)(2,1)S(1)} collective-permute-done((bf16[96,1152]{1,0:T(8,128)(2,1)S(1)}, bf16[96,1152]{1,0:T(8,128)(2,1)S(1)}, u32[]{:S(2)}, u32[]{:S(2)}) %collective-permute-start.17) | collective-permute-done | bytes 221216 | tf_op jit(solution)/shard_map/ppermute | solution.py:18
  159.4 5.4 %collective-permute-start.19 = (bf16[40,1152]{1,0:T(8,128)(2,1)S(1)}, bf16[40,1152]{1,0:T(8,128)(2,1)S(1)}, u32[]{:S(2)}, u32[]{:S(2)}) collective-permute-start(bf16[40,1152]{1,0:T(8,128)(2,1)S(1)} %reduce-precision_convert_fusion.8), channel_id=1, source_target_pairs={{0,256},{64,320},{128,384},{192,448},{256,512},{320,576},{384,640}... | collective-permute-start | bytes 276488 | tf_op jit(solution)/shard_map/ppermute | solution.py:23
  164.8 4.3 %collective-permute-start.18 = (bf16[40,1152]{1,0:T(8,128)(2,1)S(1)}, bf16[40,1152]{1,0:T(8,128)(2,1)S(1)}, u32[]{:S(2)}, u32[]{:S(2)}) collective-permute-start(bf16[40,1152]{1,0:T(8,128)(2,1)S(1)} %reduce-precision_convert_fusion.8), channel_id=1, source_target_pairs={{0,512},{64,576},{128,640},{192,704},{256,0},{320,64},{384,128},{4... | collective-permute-start | bytes 276488 | tf_op jit(solution)/shard_map/ppermute | solution.py:23
  169.1 1.9 fusion.19
  173.0 6.7 %collective-permute-done.18 = bf16[40,1152]{1,0:T(8,128)(2,1)S(1)} collective-permute-done((bf16[40,1152]{1,0:T(8,128)(2,1)S(1)}, bf16[40,1152]{1,0:T(8,128)(2,1)S(1)}, u32[]{:S(2)}, u32[]{:S(2)}) %collective-permute-start.18) | collective-permute-done | bytes 92192 | tf_op jit(solution)/shard_map/ppermute | solution.py:23
  183.1 3.9 %collective-permute-start.22 = (bf16[40,1152]{1,0:T(8,128)(2,1)S(1)}, bf16[40,1152]{1,0:T(8,128)(2,1)S(1)}, u32[]{:S(2)}, u32[]{:S(2)}) collective-permute-start(bf16[40,1152]{1,0:T(8,128)(2,1)S(1)} %reduce-precision_convert_fusion.7), channel_id=1, source_target_pairs={{0,8},{8,16},{16,24},{24,0},{1,9},{9,17},{17,25},{25,1},{2,10},{10... | collective-permute-start | bytes 276488 | tf_op jit(solution)/shard_map/ppermute | solution.py:23
  187.0 2.4 %collective-permute-start.21 = (bf16[40,1152]{1,0:T(8,128)(2,1)S(1)}, bf16[40,1152]{1,0:T(8,128)(2,1)S(1)}, u32[]{:S(2)}, u32[]{:S(2)}) collective-permute-start(bf16[40,1152]{1,0:T(8,128)(2,1)S(1)} %reduce-precision_convert_fusion.7), channel_id=1, source_target_pairs={{0,16},{8,24},{16,0},{24,8},{1,17},{9,25},{17,1},{25,9},{2,18},{10... | collective-permute-start | bytes 276488 | tf_op jit(solution)/shard_map/ppermute | solution.py:23
  190.9 4.1 %collective-permute-done.21 = bf16[40,1152]{1,0:T(8,128)(2,1)S(1)} collective-permute-done((bf16[40,1152]{1,0:T(8,128)(2,1)S(1)}, bf16[40,1152]{1,0:T(8,128)(2,1)S(1)}, u32[]{:S(2)}, u32[]{:S(2)}) %collective-permute-start.21) | collective-permute-done | bytes 92192 | tf_op jit(solution)/shard_map/ppermute | solution.py:23
  (89 shorter events, 35.3 us)
Async XLA Ops:
  0.6 53.9 %copy-start = (bf16[1152,1152]{1,0:T(8,128)(2,1)S(1)}, bf16[1152,1152]{1,0:T(8,128)(2,1)}, u32[]{:S(2)}) copy-start(bf16[1152,1152]{1,0:T(8,128)(2,1)} %param.10) | copy-start | bytes 7962628
  2.0 11.1 %copy-start.13 = (s32[1,192]{1,0:T(1,128)S(1)}, s32[1,192]{1,0:T(1,128)}, u32[]{:S(2)}) copy-start(s32[1,192]{1,0:T(1,128)} %param.9) | copy-start | bytes 2308
  3.2 41.5 %collective-permute-start = (bf16[192,1152]{1,0:T(8,128)(2,1)S(1)}, bf16[192,1152]{1,0:T(8,128)(2,1)S(1)}, u32[]{:S(2)}, u32[]{:S(2)}) collective-permute-start(bf16[192,1152]{1,0:T(8,128)(2,1)S(1)} %fusion.14), channel_id=1, source_target_pairs={{0,4},{2,6},{4,0},{6,2},{1,5},{3,7},{5,1},{7,3},{8,12},{10,14},{12... | collective-permute-start | bytes 1327112 | tf_op jit(solution)/shard_map/ppermute | solution.py:18
  7.2 28.0 %collective-permute-start.2 = (bf16[192,1152]{1,0:T(8,128)(2,1)}, bf16[192,1152]{1,0:T(8,128)(2,1)}, u32[]{:S(2)}, u32[]{:S(2)}) collective-permute-start(bf16[192,1152]{1,0:T(8,128)(2,1)} %param.8), channel_id=1, source_target_pairs={{760,0},{0,8},{8,16},{16,24},{24,32},{32,40},{40,48},{48,56},{56,6... | collective-permute-start | bytes 1327112 | tf_op jit(solution)/shard_map/ppermute | solution.py:145
  35.2 16.6 %collective-permute-start.3 = (bf16[192,1152]{1,0:T(8,128)(2,1)}, bf16[192,1152]{1,0:T(8,128)(2,1)S(1)}, u32[]{:S(2)}, u32[]{:S(2)}) collective-permute-start(bf16[192,1152]{1,0:T(8,128)(2,1)} %collective-permute-done.2), channel_id=1, source_target_pairs={{0,2},{2,0},{4,6},{6,4},{1,3},{3,1},{5,7},{7,5},{8,10},{10,8},{12,... | collective-permute-start | bytes 1327112 | tf_op jit(solution)/shard_map/ppermute | solution.py:18
  44.7 11.4 %collective-permute-start.1 = (bf16[384,1152]{1,0:T(8,128)(2,1)S(1)}, bf16[384,1152]{1,0:T(8,128)(2,1)S(1)}, u32[]{:S(2)}, u32[]{:S(2)}) collective-permute-start(bf16[384,1152]{1,0:T(8,128)(2,1)S(1)} %pad_maximum_fusion.1), channel_id=1, source_target_pairs={{0,1},{1,0},{2,3},{3,2},{4,5},{5,4},{6,7},{7,6},{8,9},{9,8},{10,11... | collective-permute-start | bytes 2654216 | tf_op jit(solution)/shard_map/ppermute | solution.py:18
  61.3 11.0 %collective-permute-start.4 = (bf16[640,1152]{1,0:T(8,128)(2,1)}, bf16[640,1152]{1,0:T(8,128)(2,1)}, u32[]{:S(2)}, u32[]{:S(2)}) collective-permute-start(bf16[640,1152]{1,0:T(8,128)(2,1)} %convolution_convert_fusion), channel_id=1, source_target_pairs={{0,1},{1,0},{2,3},{3,2},{4,5},{5,4},{6,7},{7,6},{8,9},{9,8},{10,11... | collective-permute-start | bytes 4423688 | tf_op jit(solution)/shard_map/ppermute | solution.py:18
  63.3 28.0 %collective-permute-start.8 = (bf16[192,1152]{1,0:T(8,128)(2,1)S(1)}, bf16[192,1152]{1,0:T(8,128)(2,1)S(1)}, u32[]{:S(2)}, u32[]{:S(2)}) collective-permute-start(bf16[192,1152]{1,0:T(8,128)(2,1)S(1)} %slice.56), channel_id=1, source_target_pairs={{0,2},{2,0},{4,6},{6,4},{1,3},{3,1},{5,7},{7,5},{8,10},{10,8},{12,... | collective-permute-start | bytes 1327112 | tf_op jit(solution)/shard_map/ppermute | solution.py:18
  73.8 27.4 %collective-permute-start.7 = (bf16[160,1152]{1,0:T(8,128)(2,1)S(1)}, bf16[160,1152]{1,0:T(8,128)(2,1)S(1)}, u32[]{:S(2)}, u32[]{:S(2)}) collective-permute-start(bf16[160,1152]{1,0:T(8,128)(2,1)S(1)} %get-tuple-element.30), channel_id=1, source_target_pairs={{0,24},{8,0},{16,8},{24,16},{1,25},{9,1},{17,9},{25,17},{2,26},{10... | collective-permute-start | bytes 1105928 | tf_op jit(solution)/shard_map/ppermute | solution.py:23
  84.8 21.7 %collective-permute-start.6 = (bf16[160,1152]{1,0:T(8,128)(2,1)S(1)}, bf16[160,1152]{1,0:T(8,128)(2,1)S(1)}, u32[]{:S(2)}, u32[]{:S(2)}) collective-permute-start(bf16[160,1152]{1,0:T(8,128)(2,1)S(1)} %get-tuple-element.31), channel_id=1, source_target_pairs={{0,8},{8,16},{16,24},{24,0},{1,9},{9,17},{17,25},{25,1},{2,10},{10... | collective-permute-start | bytes 1105928 | tf_op jit(solution)/shard_map/ppermute | solution.py:23
  86.7 19.8 %collective-permute-start.5 = (bf16[160,1152]{1,0:T(8,128)(2,1)S(1)}, bf16[160,1152]{1,0:T(8,128)(2,1)S(1)}, u32[]{:S(2)}, u32[]{:S(2)}) collective-permute-start(bf16[160,1152]{1,0:T(8,128)(2,1)S(1)} %get-tuple-element.32), channel_id=1, source_target_pairs={{0,16},{8,24},{16,0},{24,8},{1,17},{9,25},{17,1},{25,9},{2,18},{10... | collective-permute-start | bytes 1105928 | tf_op jit(solution)/shard_map/ppermute | solution.py:23
  90.1 16.4 %copy-start.4 = (bf16[1,160,1152]{2,1,0:T(8,128)(2,1)}, bf16[1,160,1152]{2,1,0:T(8,128)(2,1)S(1)}, u32[]{:S(2)}) copy-start(bf16[1,160,1152]{2,1,0:T(8,128)(2,1)S(1)} %constant_dynamic-slice_fusion.1) | copy-start | bytes 1105924
  91.3 16.2 %copy-start.5 = (bf16[1,160,1152]{2,1,0:T(8,128)(2,1)}, bf16[1,160,1152]{2,1,0:T(8,128)(2,1)S(1)}, u32[]{:S(2)}) copy-start(bf16[1,160,1152]{2,1,0:T(8,128)(2,1)S(1)} %constant_dynamic-slice_fusion) | copy-start | bytes 1105924
  91.3 16.2 %copy-start.8 = (bf16[192,1152]{1,0:T(8,128)(2,1)}, bf16[192,1152]{1,0:T(8,128)(2,1)S(1)}, u32[]{:S(2)}) copy-start(bf16[192,1152]{1,0:T(8,128)(2,1)S(1)} %collective-permute-done.8) | copy-start | bytes 1327108
  101.2 10.4 %copy-start.10 = (bf16[160,1152]{1,0:T(8,128)(2,1)}, bf16[160,1152]{1,0:T(8,128)(2,1)S(1)}, u32[]{:S(2)}) copy-start(bf16[160,1152]{1,0:T(8,128)(2,1)S(1)} %collective-permute-done.7) | copy-start | bytes 1105924
  107.5 12.1 %collective-permute-start.10 = (bf16[40,1152]{1,0:T(8,128)(2,1)}, bf16[40,1152]{1,0:T(8,128)(2,1)}, u32[]{:S(2)}, u32[]{:S(2)}) collective-permute-start(bf16[40,1152]{1,0:T(8,128)(2,1)} %get-tuple-element.33), channel_id=1, source_target_pairs={{0,4},{2,6},{4,0},{6,2},{1,5},{3,7},{5,1},{7,3},{8,12},{10,14},{12... | collective-permute-start | bytes 276488 | tf_op jit(solution)/shard_map/ppermute | solution.py:18
  111.6 8.0 %collective-permute-start.12 = (bf16[40,1152]{1,0:T(8,128)(2,1)}, bf16[40,1152]{1,0:T(8,128)(2,1)}, u32[]{:S(2)}, u32[]{:S(2)}) collective-permute-start(bf16[40,1152]{1,0:T(8,128)(2,1)} %get-tuple-element.34), channel_id=1, source_target_pairs={{0,2},{2,0},{4,6},{6,4},{1,3},{3,1},{5,7},{7,5},{8,10},{10,8},{12,... | collective-permute-start | bytes 276488 | tf_op jit(solution)/shard_map/ppermute | solution.py:18
  113.8 8.7 %collective-permute-start.11 = (bf16[40,1152]{1,0:T(8,128)(2,1)}, bf16[40,1152]{1,0:T(8,128)(2,1)}, u32[]{:S(2)}, u32[]{:S(2)}) collective-permute-start(bf16[40,1152]{1,0:T(8,128)(2,1)} %get-tuple-element.35), channel_id=1, source_target_pairs={{0,6},{2,4},{4,2},{6,0},{1,7},{3,5},{5,3},{7,1},{8,14},{10,12},{12... | collective-permute-start | bytes 276488 | tf_op jit(solution)/shard_map/ppermute | solution.py:18
  117.7 18.4 %collective-permute-start.9 = (bf16[384,1152]{1,0:T(8,128)(2,1)}, bf16[384,1152]{1,0:T(8,128)(2,1)}, u32[]{:S(2)}, u32[]{:S(2)}) collective-permute-start(bf16[384,1152]{1,0:T(8,128)(2,1)} %slice.98), channel_id=1, source_target_pairs={{0,1},{1,0},{2,3},{3,2},{4,5},{5,4},{6,7},{7,6},{8,9},{9,8},{10,11... | collective-permute-start | bytes 2654216 | tf_op jit(solution)/shard_map/ppermute | solution.py:18
  124.4 10.7 %collective-permute-start.13 = (bf16[40,1152]{1,0:T(8,128)(2,1)}, bf16[40,1152]{1,0:T(8,128)(2,1)}, u32[]{:S(2)}, u32[]{:S(2)}) collective-permute-start(bf16[40,1152]{1,0:T(8,128)(2,1)} %fusion.27), channel_id=1, source_target_pairs={{0,32},{32,0},{1,33},{33,1},{2,34},{34,2},{3,35},{35,3},{4,36},{36... | collective-permute-start | bytes 276488 | tf_op jit(solution)/shard_map/ppermute | solution.py:18
  137.9 31.2 %copy-start.9 = (bf16[192,1152]{1,0:T(8,128)(2,1)S(1)}, bf16[192,1152]{1,0:T(8,128)(2,1)}, u32[]{:S(2)}) copy-start(bf16[192,1152]{1,0:T(8,128)(2,1)} %copy-done.8) | copy-start | bytes 1327108
  138.0 13.5 %collective-permute-start.16 = (bf16[40,1152]{1,0:T(8,128)(2,1)S(1)}, bf16[40,1152]{1,0:T(8,128)(2,1)S(1)}, u32[]{:S(2)}, u32[]{:S(2)}) collective-permute-start(bf16[40,1152]{1,0:T(8,128)(2,1)S(1)} %reduce-precision_convert_fusion.9), channel_id=1, source_target_pairs={{0,192},{64,128},{128,64},{192,0},{256,448},{320,384},{384,320},{4... | collective-permute-start | bytes 276488 | tf_op jit(solution)/shard_map/ppermute | solution.py:18
  140.0 11.4 %collective-permute-start.15 = (bf16[40,1152]{1,0:T(8,128)(2,1)S(1)}, bf16[40,1152]{1,0:T(8,128)(2,1)S(1)}, u32[]{:S(2)}, u32[]{:S(2)}) collective-permute-start(bf16[40,1152]{1,0:T(8,128)(2,1)S(1)} %reduce-precision_convert_fusion.9), channel_id=1, source_target_pairs={{0,128},{64,192},{128,0},{192,64},{256,384},{320,448},{384,256},{4... | collective-permute-start | bytes 276488 | tf_op jit(solution)/shard_map/ppermute | solution.py:18
  141.9 9.5 %collective-permute-start.14 = (bf16[40,1152]{1,0:T(8,128)(2,1)S(1)}, bf16[40,1152]{1,0:T(8,128)(2,1)S(1)}, u32[]{:S(2)}, u32[]{:S(2)}) collective-permute-start(bf16[40,1152]{1,0:T(8,128)(2,1)S(1)} %reduce-precision_convert_fusion.9), channel_id=1, source_target_pairs={{0,64},{64,0},{128,192},{192,128},{256,320},{320,256},{384,448},{4... | collective-permute-start | bytes 276488 | tf_op jit(solution)/shard_map/ppermute | solution.py:18
  148.3 11.1 %collective-permute-start.17 = (bf16[96,1152]{1,0:T(8,128)(2,1)S(1)}, bf16[96,1152]{1,0:T(8,128)(2,1)S(1)}, u32[]{:S(2)}, u32[]{:S(2)}) collective-permute-start(bf16[96,1152]{1,0:T(8,128)(2,1)S(1)} %get-tuple-element.37), channel_id=1, source_target_pairs={{0,4},{2,6},{4,0},{6,2},{1,5},{3,7},{5,1},{7,3},{8,12},{10,14},{12... | collective-permute-start | bytes 663560 | tf_op jit(solution)/shard_map/ppermute | solution.py:18
  151.5 37.8 %copy-start.3 = (bf16[192,1152]{1,0:T(8,128)(2,1)S(1)}, bf16[192,1152]{1,0:T(8,128)(2,1)}, u32[]{:S(2)}) copy-start(bf16[192,1152]{1,0:T(8,128)(2,1)} %param.7) | copy-start | bytes 1327108
  159.4 13.6 %collective-permute-start.19 = (bf16[40,1152]{1,0:T(8,128)(2,1)S(1)}, bf16[40,1152]{1,0:T(8,128)(2,1)S(1)}, u32[]{:S(2)}, u32[]{:S(2)}) collective-permute-start(bf16[40,1152]{1,0:T(8,128)(2,1)S(1)} %reduce-precision_convert_fusion.8), channel_id=1, source_target_pairs={{0,256},{64,320},{128,384},{192,448},{256,512},{320,576},{384,640}... | collective-permute-start | bytes 276488 | tf_op jit(solution)/shard_map/ppermute | solution.py:23
  164.8 14.9 %collective-permute-start.18 = (bf16[40,1152]{1,0:T(8,128)(2,1)S(1)}, bf16[40,1152]{1,0:T(8,128)(2,1)S(1)}, u32[]{:S(2)}, u32[]{:S(2)}) collective-permute-start(bf16[40,1152]{1,0:T(8,128)(2,1)S(1)} %reduce-precision_convert_fusion.8), channel_id=1, source_target_pairs={{0,512},{64,576},{128,640},{192,704},{256,0},{320,64},{384,128},{4... | collective-permute-start | bytes 276488 | tf_op jit(solution)/shard_map/ppermute | solution.py:23
  171.1 10.1 %collective-permute-start.20 = (bf16[96,1152]{1,0:T(8,128)(2,1)S(1)}, bf16[96,1152]{1,0:T(8,128)(2,1)S(1)}, u32[]{:S(2)}, u32[]{:S(2)}) collective-permute-start(bf16[96,1152]{1,0:T(8,128)(2,1)S(1)} %get-tuple-element.36), channel_id=1, source_target_pairs={{0,4},{2,6},{4,0},{6,2},{1,5},{3,7},{5,1},{7,3},{8,12},{10,14},{12... | collective-permute-start | bytes 663560 | tf_op jit(solution)/shard_map/ppermute | solution.py:18
  181.2 9.7 %collective-permute-start.23 = (bf16[40,1152]{1,0:T(8,128)(2,1)S(1)}, bf16[40,1152]{1,0:T(8,128)(2,1)S(1)}, u32[]{:S(2)}, u32[]{:S(2)}) collective-permute-start(bf16[40,1152]{1,0:T(8,128)(2,1)S(1)} %reduce-precision_convert_fusion.7), channel_id=1, source_target_pairs={{0,24},{8,0},{16,8},{24,16},{1,25},{9,1},{17,9},{25,17},{2,26},{10... | collective-permute-start | bytes 276488 | tf_op jit(solution)/shard_map/ppermute | solution.py:23
  183.1 7.8 %collective-permute-start.22 = (bf16[40,1152]{1,0:T(8,128)(2,1)S(1)}, bf16[40,1152]{1,0:T(8,128)(2,1)S(1)}, u32[]{:S(2)}, u32[]{:S(2)}) collective-permute-start(bf16[40,1152]{1,0:T(8,128)(2,1)S(1)} %reduce-precision_convert_fusion.7), channel_id=1, source_target_pairs={{0,8},{8,16},{16,24},{24,0},{1,9},{9,17},{17,25},{25,1},{2,10},{10... | collective-permute-start | bytes 276488 | tf_op jit(solution)/shard_map/ppermute | solution.py:23
  187.0 7.9 %collective-permute-start.21 = (bf16[40,1152]{1,0:T(8,128)(2,1)S(1)}, bf16[40,1152]{1,0:T(8,128)(2,1)S(1)}, u32[]{:S(2)}, u32[]{:S(2)}) collective-permute-start(bf16[40,1152]{1,0:T(8,128)(2,1)S(1)} %reduce-precision_convert_fusion.7), channel_id=1, source_target_pairs={{0,16},{8,24},{16,0},{24,8},{1,17},{9,25},{17,1},{25,9},{2,18},{10... | collective-permute-start | bytes 276488 | tf_op jit(solution)/shard_map/ppermute | solution.py:23
  (7 other events, 20.9 us)

commit v3 on v2

--- a/solution.py
+++ b/solution.py
@@ -62,20 +62,22 @@
     rows = pictures.shape[0]
     z, x, y, k = (lax.axis_index(a) for a in ("z", "x", "y", "k"))
 
-    paired = turn_col(captions)
+    paired, crossed = shifted(captions, x)
     picture = pictures.astype(f32)
     image_scale = lax.rsqrt(jnp.sum(picture * picture, -1, keepdims=True) + eps)
     image_unit = picture * image_scale
     image_low = image_unit.astype(bf16)
-    pair = jnp.concatenate([image_low, swap(image_low, "y", 2)])
-    images = jnp.concatenate([pair, swap(pair, "k", 1)])
+    image_core = swap(image_low, "k", 1)
+    image_out, _ = tie(image_low, crossed)
+    image_far = swap(image_out, "y", 2)
+    images = jnp.concatenate([image_low, image_far, image_core, swap(image_far, "k", 1)])
     texts = jnp.concatenate([paired, swap(paired, "y", 1)])
 
     projected = dot(texts, matrix, 1, 0) + intercept
     text_scale = lax.rsqrt(jnp.sum(projected * projected, -1, keepdims=True) + eps)
     text_unit = projected * text_scale
     text_low = text_unit.astype(bf16)
-    texts_sent, texts_kept = tie(head_rows(texts, 1 - k), head_rows(texts, k))
+    (texts_sent,) = tie(head_rows(texts, 1 - k))
 
     scores = sharp * dot(images, text_low, 1, 1) + moved
     wanted = jnp.concatenate([slot[0], jnp.full((3 * rows,), -1, jnp.int32)])
@@ -89,15 +91,22 @@
     grad_low = low(grad)
 
     sent = dot(texts_sent, grad_low, 0, 0).astype(bf16)
+    sent, texts = tie(sent, texts)
     arrived = swap(sent, "k", 1)
-    kept = dot(texts_kept, grad_low, 0, 0).astype(bf16)
+    kept = dot(head_rows(texts, k), grad_low, 0, 0).astype(bf16)
     parts = [p.reshape(4, 4 * PAD, D) for p in (kept, arrived)]
 
-    over_x = {d: turn(low(pick(parts, (x + d) % 4)), "x", d) for d in (2, 1, 3)}
-    grad_far = swap(grad_low[rows:], "y", 1)
-    image_dir = sharp * dot(weight, text_low, 1, 0)
-    image_sent = image_dir[2 * rows :].astype(bf16)
-    *over_x, image_sent, grad_far = tie(*over_x.values(), image_sent, grad_far)
+    pieces = [low(pick(parts, (x + d) % 4)) for d in (2, 1, 3)]
+    *pieces, weight, grad_sent = tie(*pieces, weight, grad_low[rows:])
+    over_x = [turn(piece, "x", d) for piece, d in zip(pieces, (2, 1, 3))]
+    image_sent = (sharp * dot(weight[2 * rows :], text_low, 1, 0)).astype(bf16)
+    image_core = swap(image_sent, "k", 1)
+    grad_far = swap(grad_sent, "y", 1)
+    image_kept = sharp * dot(weight[: 2 * rows], text_low, 1, 0)
+    image_sent = low(image_kept[rows:] + image_core[rows:].astype(f32))
+    far_one = swap(image_sent[: rows // 2], "y", 2)
+    *over_x, image_sent, grad_far, far_one = tie(*over_x, image_sent, grad_far, far_one)
+    far_two = swap(image_sent[rows // 2 :], "y", 2)
     projected_grad = grad_low[:rows].astype(f32) + grad_far.astype(f32)
     text_grad = dot(projected_grad.astype(bf16), matrix, 1, 1)
 
@@ -110,23 +119,19 @@
     head = low(total)
     head = low(head.astype(f32) + swap(head, "h", 1).astype(f32))
 
-    mine = image_dir[: 2 * rows] + swap(image_sent, "k", 1).astype(f32)
-    image_far = mine[rows:].astype(bf16)
-    head, image_far = tie(head, image_far)
+    head, far_two = tie(head, far_two)
+    own = image_kept[:rows] + image_core[:rows].astype(f32)
+    own = own + jnp.concatenate([far_one, far_two]).astype(f32)
 
     over_z = {m: swap(head, "z", m).astype(f32) for m in (2, 3, 1)}
     head = low((head.astype(f32) + over_z[1]) + (over_z[2] + over_z[3]))
-    far_one = swap(image_far[: rows // 2], "y", 2)
-    head, far_one = tie(head, far_one)
     ring = [head, turn(head, "z", 8), turn(head, "z", 4)]
     u = z // 4
     total = 0.0
     for j in range(3):
         at = (j - u) % 3
         total = total + jnp.where(at == 0, ring[0], jnp.where(at == 1, ring[1], ring[2])).astype(f32)
-    far_two = swap(image_far[rows // 2 :], "y", 2)
-    head, far_two = tie(low(total), far_two)
-    own = mine[:rows] + jnp.concatenate([far_one, far_two]).astype(f32)
+    head = low(total)
     around = [head] + [turn(head, "x", d) for d in (2, 1, 3)]
     ordered = []
     for q in range(4):
@@ -141,8 +146,20 @@
     return (image_grad, text_grad, head_grad, bias_grad)
 
 
-def turn_col(block):
-    return lax.ppermute(block, COL, [((i - 1) % 96, i) for i in range(96)])
+def shifted(block, x):
+    def cross(half, plane):
+        pairs = []
+        for group in range(plane, 96, 4):
+            pairs.append((group, (group + 4) % 96))
+        return lax.ppermute(half, COL, pairs)
+
+    half = block.shape[0] // 2
+    low_half, high_half = tie(block[:half], block[half:])
+    crossed = cross(high_half, 3)
+    moved = turn(low_half, "x", 1)
+    first = jnp.where(x == 0, cross(moved, 0), moved)
+    second = turn(jnp.where(x == 3, crossed, high_half), "x", 1)
+    return jnp.concatenate([first, second]), crossed
 
 
 def solution(mesh):

time: 200 us -> 212 us (1.060)
  the two profiles are of different devices: /device:TPU:56 before, /device:TPU:134 now
where the time goes in v3:
time: 212 us; the launch traced here: 211 us
  starting transfers between devices  106 us (50%)
  waiting for transfers between devices  55.5 us (26%)
  matrix products  21.3 us (10%)
  other arithmetic  20.7 us (10%)
  local copies, waits for them, and re-layouts  5.17 us (2%)
  between operations  2.76 us (1%)
    ppermute x16, starting transfers between devices, swap(): return lax.ppermute(block, axis, [(i, i ^ mask) for i in range(n)])  52.5 us
    ppermute x10, starting transfers between devices, turn(): lax.ppermute(block, axis, [(i, (i + distance) % n) for i in range(n)])  44.6 us
    ppermute x16, waiting for transfers between devices, swap(): return lax.ppermute(block, axis, [(i, i ^ mask) for i in range(n)])  35 us
    dot_general x9, matrix products, dot(): lax.dot_general(a, b, (((ca,), (cb,)), ((), ())), preferred_element_type=...  21.3 us
    ppermute x10, waiting for transfers between devices, turn(): lax.ppermute(block, axis, [(i, (i + distance) % n) for i in range(n)])  20.2 us
    convert_element_type x8, other arithmetic, low(): return lax.reduce_precision(values, 8, 7).astype(bf16)  8.45 us
    ppermute x2, starting transfers between devices, cross(): return lax.ppermute(half, COL, pairs)  8.4 us
  transfers between devices with their start and end apart: 28, of which 13 were waited for; matrix products, arithmetic and copies ran while one was open for 14% of the time, Pallas kernels for 0%

profile of v3, /device:TPU:134, one launch (start us, length us, event | category | flops | bytes accessed | tf_op | source)
XLA Modules:
  0.0 210.9 jit_solution(15818997792909662853)
XLA Ops:
  1.9 7.7 %collective-permute-start.2 = (bf16[96,1152]{1,0:T(8,128)(2,1)S(1)}, bf16[96,1152]{1,0:T(8,128)(2,1)S(1)}, u32[]{:S(2)}, u32[]{:S(2)}) collective-permute-start(bf16[96,1152]{1,0:T(8,128)(2,1)S(1)} %get-tuple-element.23), channel_id=1, source_target_pairs={{24,56},{56,88},{88,120},{120,152},{152,184},{184,216},{216,248},{... | collective-permute-start | bytes 663560 | tf_op jit(solution)/shard_map/ppermute | solution.py:154
  19.4 6.3 %collective-permute-start.3 = (bf16[96,1152]{1,0:T(8,128)(2,1)S(1)}, bf16[96,1152]{1,0:T(8,128)(2,1)S(1)}, u32[]{:S(2)}, u32[]{:S(2)}) collective-permute-start(bf16[96,1152]{1,0:T(8,128)(2,1)S(1)} %broadcast_select_fusion), channel_id=1, source_target_pairs={{0,8},{8,16},{16,24},{24,0},{1,9},{9,17},{17,25},{25,1},{2,10},{10... | collective-permute-start | bytes 663560 | tf_op jit(solution)/shard_map/ppermute | solution.py:23
  25.7 4.5 %collective-permute-start.5 = (bf16[192,1152]{1,0:T(8,128)(2,1)}, bf16[192,1152]{1,0:T(8,128)(2,1)S(1)}, u32[]{:S(2)}, u32[]{:S(2)}) collective-permute-start(bf16[192,1152]{1,0:T(8,128)(2,1)} %fusion.15), channel_id=1, source_target_pairs={{0,4},{2,6},{4,0},{6,2},{1,5},{3,7},{5,1},{7,3},{8,12},{10,14},{12... | collective-permute-start | bytes 1327112 | tf_op jit(solution)/shard_map/ppermute | solution.py:18
  30.3 3.5 %collective-permute-start.4 = (bf16[192,1152]{1,0:T(8,128)(2,1)S(1)}, bf16[192,1152]{1,0:T(8,128)(2,1)S(1)}, u32[]{:S(2)}, u32[]{:S(2)}) collective-permute-start(bf16[192,1152]{1,0:T(8,128)(2,1)S(1)} %pad_maximum_fusion.2), channel_id=1, source_target_pairs={{0,2},{2,0},{4,6},{6,4},{1,3},{3,1},{5,7},{7,5},{8,10},{10,8},{12,... | collective-permute-start | bytes 1327112 | tf_op jit(solution)/shard_map/ppermute | solution.py:18
  34.4 14.4 %collective-permute-done.5 = bf16[192,1152]{1,0:T(8,128)(2,1)S(1)} collective-permute-done((bf16[192,1152]{1,0:T(8,128)(2,1)}, bf16[192,1152]{1,0:T(8,128)(2,1)S(1)}, u32[]{:S(2)}, u32[]{:S(2)}) %collective-permute-start.5) | collective-permute-done | bytes 442400 | tf_op jit(solution)/shard_map/ppermute | solution.py:18
  54.4 2.8 %fusion.12 = bf16[768,384]{1,0:T(8,128)(2,1)S(1)} fusion(bf16[384,1152]{1,0:T(8,128)(2,1)S(1)} %multiply_convert_fusion, f32[]{:T(128)} %bitcast.50, f32[]{:T(128)} %bitcast.47, s32[768]{0:T(1024)S(1)} %concatenate.21, bf16[192,1152]{1,0:T(8,128)(2,1)S(1)} %collective-permute-done.7, bf16[192,1152]{1,0:T(8,128)(2,1)} %collective-permute-done.6, ...), kind=kOutput, calls=%fused_computation.28 | convolution fusion | flops 689799168 | bytes 3247112 | tf_op jit(solution)/shard_map/dot_general | solution.py:31
  57.3 2.5 %multiply_reduce_fusion = (f32[384]{0:T(512)S(1)}, f32[384,1152]{1,0:T(8,128)S(1)}) fusion(f32[384,1152]{1,0:T(8,128)S(1)} %get-tuple-element.51, f32[384]{0:T(512)S(1)} %add_rsqrt_fusion, bf16[768,384]{1,0:T(8,128)(2,1)S(1)} %fusion.12, bf16[192,1152]{1,0:T(8,128)(2,1)S(1)} %collective-permute-done.7, bf16[192,1152]{1,0:T(8,128)(2,1)} %collective-permute-done.6, ...), kind=kOutput, calls=%fused_computation.13 | convolution fusion | flops 688324224 | bytes 5901316 | tf_op jit(solution)/shard_map/dot_general | solution.py:31
  62.3 2.3 %collective-permute-start.8 = (bf16[640,1152]{1,0:T(8,128)(2,1)}, bf16[640,1152]{1,0:T(8,128)(2,1)}, u32[]{:S(2)}, u32[]{:S(2)}) collective-permute-start(bf16[640,1152]{1,0:T(8,128)(2,1)} %convolution_convert_fusion.1), channel_id=1, source_target_pairs={{0,1},{1,0},{2,3},{3,2},{4,5},{5,4},{6,7},{7,6},{8,9},{9,8},{10,11... | collective-permute-start | bytes 4423688 | tf_op jit(solution)/shard_map/ppermute | solution.py:18
  67.2 4.9 %convolution_convert_fusion = bf16[640,1152]{1,0:T(8,128)(2,1)} fusion(bf16[384,1152]{1,0:T(8,128)(2,1)S(1)} %reduce-precision_convert_fusion, bf16[384,1152]{1,0:T(8,128)(2,1)} %pad_maximum_fusion.1, bf16[1152,640]{1,0:T(8,128)(2,1)} %fusion.1, f32[640]{0:T(1024)S(1)} %fusion.47), kind=kOutput, calls=%fused_computation | convolution fusion | flops 1133690880 | bytes 4721152 | tf_op jit(solution)/shard_map/dot_general | solution.py:31
  72.2 2.8 %fusion.28 = (bf16[160,1152]{1,0:T(8,128)(2,1)}, bf16[160,1152]{1,0:T(8,128)(2,1)}, bf16[160,1152]{1,0:T(8,128)(2,1)}) fusion(bf16[4,160,1152]{2,1,0:T(8,128)(2,1)} %bitcast.4, s32[]{:T(128)S(6)} %select_n.330, bf16[4,160,1152]{2,1,0:T(8,128)(2,1)} %bitcast.55, s32[]{:T(128)S(6)} %select_n.328, s32[]{:T(128)S(6)} %select_n.326), kind=kLoop, calls=%fused_computation.55 | loop fusion | flops 2764800 | bytes 3317772 | tf_op jit(solution)/shard_map/convert_element_type | solution.py:27
  79.6 2.6 %collective-permute-start.13 = (bf16[192,1152]{1,0:T(8,128)(2,1)}, bf16[192,1152]{1,0:T(8,128)(2,1)S(1)}, u32[]{:S(2)}, u32[]{:S(2)}) collective-permute-start(bf16[192,1152]{1,0:T(8,128)(2,1)} %slice.68), channel_id=1, source_target_pairs={{0,2},{2,0},{4,6},{6,4},{1,3},{3,1},{5,7},{7,5},{8,10},{10,8},{12,... | collective-permute-start | bytes 1327112 | tf_op jit(solution)/shard_map/ppermute | solution.py:18
  82.1 3.5 %collective-permute-start.10 = (bf16[160,1152]{1,0:T(8,128)(2,1)}, bf16[160,1152]{1,0:T(8,128)(2,1)S(1)}, u32[]{:S(2)}, u32[]{:S(2)}) collective-permute-start(bf16[160,1152]{1,0:T(8,128)(2,1)} %get-tuple-element.28), channel_id=1, source_target_pairs={{0,16},{8,24},{16,0},{24,8},{1,17},{9,25},{17,1},{25,9},{2,18},{10... | collective-permute-start | bytes 1105928 | tf_op jit(solution)/shard_map/ppermute | solution.py:23
  85.6 6.3 %collective-permute-start.11 = (bf16[160,1152]{1,0:T(8,128)(2,1)}, bf16[160,1152]{1,0:T(8,128)(2,1)S(1)}, u32[]{:S(2)}, u32[]{:S(2)}) collective-permute-start(bf16[160,1152]{1,0:T(8,128)(2,1)} %get-tuple-element.29), channel_id=1, source_target_pairs={{0,8},{8,16},{16,24},{24,0},{1,9},{9,17},{17,25},{25,1},{2,10},{10... | collective-permute-start | bytes 1105928 | tf_op jit(solution)/shard_map/ppermute | solution.py:23
  92.0 2.8 %collective-permute-start.12 = (bf16[160,1152]{1,0:T(8,128)(2,1)}, bf16[160,1152]{1,0:T(8,128)(2,1)S(1)}, u32[]{:S(2)}, u32[]{:S(2)}) collective-permute-start(bf16[160,1152]{1,0:T(8,128)(2,1)} %get-tuple-element.30), channel_id=1, source_target_pairs={{0,24},{8,0},{16,8},{24,16},{1,25},{9,1},{17,9},{25,17},{2,26},{10... | collective-permute-start | bytes 1105928 | tf_op jit(solution)/shard_map/ppermute | solution.py:23
  98.1 3.3 %collective-permute-start.14 = (bf16[96,1152]{1,0:T(8,128)(2,1)S(1)}, bf16[96,1152]{1,0:T(8,128)(2,1)}, u32[]{:S(2)}, u32[]{:S(2)}) collective-permute-start(bf16[96,1152]{1,0:T(8,128)(2,1)S(1)} %slice.73), channel_id=1, source_target_pairs={{0,4},{2,6},{4,0},{6,2},{1,5},{3,7},{5,1},{7,3},{8,12},{10,14},{12... | collective-permute-start | bytes 663560 | tf_op jit(solution)/shard_map/ppermute | solution.py:18
  102.5 5.5 %collective-permute-done.11 = bf16[160,1152]{1,0:T(8,128)(2,1)S(1)} collective-permute-done((bf16[160,1152]{1,0:T(8,128)(2,1)}, bf16[160,1152]{1,0:T(8,128)(2,1)S(1)}, u32[]{:S(2)}, u32[]{:S(2)}) %collective-permute-start.11) | collective-permute-done | bytes 368672 | tf_op jit(solution)/shard_map/ppermute | solution.py:23
  108.0 5.0 %collective-permute-done.14 = bf16[96,1152]{1,0:T(8,128)(2,1)} collective-permute-done((bf16[96,1152]{1,0:T(8,128)(2,1)S(1)}, bf16[96,1152]{1,0:T(8,128)(2,1)}, u32[]{:S(2)}, u32[]{:S(2)}) %collective-permute-start.14) | collective-permute-done | bytes 221216 | tf_op jit(solution)/shard_map/ppermute | solution.py:18
  115.9 3.3 %collective-permute-start.16 = (bf16[40,1152]{1,0:T(8,128)(2,1)}, bf16[40,1152]{1,0:T(8,128)(2,1)}, u32[]{:S(2)}, u32[]{:S(2)}) collective-permute-start(bf16[40,1152]{1,0:T(8,128)(2,1)} %get-tuple-element.45), channel_id=1, source_target_pairs={{0,6},{2,4},{4,2},{6,0},{1,7},{3,5},{5,3},{7,1},{8,14},{10,12},{12... | collective-permute-start | bytes 276488 | tf_op jit(solution)/shard_map/ppermute | solution.py:18
  119.2 4.0 %collective-permute-start.17 = (bf16[40,1152]{1,0:T(8,128)(2,1)}, bf16[40,1152]{1,0:T(8,128)(2,1)}, u32[]{:S(2)}, u32[]{:S(2)}) collective-permute-start(bf16[40,1152]{1,0:T(8,128)(2,1)} %get-tuple-element.44), channel_id=1, source_target_pairs={{0,2},{2,0},{4,6},{6,4},{1,3},{3,1},{5,7},{7,5},{8,10},{10,8},{12,... | collective-permute-start | bytes 276488 | tf_op jit(solution)/shard_map/ppermute | solution.py:18
  128.4 7.5 %collective-permute-start.18 = (bf16[40,1152]{1,0:T(8,128)(2,1)}, bf16[40,1152]{1,0:T(8,128)(2,1)}, u32[]{:S(2)}, u32[]{:S(2)}) collective-permute-start(bf16[40,1152]{1,0:T(8,128)(2,1)} %fusion.34), channel_id=1, source_target_pairs={{0,32},{32,0},{1,33},{33,1},{2,34},{34,2},{3,35},{35,3},{4,36},{36... | collective-permute-start | bytes 276488 | tf_op jit(solution)/shard_map/ppermute | solution.py:18
  137.1 3.9 %collective-permute-start.19 = (bf16[96,1152]{1,0:T(8,128)(2,1)S(1)}, bf16[96,1152]{1,0:T(8,128)(2,1)S(1)}, u32[]{:S(2)}, u32[]{:S(2)}) collective-permute-start(bf16[96,1152]{1,0:T(8,128)(2,1)S(1)} %slice.61), channel_id=1, source_target_pairs={{0,4},{2,6},{4,0},{6,2},{1,5},{3,7},{5,1},{7,3},{8,12},{10,14},{12... | collective-permute-start | bytes 663560 | tf_op jit(solution)/shard_map/ppermute | solution.py:18
  142.0 8.7 %collective-permute-done.19 = bf16[96,1152]{1,0:T(8,128)(2,1)S(1)} collective-permute-done((bf16[96,1152]{1,0:T(8,128)(2,1)S(1)}, bf16[96,1152]{1,0:T(8,128)(2,1)S(1)}, u32[]{:S(2)}, u32[]{:S(2)}) %collective-permute-start.19) | collective-permute-done | bytes 221216 | tf_op jit(solution)/shard_map/ppermute | solution.py:18
  150.6 4.6 %collective-permute-start.20 = (bf16[40,1152]{1,0:T(8,128)(2,1)S(1)}, bf16[40,1152]{1,0:T(8,128)(2,1)S(1)}, u32[]{:S(2)}, u32[]{:S(2)}) collective-permute-start(bf16[40,1152]{1,0:T(8,128)(2,1)S(1)} %reduce-precision_convert_fusion.9), channel_id=1, source_target_pairs={{0,64},{64,0},{128,192},{192,128},{256,320},{320,256},{384,448},{4... | collective-permute-start | bytes 276488 | tf_op jit(solution)/shard_map/ppermute | solution.py:18
  157.2 3.4 %collective-permute-start.22 = (bf16[40,1152]{1,0:T(8,128)(2,1)S(1)}, bf16[40,1152]{1,0:T(8,128)(2,1)S(1)}, u32[]{:S(2)}, u32[]{:S(2)}) collective-permute-start(bf16[40,1152]{1,0:T(8,128)(2,1)S(1)} %reduce-precision_convert_fusion.9), channel_id=1, source_target_pairs={{0,192},{64,128},{128,64},{192,0},{256,448},{320,384},{384,320},{4... | collective-permute-start | bytes 276488 | tf_op jit(solution)/shard_map/ppermute | solution.py:18
  160.5 3.0 %fusion.24 = f32[192,1152]{1,0:T(8,128)} fusion(bf16[1152,1152]{1,0:T(8,128)(2,1)S(1)} %copy-done, bf16[192,1152]{1,0:T(8,128)(2,1)} %copy-done.9, bf16[384,1152]{1,0:T(8,128)(2,1)S(1)} %reduce-precision_convert_fusion), kind=kOutput, calls=%fused_computation.50 | convolution fusion | flops 510492672 | bytes 4423680 | tf_op jit(solution)/shard_map/dot_general | solution.py:31
  163.5 3.6 %collective-permute-done.22 = bf16[40,1152]{1,0:T(8,128)(2,1)S(1)} collective-permute-done((bf16[40,1152]{1,0:T(8,128)(2,1)S(1)}, bf16[40,1152]{1,0:T(8,128)(2,1)S(1)}, u32[]{:S(2)}, u32[]{:S(2)}) %collective-permute-start.22) | collective-permute-done | bytes 92192 | tf_op jit(solution)/shard_map/ppermute | solution.py:18
  167.1 11.8 %collective-permute-start.23 = (bf16[40,1152]{1,0:T(8,128)(2,1)S(1)}, bf16[40,1152]{1,0:T(8,128)(2,1)S(1)}, u32[]{:S(2)}, u32[]{:S(2)}) collective-permute-start(bf16[40,1152]{1,0:T(8,128)(2,1)S(1)} %reduce-precision_convert_fusion.8), channel_id=1, source_target_pairs={{0,512},{64,576},{128,640},{192,704},{256,0},{320,64},{384,128},{4... | collective-permute-start | bytes 276488 | tf_op jit(solution)/shard_map/ppermute | solution.py:23
  184.6 8.6 %collective-permute-done.24 = bf16[40,1152]{1,0:T(8,128)(2,1)S(1)} collective-permute-done((bf16[40,1152]{1,0:T(8,128)(2,1)S(1)}, bf16[40,1152]{1,0:T(8,128)(2,1)S(1)}, u32[]{:S(2)}, u32[]{:S(2)}) %collective-permute-start.24) | collective-permute-done | bytes 92192 | tf_op jit(solution)/shard_map/ppermute | solution.py:23
  193.4 4.0 %collective-permute-start.25 = (bf16[40,1152]{1,0:T(8,128)(2,1)S(1)}, bf16[40,1152]{1,0:T(8,128)(2,1)S(1)}, u32[]{:S(2)}, u32[]{:S(2)}) collective-permute-start(bf16[40,1152]{1,0:T(8,128)(2,1)S(1)} %reduce-precision_convert_fusion.7), channel_id=1, source_target_pairs={{0,16},{8,24},{16,0},{24,8},{1,17},{9,25},{17,1},{25,9},{2,18},{10... | collective-permute-start | bytes 276488 | tf_op jit(solution)/shard_map/ppermute | solution.py:23
  197.3 4.2 %collective-permute-start.26 = (bf16[40,1152]{1,0:T(8,128)(2,1)S(1)}, bf16[40,1152]{1,0:T(8,128)(2,1)S(1)}, u32[]{:S(2)}, u32[]{:S(2)}) collective-permute-start(bf16[40,1152]{1,0:T(8,128)(2,1)S(1)} %reduce-precision_convert_fusion.7), channel_id=1, source_target_pairs={{0,8},{8,16},{16,24},{24,0},{1,9},{9,17},{17,25},{25,1},{2,10},{10... | collective-permute-start | bytes 276488 | tf_op jit(solution)/shard_map/ppermute | solution.py:23
  203.5 2.4 %fusion.18 = f32[192,1152]{1,0:T(8,128)} fusion(bf16[192,1152]{1,0:T(8,128)(2,1)S(1)} %copy-done.3, f32[192]{0:T(256)S(1)} %fusion.16, f32[192]{0:T(256)S(1)} %add_rsqrt_fusion.1, bf16[96,1152]{1,0:T(8,128)(2,1)S(1)} %collective-permute-done.19, bf16[96,1152]{1,0:T(8,128)(2,1)} %collective-permute-done.14, bf16[384,1152]{1,0:T(8,128)(2,1)} %collective-permute-done.9, ...), kind=kLoop, calls=%fused_computation.37 | loop fusion | flops 2654208 | bytes 3098112 | tf_op jit(solution)/shard_map/mul | solution.py:145
  205.9 3.4 %collective-permute-done.27 = bf16[40,1152]{1,0:T(8,128)(2,1)S(1)} collective-permute-done((bf16[40,1152]{1,0:T(8,128)(2,1)S(1)}, bf16[40,1152]{1,0:T(8,128)(2,1)S(1)}, u32[]{:S(2)}, u32[]{:S(2)}) %collective-permute-start.27) | collective-permute-done | bytes 92192 | tf_op jit(solution)/shard_map/ppermute | solution.py:23
  (103 shorter events, 51.2 us)
Async XLA Ops:
  0.6 50.1 %copy-start = (bf16[1152,1152]{1,0:T(8,128)(2,1)S(1)}, bf16[1152,1152]{1,0:T(8,128)(2,1)}, u32[]{:S(2)}) copy-start(bf16[1152,1152]{1,0:T(8,128)(2,1)} %param.10) | copy-start | bytes 7962628
  1.9 17.5 %collective-permute-start.2 = (bf16[96,1152]{1,0:T(8,128)(2,1)S(1)}, bf16[96,1152]{1,0:T(8,128)(2,1)S(1)}, u32[]{:S(2)}, u32[]{:S(2)}) collective-permute-start(bf16[96,1152]{1,0:T(8,128)(2,1)S(1)} %get-tuple-element.23), channel_id=1, source_target_pairs={{24,56},{56,88},{88,120},{120,152},{152,184},{184,216},{216,248},{... | collective-permute-start | bytes 663560 | tf_op jit(solution)/shard_map/ppermute | solution.py:154
  9.6 8.8 %collective-permute-start = (bf16[96,1152]{1,0:T(8,128)(2,1)S(1)}, bf16[96,1152]{1,0:T(8,128)(2,1)S(1)}, u32[]{:S(2)}, u32[]{:S(2)}) collective-permute-start(bf16[96,1152]{1,0:T(8,128)(2,1)S(1)} %get-tuple-element.22), channel_id=1, source_target_pairs={{0,8},{8,16},{16,24},{24,0},{1,9},{9,17},{17,25},{25,1},{2,10},{10... | collective-permute-start | bytes 663560 | tf_op jit(solution)/shard_map/ppermute | solution.py:23
  14.7 39.8 %collective-permute-start.6 = (bf16[192,1152]{1,0:T(8,128)(2,1)}, bf16[192,1152]{1,0:T(8,128)(2,1)}, u32[]{:S(2)}, u32[]{:S(2)}) collective-permute-start(bf16[192,1152]{1,0:T(8,128)(2,1)} %fusion.15), channel_id=1, source_target_pairs={{0,1},{1,0},{2,3},{3,2},{4,5},{5,4},{6,7},{7,6},{8,9},{9,8},{10,11... | collective-permute-start | bytes 1327112 | tf_op jit(solution)/shard_map/ppermute | solution.py:18
  18.4 11.8 %collective-permute-start.1 = (bf16[96,1152]{1,0:T(8,128)(2,1)S(1)}, bf16[96,1152]{1,0:T(8,128)(2,1)S(1)}, u32[]{:S(2)}, u32[]{:S(2)}) collective-permute-start(bf16[96,1152]{1,0:T(8,128)(2,1)S(1)} %collective-permute-done), channel_id=1, source_target_pairs={{0,32},{32,64},{64,96},{96,128},{128,160},{160,192},{192,224},{224... | collective-permute-start | bytes 663560 | tf_op jit(solution)/shard_map/ppermute | solution.py:154
  19.4 10.9 %collective-permute-start.3 = (bf16[96,1152]{1,0:T(8,128)(2,1)S(1)}, bf16[96,1152]{1,0:T(8,128)(2,1)S(1)}, u32[]{:S(2)}, u32[]{:S(2)}) collective-permute-start(bf16[96,1152]{1,0:T(8,128)(2,1)S(1)} %broadcast_select_fusion), channel_id=1, source_target_pairs={{0,8},{8,16},{16,24},{24,0},{1,9},{9,17},{17,25},{25,1},{2,10},{10... | collective-permute-start | bytes 663560 | tf_op jit(solution)/shard_map/ppermute | solution.py:23
  25.7 23.1 %collective-permute-start.5 = (bf16[192,1152]{1,0:T(8,128)(2,1)}, bf16[192,1152]{1,0:T(8,128)(2,1)S(1)}, u32[]{:S(2)}, u32[]{:S(2)}) collective-permute-start(bf16[192,1152]{1,0:T(8,128)(2,1)} %fusion.15), channel_id=1, source_target_pairs={{0,4},{2,6},{4,0},{6,2},{1,5},{3,7},{5,1},{7,3},{8,12},{10,14},{12... | collective-permute-start | bytes 1327112 | tf_op jit(solution)/shard_map/ppermute | solution.py:18
  30.3 20.5 %collective-permute-start.4 = (bf16[192,1152]{1,0:T(8,128)(2,1)S(1)}, bf16[192,1152]{1,0:T(8,128)(2,1)S(1)}, u32[]{:S(2)}, u32[]{:S(2)}) collective-permute-start(bf16[192,1152]{1,0:T(8,128)(2,1)S(1)} %pad_maximum_fusion.2), channel_id=1, source_target_pairs={{0,2},{2,0},{4,6},{6,4},{1,3},{3,1},{5,7},{7,5},{8,10},{10,8},{12,... | collective-permute-start | bytes 1327112 | tf_op jit(solution)/shard_map/ppermute | solution.py:18
  48.8 5.7 %collective-permute-start.7 = (bf16[192,1152]{1,0:T(8,128)(2,1)S(1)}, bf16[192,1152]{1,0:T(8,128)(2,1)S(1)}, u32[]{:S(2)}, u32[]{:S(2)}) collective-permute-start(bf16[192,1152]{1,0:T(8,128)(2,1)S(1)} %collective-permute-done.5), channel_id=1, source_target_pairs={{0,1},{1,0},{2,3},{3,2},{4,5},{5,4},{6,7},{7,6},{8,9},{9,8},{10,11... | collective-permute-start | bytes 1327112 | tf_op jit(solution)/shard_map/ppermute | solution.py:18
  62.3 9.9 %collective-permute-start.8 = (bf16[640,1152]{1,0:T(8,128)(2,1)}, bf16[640,1152]{1,0:T(8,128)(2,1)}, u32[]{:S(2)}, u32[]{:S(2)}) collective-permute-start(bf16[640,1152]{1,0:T(8,128)(2,1)} %convolution_convert_fusion.1), channel_id=1, source_target_pairs={{0,1},{1,0},{2,3},{3,2},{4,5},{5,4},{6,7},{7,6},{8,9},{9,8},{10,11... | collective-permute-start | bytes 4423688 | tf_op jit(solution)/shard_map/ppermute | solution.py:18
  76.5 20.1 %collective-permute-start.9 = (bf16[384,1152]{1,0:T(8,128)(2,1)}, bf16[384,1152]{1,0:T(8,128)(2,1)}, u32[]{:S(2)}, u32[]{:S(2)}) collective-permute-start(bf16[384,1152]{1,0:T(8,128)(2,1)} %fusion.2), channel_id=1, source_target_pairs={{0,1},{1,0},{2,3},{3,2},{4,5},{5,4},{6,7},{7,6},{8,9},{9,8},{10,11... | collective-permute-start | bytes 2654216 | tf_op jit(solution)/shard_map/ppermute | solution.py:18
  79.5 33.5 %copy-start.7 = (bf16[1,160,1152]{2,1,0:T(8,128)(2,1)}, bf16[1,160,1152]{2,1,0:T(8,128)(2,1)S(1)}, u32[]{:S(2)}) copy-start(bf16[1,160,1152]{2,1,0:T(8,128)(2,1)S(1)} %constant_dynamic-slice_fusion.1) | copy-start | bytes 1105924
  79.6 28.4 %collective-permute-start.13 = (bf16[192,1152]{1,0:T(8,128)(2,1)}, bf16[192,1152]{1,0:T(8,128)(2,1)S(1)}, u32[]{:S(2)}, u32[]{:S(2)}) collective-permute-start(bf16[192,1152]{1,0:T(8,128)(2,1)} %slice.68), channel_id=1, source_target_pairs={{0,2},{2,0},{4,6},{6,4},{1,3},{3,1},{5,7},{7,5},{8,10},{10,8},{12,... | collective-permute-start | bytes 1327112 | tf_op jit(solution)/shard_map/ppermute | solution.py:18
  82.1 20.3 %collective-permute-start.10 = (bf16[160,1152]{1,0:T(8,128)(2,1)}, bf16[160,1152]{1,0:T(8,128)(2,1)S(1)}, u32[]{:S(2)}, u32[]{:S(2)}) collective-permute-start(bf16[160,1152]{1,0:T(8,128)(2,1)} %get-tuple-element.28), channel_id=1, source_target_pairs={{0,16},{8,24},{16,0},{24,8},{1,17},{9,25},{17,1},{25,9},{2,18},{10... | collective-permute-start | bytes 1105928 | tf_op jit(solution)/shard_map/ppermute | solution.py:23
  85.6 22.3 %collective-permute-start.11 = (bf16[160,1152]{1,0:T(8,128)(2,1)}, bf16[160,1152]{1,0:T(8,128)(2,1)S(1)}, u32[]{:S(2)}, u32[]{:S(2)}) collective-permute-start(bf16[160,1152]{1,0:T(8,128)(2,1)} %get-tuple-element.29), channel_id=1, source_target_pairs={{0,8},{8,16},{16,24},{24,0},{1,9},{9,17},{17,25},{25,1},{2,10},{10... | collective-permute-start | bytes 1105928 | tf_op jit(solution)/shard_map/ppermute | solution.py:23
  92.0 16.0 %collective-permute-start.12 = (bf16[160,1152]{1,0:T(8,128)(2,1)}, bf16[160,1152]{1,0:T(8,128)(2,1)S(1)}, u32[]{:S(2)}, u32[]{:S(2)}) collective-permute-start(bf16[160,1152]{1,0:T(8,128)(2,1)} %get-tuple-element.30), channel_id=1, source_target_pairs={{0,24},{8,0},{16,8},{24,16},{1,25},{9,1},{17,9},{25,17},{2,26},{10... | collective-permute-start | bytes 1105928 | tf_op jit(solution)/shard_map/ppermute | solution.py:23
  98.1 14.9 %collective-permute-start.14 = (bf16[96,1152]{1,0:T(8,128)(2,1)S(1)}, bf16[96,1152]{1,0:T(8,128)(2,1)}, u32[]{:S(2)}, u32[]{:S(2)}) collective-permute-start(bf16[96,1152]{1,0:T(8,128)(2,1)S(1)} %slice.73), channel_id=1, source_target_pairs={{0,4},{2,6},{4,0},{6,2},{1,5},{3,7},{5,1},{7,3},{8,12},{10,14},{12... | collective-permute-start | bytes 663560 | tf_op jit(solution)/shard_map/ppermute | solution.py:18
  113.9 10.7 %collective-permute-start.15 = (bf16[40,1152]{1,0:T(8,128)(2,1)}, bf16[40,1152]{1,0:T(8,128)(2,1)}, u32[]{:S(2)}, u32[]{:S(2)}) collective-permute-start(bf16[40,1152]{1,0:T(8,128)(2,1)} %get-tuple-element.43), channel_id=1, source_target_pairs={{0,4},{2,6},{4,0},{6,2},{1,5},{3,7},{5,1},{7,3},{8,12},{10,14},{12... | collective-permute-start | bytes 276488 | tf_op jit(solution)/shard_map/ppermute | solution.py:18
  115.9 8.8 %collective-permute-start.16 = (bf16[40,1152]{1,0:T(8,128)(2,1)}, bf16[40,1152]{1,0:T(8,128)(2,1)}, u32[]{:S(2)}, u32[]{:S(2)}) collective-permute-start(bf16[40,1152]{1,0:T(8,128)(2,1)} %get-tuple-element.45), channel_id=1, source_target_pairs={{0,6},{2,4},{4,2},{6,0},{1,7},{3,5},{5,3},{7,1},{8,14},{10,12},{12... | collective-permute-start | bytes 276488 | tf_op jit(solution)/shard_map/ppermute | solution.py:18
  119.2 7.3 %collective-permute-start.17 = (bf16[40,1152]{1,0:T(8,128)(2,1)}, bf16[40,1152]{1,0:T(8,128)(2,1)}, u32[]{:S(2)}, u32[]{:S(2)}) collective-permute-start(bf16[40,1152]{1,0:T(8,128)(2,1)} %get-tuple-element.44), channel_id=1, source_target_pairs={{0,2},{2,0},{4,6},{6,4},{1,3},{3,1},{5,7},{7,5},{8,10},{10,8},{12,... | collective-permute-start | bytes 276488 | tf_op jit(solution)/shard_map/ppermute | solution.py:18
  128.4 12.6 %collective-permute-start.18 = (bf16[40,1152]{1,0:T(8,128)(2,1)}, bf16[40,1152]{1,0:T(8,128)(2,1)}, u32[]{:S(2)}, u32[]{:S(2)}) collective-permute-start(bf16[40,1152]{1,0:T(8,128)(2,1)} %fusion.34), channel_id=1, source_target_pairs={{0,32},{32,0},{1,33},{33,1},{2,34},{34,2},{3,35},{35,3},{4,36},{36... | collective-permute-start | bytes 276488 | tf_op jit(solution)/shard_map/ppermute | solution.py:18
  137.1 13.6 %collective-permute-start.19 = (bf16[96,1152]{1,0:T(8,128)(2,1)S(1)}, bf16[96,1152]{1,0:T(8,128)(2,1)S(1)}, u32[]{:S(2)}, u32[]{:S(2)}) collective-permute-start(bf16[96,1152]{1,0:T(8,128)(2,1)S(1)} %slice.61), channel_id=1, source_target_pairs={{0,4},{2,6},{4,0},{6,2},{1,5},{3,7},{5,1},{7,3},{8,12},{10,14},{12... | collective-permute-start | bytes 663560 | tf_op jit(solution)/shard_map/ppermute | solution.py:18
  142.0 38.9 %copy-start.2 = (f32[384,1152]{1,0:T(8,128)S(1)}, f32[384,1152]{1,0:T(8,128)}, u32[]{:S(2)}) copy-start(f32[384,1152]{1,0:T(8,128)} %copy-done.1) | copy-start | bytes 5308420
  142.0 38.9 %copy-start.3 = (bf16[192,1152]{1,0:T(8,128)(2,1)S(1)}, bf16[192,1152]{1,0:T(8,128)(2,1)}, u32[]{:S(2)}) copy-start(bf16[192,1152]{1,0:T(8,128)(2,1)} %param.7) | copy-start | bytes 1327108
  150.6 12.9 %collective-permute-start.20 = (bf16[40,1152]{1,0:T(8,128)(2,1)S(1)}, bf16[40,1152]{1,0:T(8,128)(2,1)S(1)}, u32[]{:S(2)}, u32[]{:S(2)}) collective-permute-start(bf16[40,1152]{1,0:T(8,128)(2,1)S(1)} %reduce-precision_convert_fusion.9), channel_id=1, source_target_pairs={{0,64},{64,0},{128,192},{192,128},{256,320},{320,256},{384,448},{4... | collective-permute-start | bytes 276488 | tf_op jit(solution)/shard_map/ppermute | solution.py:18
  155.2 8.3 %collective-permute-start.21 = (bf16[40,1152]{1,0:T(8,128)(2,1)S(1)}, bf16[40,1152]{1,0:T(8,128)(2,1)S(1)}, u32[]{:S(2)}, u32[]{:S(2)}) collective-permute-start(bf16[40,1152]{1,0:T(8,128)(2,1)S(1)} %reduce-precision_convert_fusion.9), channel_id=1, source_target_pairs={{0,128},{64,192},{128,0},{192,64},{256,384},{320,448},{384,256},{4... | collective-permute-start | bytes 276488 | tf_op jit(solution)/shard_map/ppermute | solution.py:18
  157.2 9.9 %collective-permute-start.22 = (bf16[40,1152]{1,0:T(8,128)(2,1)S(1)}, bf16[40,1152]{1,0:T(8,128)(2,1)S(1)}, u32[]{:S(2)}, u32[]{:S(2)}) collective-permute-start(bf16[40,1152]{1,0:T(8,128)(2,1)S(1)} %reduce-precision_convert_fusion.9), channel_id=1, source_target_pairs={{0,192},{64,128},{128,64},{192,0},{256,448},{320,384},{384,320},{4... | collective-permute-start | bytes 276488 | tf_op jit(solution)/shard_map/ppermute | solution.py:18
  167.1 17.5 %collective-permute-start.23 = (bf16[40,1152]{1,0:T(8,128)(2,1)S(1)}, bf16[40,1152]{1,0:T(8,128)(2,1)S(1)}, u32[]{:S(2)}, u32[]{:S(2)}) collective-permute-start(bf16[40,1152]{1,0:T(8,128)(2,1)S(1)} %reduce-precision_convert_fusion.8), channel_id=1, source_target_pairs={{0,512},{64,576},{128,640},{192,704},{256,0},{320,64},{384,128},{4... | collective-permute-start | bytes 276488 | tf_op jit(solution)/shard_map/ppermute | solution.py:23
  179.0 14.3 %collective-permute-start.24 = (bf16[40,1152]{1,0:T(8,128)(2,1)S(1)}, bf16[40,1152]{1,0:T(8,128)(2,1)S(1)}, u32[]{:S(2)}, u32[]{:S(2)}) collective-permute-start(bf16[40,1152]{1,0:T(8,128)(2,1)S(1)} %reduce-precision_convert_fusion.8), channel_id=1, source_target_pairs={{0,256},{64,320},{128,384},{192,448},{256,512},{320,576},{384,640}... | collective-permute-start | bytes 276488 | tf_op jit(solution)/shard_map/ppermute | solution.py:23
  193.4 12.5 %collective-permute-start.25 = (bf16[40,1152]{1,0:T(8,128)(2,1)S(1)}, bf16[40,1152]{1,0:T(8,128)(2,1)S(1)}, u32[]{:S(2)}, u32[]{:S(2)}) collective-permute-start(bf16[40,1152]{1,0:T(8,128)(2,1)S(1)} %reduce-precision_convert_fusion.7), channel_id=1, source_target_pairs={{0,16},{8,24},{16,0},{24,8},{1,17},{9,25},{17,1},{25,9},{2,18},{10... | collective-permute-start | bytes 276488 | tf_op jit(solution)/shard_map/ppermute | solution.py:23
  197.3 8.5 %collective-permute-start.26 = (bf16[40,1152]{1,0:T(8,128)(2,1)S(1)}, bf16[40,1152]{1,0:T(8,128)(2,1)S(1)}, u32[]{:S(2)}, u32[]{:S(2)}) collective-permute-start(bf16[40,1152]{1,0:T(8,128)(2,1)S(1)} %reduce-precision_convert_fusion.7), channel_id=1, source_target_pairs={{0,8},{8,16},{16,24},{24,0},{1,9},{9,17},{17,25},{25,1},{2,10},{10... | collective-permute-start | bytes 276488 | tf_op jit(solution)/shard_map/ppermute | solution.py:23
  201.6 7.7 %collective-permute-start.27 = (bf16[40,1152]{1,0:T(8,128)(2,1)S(1)}, bf16[40,1152]{1,0:T(8,128)(2,1)S(1)}, u32[]{:S(2)}, u32[]{:S(2)}) collective-permute-start(bf16[40,1152]{1,0:T(8,128)(2,1)S(1)} %reduce-precision_convert_fusion.7), channel_id=1, source_target_pairs={{0,24},{8,0},{16,8},{24,16},{1,25},{9,1},{17,9},{25,17},{2,26},{10... | collective-permute-start | bytes 276488 | tf_op jit(solution)/shard_map/ppermute | solution.py:23
  (13 other events, 153.7 us)

commit v4 on v3

--- a/solution.py
+++ b/solution.py
@@ -62,14 +62,14 @@
     rows = pictures.shape[0]
     z, x, y, k = (lax.axis_index(a) for a in ("z", "x", "y", "k"))
 
-    paired, crossed = shifted(captions, x)
+    paired, moved_half = shifted(captions, x)
     picture = pictures.astype(f32)
     image_scale = lax.rsqrt(jnp.sum(picture * picture, -1, keepdims=True) + eps)
     image_unit = picture * image_scale
     image_low = image_unit.astype(bf16)
-    image_core = swap(image_low, "k", 1)
-    image_out, _ = tie(image_low, crossed)
+    image_out, _ = tie(image_low, moved_half)
     image_far = swap(image_out, "y", 2)
+    image_core = swap(image_out, "k", 1)
     images = jnp.concatenate([image_low, image_far, image_core, swap(image_far, "k", 1)])
     texts = jnp.concatenate([paired, swap(paired, "y", 1)])
 
@@ -77,7 +77,7 @@
     text_scale = lax.rsqrt(jnp.sum(projected * projected, -1, keepdims=True) + eps)
     text_unit = projected * text_scale
     text_low = text_unit.astype(bf16)
-    (texts_sent,) = tie(head_rows(texts, 1 - k))
+    texts_sent, texts_kept = tie(head_rows(texts, 1 - k), head_rows(texts, k))
 
     scores = sharp * dot(images, text_low, 1, 1) + moved
     wanted = jnp.concatenate([slot[0], jnp.full((3 * rows,), -1, jnp.int32)])
@@ -91,41 +91,40 @@
     grad_low = low(grad)
 
     sent = dot(texts_sent, grad_low, 0, 0).astype(bf16)
-    sent, texts = tie(sent, texts)
     arrived = swap(sent, "k", 1)
-    kept = dot(head_rows(texts, k), grad_low, 0, 0).astype(bf16)
+    kept = dot(texts_kept, grad_low, 0, 0).astype(bf16)
     parts = [p.reshape(4, 4 * PAD, D) for p in (kept, arrived)]
 
-    pieces = [low(pick(parts, (x + d) % 4)) for d in (2, 1, 3)]
-    *pieces, weight, grad_sent = tie(*pieces, weight, grad_low[rows:])
-    over_x = [turn(piece, "x", d) for piece, d in zip(pieces, (2, 1, 3))]
+    over_x = [turn(low(pick(parts, (x + d) % 4)), "x", d) for d in (2, 1, 3)]
+    grad_far = swap(grad_low[rows:], "y", 1)
     image_sent = (sharp * dot(weight[2 * rows :], text_low, 1, 0)).astype(bf16)
+    image_kept = sharp * dot(weight[: 2 * rows], text_low, 1, 0)
+    *over_x, image_sent, grad_far = tie(*over_x, image_sent, grad_far)
     image_core = swap(image_sent, "k", 1)
-    grad_far = swap(grad_sent, "y", 1)
-    image_kept = sharp * dot(weight[: 2 * rows], text_low, 1, 0)
-    image_sent = low(image_kept[rows:] + image_core[rows:].astype(f32))
-    far_one = swap(image_sent[: rows // 2], "y", 2)
-    *over_x, image_sent, grad_far, far_one = tie(*over_x, image_sent, grad_far, far_one)
-    far_two = swap(image_sent[rows // 2 :], "y", 2)
     projected_grad = grad_low[:rows].astype(f32) + grad_far.astype(f32)
     text_grad = dot(projected_grad.astype(bf16), matrix, 1, 1)
 
     parts = [lax.dynamic_index_in_dim(p, x, 0, keepdims=False) for p in parts] + over_x
     parts = [p.reshape(4, PAD, D) for p in parts]
     over_y = {m: swap(low(pick(parts, y ^ m)), "y", m) for m in (2, 3, 1)}
+    *over_y, image_core = tie(*over_y.values(), image_core)
     total = pick(parts, y)
-    for other in over_y.values():
+    for other in over_y:
         total = total + other.astype(f32)
     head = low(total)
     head = low(head.astype(f32) + swap(head, "h", 1).astype(f32))
 
-    head, far_two = tie(head, far_two)
-    own = image_kept[:rows] + image_core[:rows].astype(f32)
-    own = own + jnp.concatenate([far_one, far_two]).astype(f32)
-
-    over_z = {m: swap(head, "z", m).astype(f32) for m in (2, 3, 1)}
-    head = low((head.astype(f32) + over_z[1]) + (over_z[2] + over_z[3]))
-    ring = [head, turn(head, "z", 8), turn(head, "z", 4)]
+    image_out = (image_kept[rows:] + image_core[rows:].astype(f32)).astype(bf16)
+    head, image_out = tie(head, image_out)
+    third = rows // 3
+    far = [swap(image_out[i * third : (i + 1) * third], "y", 2) for i in range(3)]
+    over_z = [swap(head, "z", m) for m in (2, 3, 1)]
+    *over_z, far[0] = tie(*over_z, far[0])
+    over_z = [other.astype(f32) for other in over_z]
+    head = low((head.astype(f32) + over_z[2]) + (over_z[0] + over_z[1]))
+    over_z = [turn(head, "z", 8), turn(head, "z", 4)]
+    *over_z, far[1] = tie(*over_z, far[1])
+    ring = [head] + over_z
     u = z // 4
     total = 0.0
     for j in range(3):
@@ -141,6 +140,7 @@
     head_grad = jnp.concatenate([one[:PART] for one in ordered]).astype(f32)
     bias_grad = lax.dynamic_slice(ordered[0][PART].astype(f32), ((2 * y + k) * 144,), (144,))
 
+    own = image_kept[:rows] + image_core[:rows].astype(f32) + jnp.concatenate(far).astype(f32)
     along = jnp.sum(image_unit * own, -1, keepdims=True)
     image_grad = (own - image_unit * along) * image_scale
     return (image_grad, text_grad, head_grad, bias_grad)
@@ -159,7 +159,7 @@
     moved = turn(low_half, "x", 1)
     first = jnp.where(x == 0, cross(moved, 0), moved)
     second = turn(jnp.where(x == 3, crossed, high_half), "x", 1)
-    return jnp.concatenate([first, second]), crossed
+    return jnp.concatenate([first, second]), moved
 
 
 def solution(mesh):

time: 212 us -> 199 us (0.939)
  the two profiles are of different devices: /device:TPU:134 before, /device:TPU:56 now
where the time goes in v4:
time: 199 us; the launch traced here: 197 us
  starting transfers between devices  104 us (52%)
  waiting for transfers between devices  48.9 us (25%)
  matrix products  18.2 us (9%)
  other arithmetic  17.1 us (9%)
  local copies, waits for them, and re-layouts  6.05 us (3%)
  between operations  2.81 us (1%)
    ppermute x17, starting transfers between devices, swap(): return lax.ppermute(block, axis, [(i, i ^ mask) for i in range(n)])  61 us
    ppermute x10, starting transfers between devices, turn(): lax.ppermute(block, axis, [(i, (i + distance) % n) for i in range(n)])  37 us
    ppermute x10, waiting for transfers between devices, turn(): lax.ppermute(block, axis, [(i, (i + distance) % n) for i in range(n)])  26.8 us
    ppermute x17, waiting for transfers between devices, swap(): return lax.ppermute(block, axis, [(i, i ^ mask) for i in range(n)])  20 us
    dot_general x10, matrix products, dot(): lax.dot_general(a, b, (((ca,), (cb,)), ((), ())), preferred_element_type=...  18.2 us
    convert_element_type x7, other arithmetic, low(): return lax.reduce_precision(values, 8, 7).astype(bf16)  7.29 us
    ppermute x2, starting transfers between devices, cross(): return lax.ppermute(half, COL, pairs)  6.38 us
  transfers between devices with their start and end apart: 29, of which 11 were waited for; matrix products, arithmetic and copies ran while one was open for 14% of the time, Pallas kernels for 0%

profile of v4, /device:TPU:56, one launch (start us, length us, event | category | flops | bytes accessed | tf_op | source)
XLA Modules:
  0.0 197.4 jit_solution(321018493568934325)
XLA Ops:
  3.3 3.4 %collective-permute-start = (bf16[96,1152]{1,0:T(8,128)(2,1)S(1)}, bf16[96,1152]{1,0:T(8,128)(2,1)}, u32[]{:S(2)}, u32[]{:S(2)}) collective-permute-start(bf16[96,1152]{1,0:T(8,128)(2,1)S(1)} %get-tuple-element.27), channel_id=1, source_target_pairs={{0,8},{8,16},{16,24},{24,0},{1,9},{9,17},{17,25},{25,1},{2,10},{10... | collective-permute-start | bytes 663560 | tf_op jit(solution)/shard_map/ppermute | solution.py:23
  10.5 7.8 %collective-permute-done = bf16[96,1152]{1,0:T(8,128)(2,1)} collective-permute-done((bf16[96,1152]{1,0:T(8,128)(2,1)S(1)}, bf16[96,1152]{1,0:T(8,128)(2,1)}, u32[]{:S(2)}, u32[]{:S(2)}) %collective-permute-start) | collective-permute-done | bytes 221216 | tf_op jit(solution)/shard_map/ppermute | solution.py:23
  18.3 5.0 %collective-permute-start.4 = (bf16[96,1152]{1,0:T(8,128)(2,1)}, bf16[96,1152]{1,0:T(8,128)(2,1)S(1)}, u32[]{:S(2)}, u32[]{:S(2)}) collective-permute-start(bf16[96,1152]{1,0:T(8,128)(2,1)} %collective-permute-done), channel_id=1, source_target_pairs={{0,32},{32,64},{64,96},{96,128},{128,160},{160,192},{192,224},{224... | collective-permute-start | bytes 663560 | tf_op jit(solution)/shard_map/ppermute | solution.py:154
  25.4 4.0 %collective-permute-start.1 = (bf16[192,1152]{1,0:T(8,128)(2,1)}, bf16[192,1152]{1,0:T(8,128)(2,1)S(1)}, u32[]{:S(2)}, u32[]{:S(2)}) collective-permute-start(bf16[192,1152]{1,0:T(8,128)(2,1)} %fusion.15), channel_id=1, source_target_pairs={{0,4},{2,6},{4,0},{6,2},{1,5},{3,7},{5,1},{7,3},{8,12},{10,14},{12... | collective-permute-start | bytes 1327112 | tf_op jit(solution)/shard_map/ppermute | solution.py:18
  29.4 2.1 %collective-permute-done.4 = bf16[96,1152]{1,0:T(8,128)(2,1)S(1)} collective-permute-done((bf16[96,1152]{1,0:T(8,128)(2,1)}, bf16[96,1152]{1,0:T(8,128)(2,1)S(1)}, u32[]{:S(2)}, u32[]{:S(2)}) %collective-permute-start.4) | collective-permute-done | bytes 221216 | tf_op jit(solution)/shard_map/ppermute | solution.py:154
  32.6 8.7 %collective-permute-start.7 = (bf16[192,1152]{1,0:T(8,128)(2,1)S(1)}, bf16[192,1152]{1,0:T(8,128)(2,1)S(1)}, u32[]{:S(2)}, u32[]{:S(2)}) collective-permute-start(bf16[192,1152]{1,0:T(8,128)(2,1)S(1)} %pad_maximum_fusion.2), channel_id=1, source_target_pairs={{0,2},{2,0},{4,6},{6,4},{1,3},{3,1},{5,7},{7,5},{8,10},{10,8},{12,... | collective-permute-start | bytes 1327112 | tf_op jit(solution)/shard_map/ppermute | solution.py:18
  45.1 13.0 %collective-permute-done.1 = bf16[192,1152]{1,0:T(8,128)(2,1)S(1)} collective-permute-done((bf16[192,1152]{1,0:T(8,128)(2,1)}, bf16[192,1152]{1,0:T(8,128)(2,1)S(1)}, u32[]{:S(2)}, u32[]{:S(2)}) %collective-permute-start.1) | collective-permute-done | bytes 442400 | tf_op jit(solution)/shard_map/ppermute | solution.py:18
  64.5 3.1 %fusion.12 = bf16[768,384]{1,0:T(8,128)(2,1)S(1)} fusion(bf16[384,1152]{1,0:T(8,128)(2,1)S(1)} %multiply_convert_fusion, f32[]{:T(128)} %bitcast.50, f32[]{:T(128)} %bitcast.47, s32[768]{0:T(1024)S(1)} %concatenate.19, bf16[192,1152]{1,0:T(8,128)(2,1)S(1)} %collective-permute-done.3, bf16[192,1152]{1,0:T(8,128)(2,1)S(1)} %collective-permute-done.2, ...), kind=kOutput, calls=%fused_computation.28 | convolution fusion | flops 689799168 | bytes 3247112 | tf_op jit(solution)/shard_map/dot_general | solution.py:31
  69.1 2.2 %convolution_convert_fusion = bf16[640,1152]{1,0:T(8,128)(2,1)} fusion(bf16[384,640]{1,0:T(8,128)(2,1)S(1)} %fusion.8, bf16[384,1152]{1,0:T(8,128)(2,1)S(1)} %reduce-precision_convert_fusion), kind=kOutput, calls=%fused_computation | convolution fusion | flops 566968320 | bytes 2850816 | tf_op jit(solution)/shard_map/dot_general | solution.py:31
  71.3 2.4 %collective-permute-start.8 = (bf16[640,1152]{1,0:T(8,128)(2,1)}, bf16[640,1152]{1,0:T(8,128)(2,1)}, u32[]{:S(2)}, u32[]{:S(2)}) collective-permute-start(bf16[640,1152]{1,0:T(8,128)(2,1)} %convolution_convert_fusion), channel_id=1, source_target_pairs={{0,1},{1,0},{2,3},{3,2},{4,5},{5,4},{6,7},{7,6},{8,9},{9,8},{10,11... | collective-permute-start | bytes 4423688 | tf_op jit(solution)/shard_map/ppermute | solution.py:18
  76.5 2.1 %convolution_convert_fusion.1 = bf16[640,1152]{1,0:T(8,128)(2,1)S(1)} fusion(bf16[384,640]{1,0:T(8,128)(2,1)} %fusion.9, bf16[384,1152]{1,0:T(8,128)(2,1)S(1)} %reduce-precision_convert_fusion), kind=kOutput, calls=%fused_computation.1 | convolution fusion | flops 566968320 | bytes 2850816 | tf_op jit(solution)/shard_map/dot_general | solution.py:31
  79.6 2.4 %fusion.26 = (bf16[160,1152]{1,0:T(8,128)(2,1)}, bf16[160,1152]{1,0:T(8,128)(2,1)}, bf16[160,1152]{1,0:T(8,128)(2,1)}) fusion(bf16[4,160,1152]{2,1,0:T(8,128)(2,1)} %bitcast.5, s32[]{:T(128)S(6)} %select_n.332, bf16[4,160,1152]{2,1,0:T(8,128)(2,1)S(1)} %bitcast.51, s32[]{:T(128)S(6)} %select_n.330, s32[]{:T(128)S(6)} %select_n.328), kind=kLoop, calls=%fused_computation.53 | loop fusion | flops 2764800 | bytes 3317772 | tf_op jit(solution)/shard_map/convert_element_type | solution.py:27
  85.8 5.1 %collective-permute-start.11 = (bf16[160,1152]{1,0:T(8,128)(2,1)}, bf16[160,1152]{1,0:T(8,128)(2,1)}, u32[]{:S(2)}, u32[]{:S(2)}) collective-permute-start(bf16[160,1152]{1,0:T(8,128)(2,1)} %get-tuple-element.50), channel_id=1, source_target_pairs={{0,24},{8,0},{16,8},{24,16},{1,25},{9,1},{17,9},{25,17},{2,26},{10... | collective-permute-start | bytes 1105928 | tf_op jit(solution)/shard_map/ppermute | solution.py:23
  93.0 4.2 %collective-permute-done.9 = bf16[160,1152]{1,0:T(8,128)(2,1)} collective-permute-done((bf16[160,1152]{1,0:T(8,128)(2,1)}, bf16[160,1152]{1,0:T(8,128)(2,1)}, u32[]{:S(2)}, u32[]{:S(2)}) %collective-permute-start.9) | collective-permute-done | bytes 368672 | tf_op jit(solution)/shard_map/ppermute | solution.py:23
  97.2 6.9 %collective-permute-done.10 = bf16[160,1152]{1,0:T(8,128)(2,1)} collective-permute-done((bf16[160,1152]{1,0:T(8,128)(2,1)}, bf16[160,1152]{1,0:T(8,128)(2,1)}, u32[]{:S(2)}, u32[]{:S(2)}) %collective-permute-start.10) | collective-permute-done | bytes 368672 | tf_op jit(solution)/shard_map/ppermute | solution.py:23
  109.5 4.1 %collective-permute-start.13 = (bf16[40,1152]{1,0:T(8,128)(2,1)S(1)}, bf16[40,1152]{1,0:T(8,128)(2,1)S(1)}, u32[]{:S(2)}, u32[]{:S(2)}) collective-permute-start(bf16[40,1152]{1,0:T(8,128)(2,1)S(1)} %get-tuple-element.55), channel_id=1, source_target_pairs={{0,4},{2,6},{4,0},{6,2},{1,5},{3,7},{5,1},{7,3},{8,12},{10,14},{12... | collective-permute-start | bytes 276488 | tf_op jit(solution)/shard_map/ppermute | solution.py:18
  113.6 3.8 %collective-permute-start.14 = (bf16[40,1152]{1,0:T(8,128)(2,1)S(1)}, bf16[40,1152]{1,0:T(8,128)(2,1)S(1)}, u32[]{:S(2)}, u32[]{:S(2)}) collective-permute-start(bf16[40,1152]{1,0:T(8,128)(2,1)S(1)} %get-tuple-element.54), channel_id=1, source_target_pairs={{0,6},{2,4},{4,2},{6,0},{1,7},{3,5},{5,3},{7,1},{8,14},{10,12},{12... | collective-permute-start | bytes 276488 | tf_op jit(solution)/shard_map/ppermute | solution.py:18
  117.4 2.1 %collective-permute-start.15 = (bf16[40,1152]{1,0:T(8,128)(2,1)S(1)}, bf16[40,1152]{1,0:T(8,128)(2,1)S(1)}, u32[]{:S(2)}, u32[]{:S(2)}) collective-permute-start(bf16[40,1152]{1,0:T(8,128)(2,1)S(1)} %get-tuple-element.53), channel_id=1, source_target_pairs={{0,2},{2,0},{4,6},{6,4},{1,3},{3,1},{5,7},{7,5},{8,10},{10,8},{12,... | collective-permute-start | bytes 276488 | tf_op jit(solution)/shard_map/ppermute | solution.py:18
  120.2 2.0 %collective-permute-done.14 = bf16[40,1152]{1,0:T(8,128)(2,1)S(1)} collective-permute-done((bf16[40,1152]{1,0:T(8,128)(2,1)S(1)}, bf16[40,1152]{1,0:T(8,128)(2,1)S(1)}, u32[]{:S(2)}, u32[]{:S(2)}) %collective-permute-start.14) | collective-permute-done | bytes 92192 | tf_op jit(solution)/shard_map/ppermute | solution.py:18
  125.5 7.2 %collective-permute-start.17 = (bf16[40,1152]{1,0:T(8,128)(2,1)S(1)}, bf16[40,1152]{1,0:T(8,128)(2,1)S(1)}, u32[]{:S(2)}, u32[]{:S(2)}) collective-permute-start(bf16[40,1152]{1,0:T(8,128)(2,1)S(1)} %fusion.32), channel_id=1, source_target_pairs={{0,32},{32,0},{1,33},{33,1},{2,34},{34,2},{3,35},{35,3},{4,36},{36... | collective-permute-start | bytes 276488 | tf_op jit(solution)/shard_map/ppermute | solution.py:18
  132.8 3.1 %collective-permute-done.17 = bf16[40,1152]{1,0:T(8,128)(2,1)S(1)} collective-permute-done((bf16[40,1152]{1,0:T(8,128)(2,1)S(1)}, bf16[40,1152]{1,0:T(8,128)(2,1)S(1)}, u32[]{:S(2)}, u32[]{:S(2)}) %collective-permute-start.17) | collective-permute-done | bytes 92192 | tf_op jit(solution)/shard_map/ppermute | solution.py:18
  137.3 4.5 %collective-permute-start.21 = (bf16[64,1152]{1,0:T(8,128)(2,1)}, bf16[64,1152]{1,0:T(8,128)(2,1)}, u32[]{:S(2)}, u32[]{:S(2)}) collective-permute-start(bf16[64,1152]{1,0:T(8,128)(2,1)} %get-tuple-element.58), channel_id=1, source_target_pairs={{0,4},{2,6},{4,0},{6,2},{1,5},{3,7},{5,1},{7,3},{8,12},{10,14},{12... | collective-permute-start | bytes 442376 | tf_op jit(solution)/shard_map/ppermute | solution.py:18
  141.8 3.0 %collective-permute-start.18 = (bf16[40,1152]{1,0:T(8,128)(2,1)}, bf16[40,1152]{1,0:T(8,128)(2,1)}, u32[]{:S(2)}, u32[]{:S(2)}) collective-permute-start(bf16[40,1152]{1,0:T(8,128)(2,1)} %reduce-precision_convert_fusion.9), channel_id=1, source_target_pairs={{0,128},{64,192},{128,0},{192,64},{256,384},{320,448},{384,256},{4... | collective-permute-start | bytes 276488 | tf_op jit(solution)/shard_map/ppermute | solution.py:18
  144.9 2.7 %collective-permute-start.19 = (bf16[40,1152]{1,0:T(8,128)(2,1)}, bf16[40,1152]{1,0:T(8,128)(2,1)}, u32[]{:S(2)}, u32[]{:S(2)}) collective-permute-start(bf16[40,1152]{1,0:T(8,128)(2,1)} %reduce-precision_convert_fusion.9), channel_id=1, source_target_pairs={{0,192},{64,128},{128,64},{192,0},{256,448},{320,384},{384,320},{4... | collective-permute-start | bytes 276488 | tf_op jit(solution)/shard_map/ppermute | solution.py:18
  147.6 3.4 %collective-permute-start.20 = (bf16[40,1152]{1,0:T(8,128)(2,1)}, bf16[40,1152]{1,0:T(8,128)(2,1)}, u32[]{:S(2)}, u32[]{:S(2)}) collective-permute-start(bf16[40,1152]{1,0:T(8,128)(2,1)} %reduce-precision_convert_fusion.9), channel_id=1, source_target_pairs={{0,64},{64,0},{128,192},{192,128},{256,320},{320,256},{384,448},{4... | collective-permute-start | bytes 276488 | tf_op jit(solution)/shard_map/ppermute | solution.py:18
  151.2 3.6 %collective-permute-start.24 = (bf16[64,1152]{1,0:T(8,128)(2,1)}, bf16[64,1152]{1,0:T(8,128)(2,1)S(1)}, u32[]{:S(2)}, u32[]{:S(2)}) collective-permute-start(bf16[64,1152]{1,0:T(8,128)(2,1)} %get-tuple-element.56), channel_id=1, source_target_pairs={{0,4},{2,6},{4,0},{6,2},{1,5},{3,7},{5,1},{7,3},{8,12},{10,14},{12... | collective-permute-start | bytes 442376 | tf_op jit(solution)/shard_map/ppermute | solution.py:18
  156.0 13.0 %collective-permute-start.22 = (bf16[40,1152]{1,0:T(8,128)(2,1)S(1)}, bf16[40,1152]{1,0:T(8,128)(2,1)S(1)}, u32[]{:S(2)}, u32[]{:S(2)}) collective-permute-start(bf16[40,1152]{1,0:T(8,128)(2,1)S(1)} %reduce-precision_convert_fusion.8), channel_id=1, source_target_pairs={{0,512},{64,576},{128,640},{192,704},{256,0},{320,64},{384,128},{4... | collective-permute-start | bytes 276488 | tf_op jit(solution)/shard_map/ppermute | solution.py:23
  171.0 3.0 %fusion.22 = f32[192,1152]{1,0:T(8,128)} fusion(bf16[1152,1152]{1,0:T(8,128)(2,1)S(1)} %copy-done, bf16[192,1152]{1,0:T(8,128)(2,1)} %collective-permute-done.12, bf16[384,1152]{1,0:T(8,128)(2,1)S(1)} %reduce-precision_convert_fusion), kind=kOutput, calls=%fused_computation.48 | convolution fusion | flops 510492672 | bytes 4423680 | tf_op jit(solution)/shard_map/dot_general | solution.py:31
  174.0 3.7 %collective-permute-start.25 = (bf16[64,1152]{1,0:T(8,128)(2,1)S(1)}, bf16[64,1152]{1,0:T(8,128)(2,1)S(1)}, u32[]{:S(2)}, u32[]{:S(2)}) collective-permute-start(bf16[64,1152]{1,0:T(8,128)(2,1)S(1)} %copy-done.14), channel_id=1, source_target_pairs={{0,4},{2,6},{4,0},{6,2},{1,5},{3,7},{5,1},{7,3},{8,12},{10,14},{12... | collective-permute-start | bytes 442376 | tf_op jit(solution)/shard_map/ppermute | solution.py:18
  177.7 5.6 %collective-permute-done.23 = bf16[40,1152]{1,0:T(8,128)(2,1)S(1)} collective-permute-done((bf16[40,1152]{1,0:T(8,128)(2,1)S(1)}, bf16[40,1152]{1,0:T(8,128)(2,1)S(1)}, u32[]{:S(2)}, u32[]{:S(2)}) %collective-permute-start.23) | collective-permute-done | bytes 92192 | tf_op jit(solution)/shard_map/ppermute | solution.py:23
  187.2 3.9 %collective-permute-start.27 = (bf16[40,1152]{1,0:T(8,128)(2,1)S(1)}, bf16[40,1152]{1,0:T(8,128)(2,1)S(1)}, u32[]{:S(2)}, u32[]{:S(2)}) collective-permute-start(bf16[40,1152]{1,0:T(8,128)(2,1)S(1)} %reduce-precision_convert_fusion.7), channel_id=1, source_target_pairs={{0,8},{8,16},{16,24},{24,0},{1,9},{9,17},{17,25},{25,1},{2,10},{10... | collective-permute-start | bytes 276488 | tf_op jit(solution)/shard_map/ppermute | solution.py:23
  192.4 2.1 %fusion.18 = f32[192,1152]{1,0:T(8,128)} fusion(bf16[192,1152]{1,0:T(8,128)(2,1)S(1)} %copy-done.4, f32[192]{0:T(256)S(1)} %fusion.16, f32[192]{0:T(256)S(1)} %add_rsqrt_fusion.1, bf16[64,1152]{1,0:T(8,128)(2,1)S(1)} %collective-permute-done.25, bf16[64,1152]{1,0:T(8,128)(2,1)S(1)} %collective-permute-done.24, bf16[64,1152]{1,0:T(8,128)(2,1)} %collective-permute-done.21, ...), kind=kLoop, calls=%fused_computation.37 | loop fusion | flops 3096576 | bytes 3098112 | tf_op jit(solution)/shard_map/mul | solution.py:145
  (104 shorter events, 51.2 us)
Async XLA Ops:
  0.6 62.0 %copy-start = (bf16[1152,1152]{1,0:T(8,128)(2,1)S(1)}, bf16[1152,1152]{1,0:T(8,128)(2,1)}, u32[]{:S(2)}) copy-start(bf16[1152,1152]{1,0:T(8,128)(2,1)} %param.10) | copy-start | bytes 7962628
  1.9 21.5 %collective-permute-start.5 = (bf16[96,1152]{1,0:T(8,128)(2,1)S(1)}, bf16[96,1152]{1,0:T(8,128)(2,1)}, u32[]{:S(2)}, u32[]{:S(2)}) collective-permute-start(bf16[96,1152]{1,0:T(8,128)(2,1)S(1)} %get-tuple-element.29), channel_id=1, source_target_pairs={{24,56},{56,88},{88,120},{120,152},{152,184},{184,216},{216,248},{... | collective-permute-start | bytes 663560 | tf_op jit(solution)/shard_map/ppermute | solution.py:154
  3.3 15.1 %collective-permute-start = (bf16[96,1152]{1,0:T(8,128)(2,1)S(1)}, bf16[96,1152]{1,0:T(8,128)(2,1)}, u32[]{:S(2)}, u32[]{:S(2)}) collective-permute-start(bf16[96,1152]{1,0:T(8,128)(2,1)S(1)} %get-tuple-element.27), channel_id=1, source_target_pairs={{0,8},{8,16},{16,24},{24,0},{1,9},{9,17},{17,25},{25,1},{2,10},{10... | collective-permute-start | bytes 663560 | tf_op jit(solution)/shard_map/ppermute | solution.py:23
  10.5 49.5 %copy-start.10 = (bf16[1152,640]{1,0:T(8,128)(2,1)S(1)}, bf16[1152,640]{1,0:T(8,128)(2,1)}, u32[]{:S(2)}) copy-start(bf16[1152,640]{1,0:T(8,128)(2,1)} %fusion) | copy-start | bytes 4423684
  18.3 13.2 %collective-permute-start.4 = (bf16[96,1152]{1,0:T(8,128)(2,1)}, bf16[96,1152]{1,0:T(8,128)(2,1)S(1)}, u32[]{:S(2)}, u32[]{:S(2)}) collective-permute-start(bf16[96,1152]{1,0:T(8,128)(2,1)} %collective-permute-done), channel_id=1, source_target_pairs={{0,32},{32,64},{64,96},{96,128},{128,160},{160,192},{192,224},{224... | collective-permute-start | bytes 663560 | tf_op jit(solution)/shard_map/ppermute | solution.py:154
  23.4 9.1 %collective-permute-start.6 = (bf16[96,1152]{1,0:T(8,128)(2,1)S(1)}, bf16[96,1152]{1,0:T(8,128)(2,1)S(1)}, u32[]{:S(2)}, u32[]{:S(2)}) collective-permute-start(bf16[96,1152]{1,0:T(8,128)(2,1)S(1)} %broadcast_select_fusion), channel_id=1, source_target_pairs={{0,8},{8,16},{16,24},{24,0},{1,9},{9,17},{17,25},{25,1},{2,10},{10... | collective-permute-start | bytes 663560 | tf_op jit(solution)/shard_map/ppermute | solution.py:23
  25.4 32.7 %collective-permute-start.1 = (bf16[192,1152]{1,0:T(8,128)(2,1)}, bf16[192,1152]{1,0:T(8,128)(2,1)S(1)}, u32[]{:S(2)}, u32[]{:S(2)}) collective-permute-start(bf16[192,1152]{1,0:T(8,128)(2,1)} %fusion.15), channel_id=1, source_target_pairs={{0,4},{2,6},{4,0},{6,2},{1,5},{3,7},{5,1},{7,3},{8,12},{10,14},{12... | collective-permute-start | bytes 1327112 | tf_op jit(solution)/shard_map/ppermute | solution.py:18
  32.6 27.4 %collective-permute-start.7 = (bf16[192,1152]{1,0:T(8,128)(2,1)S(1)}, bf16[192,1152]{1,0:T(8,128)(2,1)S(1)}, u32[]{:S(2)}, u32[]{:S(2)}) collective-permute-start(bf16[192,1152]{1,0:T(8,128)(2,1)S(1)} %pad_maximum_fusion.2), channel_id=1, source_target_pairs={{0,2},{2,0},{4,6},{6,4},{1,3},{3,1},{5,7},{7,5},{8,10},{10,8},{12,... | collective-permute-start | bytes 1327112 | tf_op jit(solution)/shard_map/ppermute | solution.py:18
  43.2 21.3 %collective-permute-start.2 = (bf16[192,1152]{1,0:T(8,128)(2,1)S(1)}, bf16[192,1152]{1,0:T(8,128)(2,1)S(1)}, u32[]{:S(2)}, u32[]{:S(2)}) collective-permute-start(bf16[192,1152]{1,0:T(8,128)(2,1)S(1)} %copy-done.11), channel_id=1, source_target_pairs={{0,1},{1,0},{2,3},{3,2},{4,5},{5,4},{6,7},{7,6},{8,9},{9,8},{10,11... | collective-permute-start | bytes 1327112 | tf_op jit(solution)/shard_map/ppermute | solution.py:18
  58.1 6.4 %collective-permute-start.3 = (bf16[192,1152]{1,0:T(8,128)(2,1)S(1)}, bf16[192,1152]{1,0:T(8,128)(2,1)S(1)}, u32[]{:S(2)}, u32[]{:S(2)}) collective-permute-start(bf16[192,1152]{1,0:T(8,128)(2,1)S(1)} %collective-permute-done.1), channel_id=1, source_target_pairs={{0,1},{1,0},{2,3},{3,2},{4,5},{5,4},{6,7},{7,6},{8,9},{9,8},{10,11... | collective-permute-start | bytes 1327112 | tf_op jit(solution)/shard_map/ppermute | solution.py:18
  71.3 7.2 %collective-permute-start.8 = (bf16[640,1152]{1,0:T(8,128)(2,1)}, bf16[640,1152]{1,0:T(8,128)(2,1)}, u32[]{:S(2)}, u32[]{:S(2)}) collective-permute-start(bf16[640,1152]{1,0:T(8,128)(2,1)} %convolution_convert_fusion), channel_id=1, source_target_pairs={{0,1},{1,0},{2,3},{3,2},{4,5},{5,4},{6,7},{7,6},{8,9},{9,8},{10,11... | collective-permute-start | bytes 4423688 | tf_op jit(solution)/shard_map/ppermute | solution.py:18
  74.5 18.4 %collective-permute-start.12 = (bf16[192,1152]{1,0:T(8,128)(2,1)}, bf16[192,1152]{1,0:T(8,128)(2,1)}, u32[]{:S(2)}, u32[]{:S(2)}) collective-permute-start(bf16[192,1152]{1,0:T(8,128)(2,1)} %slice.75), channel_id=1, source_target_pairs={{0,2},{2,0},{4,6},{6,4},{1,3},{3,1},{5,7},{7,5},{8,10},{10,8},{12,... | collective-permute-start | bytes 1327112 | tf_op jit(solution)/shard_map/ppermute | solution.py:18
  82.0 15.2 %collective-permute-start.9 = (bf16[160,1152]{1,0:T(8,128)(2,1)}, bf16[160,1152]{1,0:T(8,128)(2,1)}, u32[]{:S(2)}, u32[]{:S(2)}) collective-permute-start(bf16[160,1152]{1,0:T(8,128)(2,1)} %get-tuple-element.52), channel_id=1, source_target_pairs={{0,16},{8,24},{16,0},{24,8},{1,17},{9,25},{17,1},{25,9},{2,18},{10... | collective-permute-start | bytes 1105928 | tf_op jit(solution)/shard_map/ppermute | solution.py:23
  83.9 20.2 %collective-permute-start.10 = (bf16[160,1152]{1,0:T(8,128)(2,1)}, bf16[160,1152]{1,0:T(8,128)(2,1)}, u32[]{:S(2)}, u32[]{:S(2)}) collective-permute-start(bf16[160,1152]{1,0:T(8,128)(2,1)} %get-tuple-element.51), channel_id=1, source_target_pairs={{0,8},{8,16},{16,24},{24,0},{1,9},{9,17},{17,25},{25,1},{2,10},{10... | collective-permute-start | bytes 1105928 | tf_op jit(solution)/shard_map/ppermute | solution.py:23
  85.8 18.3 %collective-permute-start.11 = (bf16[160,1152]{1,0:T(8,128)(2,1)}, bf16[160,1152]{1,0:T(8,128)(2,1)}, u32[]{:S(2)}, u32[]{:S(2)}) collective-permute-start(bf16[160,1152]{1,0:T(8,128)(2,1)} %get-tuple-element.50), channel_id=1, source_target_pairs={{0,24},{8,0},{16,8},{24,16},{1,25},{9,1},{17,9},{25,17},{2,26},{10... | collective-permute-start | bytes 1105928 | tf_op jit(solution)/shard_map/ppermute | solution.py:23
  104.1 20.1 %collective-permute-start.16 = (bf16[384,1152]{1,0:T(8,128)(2,1)S(1)}, bf16[384,1152]{1,0:T(8,128)(2,1)S(1)}, u32[]{:S(2)}, u32[]{:S(2)}) collective-permute-start(bf16[384,1152]{1,0:T(8,128)(2,1)S(1)} %fusion.2), channel_id=1, source_target_pairs={{0,1},{1,0},{2,3},{3,2},{4,5},{5,4},{6,7},{7,6},{8,9},{9,8},{10,11... | collective-permute-start | bytes 2654216 | tf_op jit(solution)/shard_map/ppermute | solution.py:18
  109.5 10.7 %collective-permute-start.13 = (bf16[40,1152]{1,0:T(8,128)(2,1)S(1)}, bf16[40,1152]{1,0:T(8,128)(2,1)S(1)}, u32[]{:S(2)}, u32[]{:S(2)}) collective-permute-start(bf16[40,1152]{1,0:T(8,128)(2,1)S(1)} %get-tuple-element.55), channel_id=1, source_target_pairs={{0,4},{2,6},{4,0},{6,2},{1,5},{3,7},{5,1},{7,3},{8,12},{10,14},{12... | collective-permute-start | bytes 276488 | tf_op jit(solution)/shard_map/ppermute | solution.py:18
  113.6 8.6 %collective-permute-start.14 = (bf16[40,1152]{1,0:T(8,128)(2,1)S(1)}, bf16[40,1152]{1,0:T(8,128)(2,1)S(1)}, u32[]{:S(2)}, u32[]{:S(2)}) collective-permute-start(bf16[40,1152]{1,0:T(8,128)(2,1)S(1)} %get-tuple-element.54), channel_id=1, source_target_pairs={{0,6},{2,4},{4,2},{6,0},{1,7},{3,5},{5,3},{7,1},{8,14},{10,12},{12... | collective-permute-start | bytes 276488 | tf_op jit(solution)/shard_map/ppermute | solution.py:18
  117.4 6.7 %collective-permute-start.15 = (bf16[40,1152]{1,0:T(8,128)(2,1)S(1)}, bf16[40,1152]{1,0:T(8,128)(2,1)S(1)}, u32[]{:S(2)}, u32[]{:S(2)}) collective-permute-start(bf16[40,1152]{1,0:T(8,128)(2,1)S(1)} %get-tuple-element.53), channel_id=1, source_target_pairs={{0,2},{2,0},{4,6},{6,4},{1,3},{3,1},{5,7},{7,5},{8,10},{10,8},{12,... | collective-permute-start | bytes 276488 | tf_op jit(solution)/shard_map/ppermute | solution.py:18
  125.5 10.4 %collective-permute-start.17 = (bf16[40,1152]{1,0:T(8,128)(2,1)S(1)}, bf16[40,1152]{1,0:T(8,128)(2,1)S(1)}, u32[]{:S(2)}, u32[]{:S(2)}) collective-permute-start(bf16[40,1152]{1,0:T(8,128)(2,1)S(1)} %fusion.32), channel_id=1, source_target_pairs={{0,32},{32,0},{1,33},{33,1},{2,34},{34,2},{3,35},{35,3},{4,36},{36... | collective-permute-start | bytes 276488 | tf_op jit(solution)/shard_map/ppermute | solution.py:18
  137.3 17.6 %collective-permute-start.21 = (bf16[64,1152]{1,0:T(8,128)(2,1)}, bf16[64,1152]{1,0:T(8,128)(2,1)}, u32[]{:S(2)}, u32[]{:S(2)}) collective-permute-start(bf16[64,1152]{1,0:T(8,128)(2,1)} %get-tuple-element.58), channel_id=1, source_target_pairs={{0,4},{2,6},{4,0},{6,2},{1,5},{3,7},{5,1},{7,3},{8,12},{10,14},{12... | collective-permute-start | bytes 442376 | tf_op jit(solution)/shard_map/ppermute | solution.py:18
  141.8 13.1 %collective-permute-start.18 = (bf16[40,1152]{1,0:T(8,128)(2,1)}, bf16[40,1152]{1,0:T(8,128)(2,1)}, u32[]{:S(2)}, u32[]{:S(2)}) collective-permute-start(bf16[40,1152]{1,0:T(8,128)(2,1)} %reduce-precision_convert_fusion.9), channel_id=1, source_target_pairs={{0,128},{64,192},{128,0},{192,64},{256,384},{320,448},{384,256},{4... | collective-permute-start | bytes 276488 | tf_op jit(solution)/shard_map/ppermute | solution.py:18
  144.9 10.0 %collective-permute-start.19 = (bf16[40,1152]{1,0:T(8,128)(2,1)}, bf16[40,1152]{1,0:T(8,128)(2,1)}, u32[]{:S(2)}, u32[]{:S(2)}) collective-permute-start(bf16[40,1152]{1,0:T(8,128)(2,1)} %reduce-precision_convert_fusion.9), channel_id=1, source_target_pairs={{0,192},{64,128},{128,64},{192,0},{256,448},{320,384},{384,320},{4... | collective-permute-start | bytes 276488 | tf_op jit(solution)/shard_map/ppermute | solution.py:18
  147.6 7.3 %collective-permute-start.20 = (bf16[40,1152]{1,0:T(8,128)(2,1)}, bf16[40,1152]{1,0:T(8,128)(2,1)}, u32[]{:S(2)}, u32[]{:S(2)}) collective-permute-start(bf16[40,1152]{1,0:T(8,128)(2,1)} %reduce-precision_convert_fusion.9), channel_id=1, source_target_pairs={{0,64},{64,0},{128,192},{192,128},{256,320},{320,256},{384,448},{4... | collective-permute-start | bytes 276488 | tf_op jit(solution)/shard_map/ppermute | solution.py:18
  151.2 26.5 %collective-permute-start.24 = (bf16[64,1152]{1,0:T(8,128)(2,1)}, bf16[64,1152]{1,0:T(8,128)(2,1)S(1)}, u32[]{:S(2)}, u32[]{:S(2)}) collective-permute-start(bf16[64,1152]{1,0:T(8,128)(2,1)} %get-tuple-element.56), channel_id=1, source_target_pairs={{0,4},{2,6},{4,0},{6,2},{1,5},{3,7},{5,1},{7,3},{8,12},{10,14},{12... | collective-permute-start | bytes 442376 | tf_op jit(solution)/shard_map/ppermute | solution.py:18
  156.0 35.2 %copy-start.2 = (f32[384,1152]{1,0:T(8,128)S(1)}, f32[384,1152]{1,0:T(8,128)}, u32[]{:S(2)}) copy-start(f32[384,1152]{1,0:T(8,128)} %copy-done.1) | copy-start | bytes 5308420
  156.0 21.7 %collective-permute-start.22 = (bf16[40,1152]{1,0:T(8,128)(2,1)S(1)}, bf16[40,1152]{1,0:T(8,128)(2,1)S(1)}, u32[]{:S(2)}, u32[]{:S(2)}) collective-permute-start(bf16[40,1152]{1,0:T(8,128)(2,1)S(1)} %reduce-precision_convert_fusion.8), channel_id=1, source_target_pairs={{0,512},{64,576},{128,640},{192,704},{256,0},{320,64},{384,128},{4... | collective-permute-start | bytes 276488 | tf_op jit(solution)/shard_map/ppermute | solution.py:23
  169.1 14.2 %collective-permute-start.23 = (bf16[40,1152]{1,0:T(8,128)(2,1)S(1)}, bf16[40,1152]{1,0:T(8,128)(2,1)S(1)}, u32[]{:S(2)}, u32[]{:S(2)}) collective-permute-start(bf16[40,1152]{1,0:T(8,128)(2,1)S(1)} %reduce-precision_convert_fusion.8), channel_id=1, source_target_pairs={{0,256},{64,320},{128,384},{192,448},{256,512},{320,576},{384,640}... | collective-permute-start | bytes 276488 | tf_op jit(solution)/shard_map/ppermute | solution.py:23
  174.0 17.2 %collective-permute-start.25 = (bf16[64,1152]{1,0:T(8,128)(2,1)S(1)}, bf16[64,1152]{1,0:T(8,128)(2,1)S(1)}, u32[]{:S(2)}, u32[]{:S(2)}) collective-permute-start(bf16[64,1152]{1,0:T(8,128)(2,1)S(1)} %copy-done.14), channel_id=1, source_target_pairs={{0,4},{2,6},{4,0},{6,2},{1,5},{3,7},{5,1},{7,3},{8,12},{10,14},{12... | collective-permute-start | bytes 442376 | tf_op jit(solution)/shard_map/ppermute | solution.py:18
  183.4 11.2 %collective-permute-start.26 = (bf16[40,1152]{1,0:T(8,128)(2,1)S(1)}, bf16[40,1152]{1,0:T(8,128)(2,1)S(1)}, u32[]{:S(2)}, u32[]{:S(2)}) collective-permute-start(bf16[40,1152]{1,0:T(8,128)(2,1)S(1)} %reduce-precision_convert_fusion.7), channel_id=1, source_target_pairs={{0,16},{8,24},{16,0},{24,8},{1,17},{9,25},{17,1},{25,9},{2,18},{10... | collective-permute-start | bytes 276488 | tf_op jit(solution)/shard_map/ppermute | solution.py:23
  185.3 9.3 %collective-permute-start.28 = (bf16[40,1152]{1,0:T(8,128)(2,1)S(1)}, bf16[40,1152]{1,0:T(8,128)(2,1)S(1)}, u32[]{:S(2)}, u32[]{:S(2)}) collective-permute-start(bf16[40,1152]{1,0:T(8,128)(2,1)S(1)} %reduce-precision_convert_fusion.7), channel_id=1, source_target_pairs={{0,24},{8,0},{16,8},{24,16},{1,25},{9,1},{17,9},{25,17},{2,26},{10... | collective-permute-start | bytes 276488 | tf_op jit(solution)/shard_map/ppermute | solution.py:23
  187.2 8.5 %collective-permute-start.27 = (bf16[40,1152]{1,0:T(8,128)(2,1)S(1)}, bf16[40,1152]{1,0:T(8,128)(2,1)S(1)}, u32[]{:S(2)}, u32[]{:S(2)}) collective-permute-start(bf16[40,1152]{1,0:T(8,128)(2,1)S(1)} %reduce-precision_convert_fusion.7), channel_id=1, source_target_pairs={{0,8},{8,16},{16,24},{24,0},{1,9},{9,17},{17,25},{25,1},{2,10},{10... | collective-permute-start | bytes 276488 | tf_op jit(solution)/shard_map/ppermute | solution.py:23
  (14 other events, 253.3 us)

commit v5 on v4

--- a/solution.py
+++ b/solution.py
@@ -62,16 +62,17 @@
     rows = pictures.shape[0]
     z, x, y, k = (lax.axis_index(a) for a in ("z", "x", "y", "k"))
 
-    paired, moved_half = shifted(captions, x)
-    picture = pictures.astype(f32)
-    image_scale = lax.rsqrt(jnp.sum(picture * picture, -1, keepdims=True) + eps)
-    image_unit = picture * image_scale
-    image_low = image_unit.astype(bf16)
-    image_out, _ = tie(image_low, moved_half)
-    image_far = swap(image_out, "y", 2)
-    image_core = swap(image_out, "k", 1)
-    images = jnp.concatenate([image_low, image_far, image_core, swap(image_far, "k", 1)])
+    paired = shifted(captions, x)
+    image_far = swap(pictures, "y", 2)
+    image_core = swap(pictures, "k", 1)
     texts = jnp.concatenate([paired, swap(paired, "y", 1)])
+    texts, image_both = tie(texts, swap(image_far, "k", 1))
+    raw = jnp.concatenate([pictures, image_far, image_core, image_both])
+    raw = raw.astype(f32)
+    image_scale = lax.rsqrt(jnp.sum(raw * raw, -1, keepdims=True) + eps)
+    images = (raw * image_scale).astype(bf16)
+    image_scale = image_scale[:rows]
+    image_unit = pictures.astype(f32) * image_scale
 
     projected = dot(texts, matrix, 1, 0) + intercept
     text_scale = lax.rsqrt(jnp.sum(projected * projected, -1, keepdims=True) + eps)
@@ -159,7 +160,7 @@
     moved = turn(low_half, "x", 1)
     first = jnp.where(x == 0, cross(moved, 0), moved)
     second = turn(jnp.where(x == 3, crossed, high_half), "x", 1)
-    return jnp.concatenate([first, second]), moved
+    return jnp.concatenate([first, second])
 
 
 def solution(mesh):

time: 199 us -> 200 us (level)
    ppermute x17, waiting for transfers between devices: 20 us -> 15.7 us  [swap(): return lax.ppermute(block, axis, [(i, i ^ mask) for i in range(n)])]
    ppermute x2, waiting for transfers between devices: 2.1 us -> 5.84 us  [cross(): return lax.ppermute(half, COL, pairs)]
  transfers between devices with their start and end apart: 29 -> 29, of which waited for: 11 -> 12; matrix products, arithmetic and copies ran while one was open for 14% -> 11% of each run, Pallas kernels for 0% -> 0%
where the time goes in v5:
time: 200 us; the launch traced here: 198 us
  starting transfers between devices  105 us (52%)
  waiting for transfers between devices  49.1 us (25%)
  matrix products  19.1 us (10%)
  other arithmetic  16.5 us (8%)
  local copies, waits for them, and re-layouts  5.89 us (3%)
  between operations  2.82 us (1%)
    ppermute x17, starting transfers between devices, swap(): return lax.ppermute(block, axis, [(i, i ^ mask) for i in range(n)])  60.6 us
    ppermute x10, starting transfers between devices, turn(): lax.ppermute(block, axis, [(i, (i + distance) % n) for i in range(n)])  36.3 us
    ppermute x10, waiting for transfers between devices, turn(): lax.ppermute(block, axis, [(i, (i + distance) % n) for i in range(n)])  27.5 us
    dot_general x10, matrix products, dot(): lax.dot_general(a, b, (((ca,), (cb,)), ((), ())), preferred_element_type=...  19.1 us
    ppermute x17, waiting for transfers between devices, swap(): return lax.ppermute(block, axis, [(i, i ^ mask) for i in range(n)])  15.7 us
    ppermute x2, starting transfers between devices, cross(): return lax.ppermute(half, COL, pairs)  8.18 us
    convert_element_type x7, other arithmetic, low(): return lax.reduce_precision(values, 8, 7).astype(bf16)  7.3 us
    ppermute x2, waiting for transfers between devices, cross(): return lax.ppermute(half, COL, pairs)  5.84 us
  transfers between devices with their start and end apart: 29, of which 12 were waited for; matrix products, arithmetic and copies ran while one was open for 11% of the time, Pallas kernels for 0%

profile of v5, /device:TPU:56, one launch (start us, length us, event | category | flops | bytes accessed | tf_op | source)
XLA Modules:
  0.0 198.5 jit_solution(9260969308072037952)
XLA Ops:
  0.6 4.3 %collective-permute-start = (bf16[192,1152]{1,0:T(8,128)(2,1)}, bf16[192,1152]{1,0:T(8,128)(2,1)S(1)}, u32[]{:S(2)}, u32[]{:S(2)}) collective-permute-start(bf16[192,1152]{1,0:T(8,128)(2,1)} %param.7), channel_id=1, source_target_pairs={{0,4},{2,6},{4,0},{6,2},{1,5},{3,7},{5,1},{7,3},{8,12},{10,14},{12... | collective-permute-start | bytes 1327112 | tf_op jit(solution)/shard_map/ppermute | solution.py:18
  9.3 3.4 %collective-permute-start.2 = (bf16[96,1152]{1,0:T(8,128)(2,1)S(1)}, bf16[96,1152]{1,0:T(8,128)(2,1)}, u32[]{:S(2)}, u32[]{:S(2)}) collective-permute-start(bf16[96,1152]{1,0:T(8,128)(2,1)S(1)} %get-tuple-element.28), channel_id=1, source_target_pairs={{0,8},{8,16},{16,24},{24,0},{1,9},{9,17},{17,25},{25,1},{2,10},{10... | collective-permute-start | bytes 663560 | tf_op jit(solution)/shard_map/ppermute | solution.py:23
  14.5 8.8 %collective-permute-done.2 = bf16[96,1152]{1,0:T(8,128)(2,1)} collective-permute-done((bf16[96,1152]{1,0:T(8,128)(2,1)S(1)}, bf16[96,1152]{1,0:T(8,128)(2,1)}, u32[]{:S(2)}, u32[]{:S(2)}) %collective-permute-start.2) | collective-permute-done | bytes 221216 | tf_op jit(solution)/shard_map/ppermute | solution.py:23
  23.3 6.8 %collective-permute-start.3 = (bf16[96,1152]{1,0:T(8,128)(2,1)}, bf16[96,1152]{1,0:T(8,128)(2,1)S(1)}, u32[]{:S(2)}, u32[]{:S(2)}) collective-permute-start(bf16[96,1152]{1,0:T(8,128)(2,1)} %collective-permute-done.2), channel_id=1, source_target_pairs={{0,32},{32,64},{64,96},{96,128},{128,160},{160,192},{192,224},{224... | collective-permute-start | bytes 663560 | tf_op jit(solution)/shard_map/ppermute | solution.py:155
  32.1 5.8 %collective-permute-done.3 = bf16[96,1152]{1,0:T(8,128)(2,1)S(1)} collective-permute-done((bf16[96,1152]{1,0:T(8,128)(2,1)}, bf16[96,1152]{1,0:T(8,128)(2,1)S(1)}, u32[]{:S(2)}, u32[]{:S(2)}) %collective-permute-start.3) | collective-permute-done | bytes 221216 | tf_op jit(solution)/shard_map/ppermute | solution.py:155
  40.1 10.2 %collective-permute-start.6 = (bf16[192,1152]{1,0:T(8,128)(2,1)S(1)}, bf16[192,1152]{1,0:T(8,128)(2,1)S(1)}, u32[]{:S(2)}, u32[]{:S(2)}) collective-permute-start(bf16[192,1152]{1,0:T(8,128)(2,1)S(1)} %pad_maximum_fusion.2), channel_id=1, source_target_pairs={{0,2},{2,0},{4,6},{6,4},{1,3},{3,1},{5,7},{7,5},{8,10},{10,8},{12,... | collective-permute-start | bytes 1327112 | tf_op jit(solution)/shard_map/ppermute | solution.py:18
  54.1 5.7 %collective-permute-done.6 = bf16[192,1152]{1,0:T(8,128)(2,1)S(1)} collective-permute-done((bf16[192,1152]{1,0:T(8,128)(2,1)S(1)}, bf16[192,1152]{1,0:T(8,128)(2,1)S(1)}, u32[]{:S(2)}, u32[]{:S(2)}) %collective-permute-start.6) | collective-permute-done | bytes 442400 | tf_op jit(solution)/shard_map/ppermute | solution.py:18
  65.7 2.8 %fusion.14 = bf16[768,384]{1,0:T(8,128)(2,1)S(1)} fusion(bf16[384,1152]{1,0:T(8,128)(2,1)S(1)} %multiply_convert_fusion, f32[768]{0:T(1024)S(1)} %add_rsqrt_fusion, f32[]{:T(128)} %bitcast.53, f32[]{:T(128)} %bitcast.50, s32[768]{0:T(1024)S(1)} %concatenate.19, bf16[192,1152]{1,0:T(8,128)(2,1)S(1)} %collective-permute-done.7, ...), kind=kOutput, calls=%fused_computation.32 | convolution fusion | flops 691568640 | bytes 3250184 | tf_op jit(solution)/shard_map/dot_general | solution.py:31
  68.6 2.4 %multiply_reduce_fusion = (f32[384]{0:T(512)S(1)}, f32[384,1152]{1,0:T(8,128)S(1)}) fusion(f32[384,1152]{1,0:T(8,128)S(1)} %get-tuple-element.66, f32[384]{0:T(512)S(1)} %add_rsqrt_fusion.1, bf16[768,384]{1,0:T(8,128)(2,1)S(1)} %fusion.14, f32[768]{0:T(1024)S(1)} %add_rsqrt_fusion, bf16[192,1152]{1,0:T(8,128)(2,1)S(1)} %collective-permute-done.7, ...), kind=kOutput, calls=%fused_computation.17 | convolution fusion | flops 690093696 | bytes 5904388 | tf_op jit(solution)/shard_map/dot_general | solution.py:31
  76.2 3.6 %collective-permute-start.12 = (bf16[192,1152]{1,0:T(8,128)(2,1)}, bf16[192,1152]{1,0:T(8,128)(2,1)}, u32[]{:S(2)}, u32[]{:S(2)}) collective-permute-start(bf16[192,1152]{1,0:T(8,128)(2,1)} %slice.80), channel_id=1, source_target_pairs={{0,2},{2,0},{4,6},{6,4},{1,3},{3,1},{5,7},{7,5},{8,10},{10,8},{12,... | collective-permute-start | bytes 1327112 | tf_op jit(solution)/shard_map/ppermute | solution.py:18
  83.1 2.4 %fusion.23 = (bf16[160,1152]{1,0:T(8,128)(2,1)}, bf16[160,1152]{1,0:T(8,128)(2,1)}, bf16[160,1152]{1,0:T(8,128)(2,1)}) fusion(bf16[4,160,1152]{2,1,0:T(8,128)(2,1)} %bitcast.5, s32[]{:T(128)S(6)} %select_n.332, bf16[4,160,1152]{2,1,0:T(8,128)(2,1)S(1)} %bitcast.54, s32[]{:T(128)S(6)} %select_n.330, s32[]{:T(128)S(6)} %select_n.328), kind=kLoop, calls=%fused_computation.51 | loop fusion | flops 2764800 | bytes 3317772 | tf_op jit(solution)/shard_map/convert_element_type | solution.py:27
  85.4 2.3 %collective-permute-start.9 = (bf16[160,1152]{1,0:T(8,128)(2,1)}, bf16[160,1152]{1,0:T(8,128)(2,1)}, u32[]{:S(2)}, u32[]{:S(2)}) collective-permute-start(bf16[160,1152]{1,0:T(8,128)(2,1)} %get-tuple-element.54), channel_id=1, source_target_pairs={{0,16},{8,24},{16,0},{24,8},{1,17},{9,25},{17,1},{25,9},{2,18},{10... | collective-permute-start | bytes 1105928 | tf_op jit(solution)/shard_map/ppermute | solution.py:23
  87.7 3.8 %collective-permute-start.10 = (bf16[160,1152]{1,0:T(8,128)(2,1)}, bf16[160,1152]{1,0:T(8,128)(2,1)}, u32[]{:S(2)}, u32[]{:S(2)}) collective-permute-start(bf16[160,1152]{1,0:T(8,128)(2,1)} %get-tuple-element.53), channel_id=1, source_target_pairs={{0,8},{8,16},{16,24},{24,0},{1,9},{9,17},{17,25},{25,1},{2,10},{10... | collective-permute-start | bytes 1105928 | tf_op jit(solution)/shard_map/ppermute | solution.py:23
  91.5 3.3 %collective-permute-start.11 = (bf16[160,1152]{1,0:T(8,128)(2,1)}, bf16[160,1152]{1,0:T(8,128)(2,1)}, u32[]{:S(2)}, u32[]{:S(2)}) collective-permute-start(bf16[160,1152]{1,0:T(8,128)(2,1)} %get-tuple-element.52), channel_id=1, source_target_pairs={{0,24},{8,0},{16,8},{24,16},{1,25},{9,1},{17,9},{25,17},{2,26},{10... | collective-permute-start | bytes 1105928 | tf_op jit(solution)/shard_map/ppermute | solution.py:23
  96.8 3.8 %collective-permute-done.9 = bf16[160,1152]{1,0:T(8,128)(2,1)} collective-permute-done((bf16[160,1152]{1,0:T(8,128)(2,1)}, bf16[160,1152]{1,0:T(8,128)(2,1)}, u32[]{:S(2)}, u32[]{:S(2)}) %collective-permute-start.9) | collective-permute-done | bytes 368672 | tf_op jit(solution)/shard_map/ppermute | solution.py:23
  100.6 7.1 %collective-permute-done.10 = bf16[160,1152]{1,0:T(8,128)(2,1)} collective-permute-done((bf16[160,1152]{1,0:T(8,128)(2,1)}, bf16[160,1152]{1,0:T(8,128)(2,1)}, u32[]{:S(2)}, u32[]{:S(2)}) %collective-permute-start.10) | collective-permute-done | bytes 368672 | tf_op jit(solution)/shard_map/ppermute | solution.py:23
  113.1 2.8 %collective-permute-start.13 = (bf16[40,1152]{1,0:T(8,128)(2,1)S(1)}, bf16[40,1152]{1,0:T(8,128)(2,1)S(1)}, u32[]{:S(2)}, u32[]{:S(2)}) collective-permute-start(bf16[40,1152]{1,0:T(8,128)(2,1)S(1)} %get-tuple-element.57), channel_id=1, source_target_pairs={{0,4},{2,6},{4,0},{6,2},{1,5},{3,7},{5,1},{7,3},{8,12},{10,14},{12... | collective-permute-start | bytes 276488 | tf_op jit(solution)/shard_map/ppermute | solution.py:18
  116.0 3.8 %collective-permute-start.14 = (bf16[40,1152]{1,0:T(8,128)(2,1)S(1)}, bf16[40,1152]{1,0:T(8,128)(2,1)S(1)}, u32[]{:S(2)}, u32[]{:S(2)}) collective-permute-start(bf16[40,1152]{1,0:T(8,128)(2,1)S(1)} %get-tuple-element.56), channel_id=1, source_target_pairs={{0,6},{2,4},{4,2},{6,0},{1,7},{3,5},{5,3},{7,1},{8,14},{10,12},{12... | collective-permute-start | bytes 276488 | tf_op jit(solution)/shard_map/ppermute | solution.py:18
  119.8 2.7 %collective-permute-start.15 = (bf16[40,1152]{1,0:T(8,128)(2,1)S(1)}, bf16[40,1152]{1,0:T(8,128)(2,1)S(1)}, u32[]{:S(2)}, u32[]{:S(2)}) collective-permute-start(bf16[40,1152]{1,0:T(8,128)(2,1)S(1)} %get-tuple-element.55), channel_id=1, source_target_pairs={{0,2},{2,0},{4,6},{6,4},{1,3},{3,1},{5,7},{7,5},{8,10},{10,8},{12,... | collective-permute-start | bytes 276488 | tf_op jit(solution)/shard_map/ppermute | solution.py:18
  128.1 5.7 %collective-permute-start.17 = (bf16[40,1152]{1,0:T(8,128)(2,1)S(1)}, bf16[40,1152]{1,0:T(8,128)(2,1)S(1)}, u32[]{:S(2)}, u32[]{:S(2)}) collective-permute-start(bf16[40,1152]{1,0:T(8,128)(2,1)S(1)} %fusion.29), channel_id=1, source_target_pairs={{0,32},{32,0},{1,33},{33,1},{2,34},{34,2},{3,35},{35,3},{4,36},{36... | collective-permute-start | bytes 276488 | tf_op jit(solution)/shard_map/ppermute | solution.py:18
  133.9 5.7 %collective-permute-done.17 = bf16[40,1152]{1,0:T(8,128)(2,1)S(1)} collective-permute-done((bf16[40,1152]{1,0:T(8,128)(2,1)S(1)}, bf16[40,1152]{1,0:T(8,128)(2,1)S(1)}, u32[]{:S(2)}, u32[]{:S(2)}) %collective-permute-start.17) | collective-permute-done | bytes 92192 | tf_op jit(solution)/shard_map/ppermute | solution.py:18
  141.0 3.6 %collective-permute-start.21 = (bf16[64,1152]{1,0:T(8,128)(2,1)}, bf16[64,1152]{1,0:T(8,128)(2,1)}, u32[]{:S(2)}, u32[]{:S(2)}) collective-permute-start(bf16[64,1152]{1,0:T(8,128)(2,1)} %get-tuple-element.60), channel_id=1, source_target_pairs={{0,4},{2,6},{4,0},{6,2},{1,5},{3,7},{5,1},{7,3},{8,12},{10,14},{12... | collective-permute-start | bytes 442376 | tf_op jit(solution)/shard_map/ppermute | solution.py:18
  144.6 2.4 %collective-permute-start.18 = (bf16[40,1152]{1,0:T(8,128)(2,1)}, bf16[40,1152]{1,0:T(8,128)(2,1)}, u32[]{:S(2)}, u32[]{:S(2)}) collective-permute-start(bf16[40,1152]{1,0:T(8,128)(2,1)} %reduce-precision_convert_fusion.9), channel_id=1, source_target_pairs={{0,128},{64,192},{128,0},{192,64},{256,384},{320,448},{384,256},{4... | collective-permute-start | bytes 276488 | tf_op jit(solution)/shard_map/ppermute | solution.py:18
  147.0 4.3 %collective-permute-start.19 = (bf16[40,1152]{1,0:T(8,128)(2,1)}, bf16[40,1152]{1,0:T(8,128)(2,1)}, u32[]{:S(2)}, u32[]{:S(2)}) collective-permute-start(bf16[40,1152]{1,0:T(8,128)(2,1)} %reduce-precision_convert_fusion.9), channel_id=1, source_target_pairs={{0,192},{64,128},{128,64},{192,0},{256,448},{320,384},{384,320},{4... | collective-permute-start | bytes 276488 | tf_op jit(solution)/shard_map/ppermute | solution.py:18
  151.3 2.5 %collective-permute-start.20 = (bf16[40,1152]{1,0:T(8,128)(2,1)}, bf16[40,1152]{1,0:T(8,128)(2,1)}, u32[]{:S(2)}, u32[]{:S(2)}) collective-permute-start(bf16[40,1152]{1,0:T(8,128)(2,1)} %reduce-precision_convert_fusion.9), channel_id=1, source_target_pairs={{0,64},{64,0},{128,192},{192,128},{256,320},{320,256},{384,448},{4... | collective-permute-start | bytes 276488 | tf_op jit(solution)/shard_map/ppermute | solution.py:18
  154.0 3.2 %collective-permute-start.24 = (bf16[64,1152]{1,0:T(8,128)(2,1)}, bf16[64,1152]{1,0:T(8,128)(2,1)S(1)}, u32[]{:S(2)}, u32[]{:S(2)}) collective-permute-start(bf16[64,1152]{1,0:T(8,128)(2,1)} %get-tuple-element.58), channel_id=1, source_target_pairs={{0,4},{2,6},{4,0},{6,2},{1,5},{3,7},{5,1},{7,3},{8,12},{10,14},{12... | collective-permute-start | bytes 442376 | tf_op jit(solution)/shard_map/ppermute | solution.py:18
  159.2 11.8 %collective-permute-start.22 = (bf16[40,1152]{1,0:T(8,128)(2,1)S(1)}, bf16[40,1152]{1,0:T(8,128)(2,1)S(1)}, u32[]{:S(2)}, u32[]{:S(2)}) collective-permute-start(bf16[40,1152]{1,0:T(8,128)(2,1)S(1)} %reduce-precision_convert_fusion.8), channel_id=1, source_target_pairs={{0,512},{64,576},{128,640},{192,704},{256,0},{320,64},{384,128},{4... | collective-permute-start | bytes 276488 | tf_op jit(solution)/shard_map/ppermute | solution.py:23
  172.9 3.0 %fusion.19 = f32[192,1152]{1,0:T(8,128)} fusion(bf16[1152,1152]{1,0:T(8,128)(2,1)S(1)} %copy-done, bf16[192,1152]{1,0:T(8,128)(2,1)} %collective-permute-done.12, bf16[384,1152]{1,0:T(8,128)(2,1)S(1)} %reduce-precision_convert_fusion), kind=kOutput, calls=%fused_computation.46 | convolution fusion | flops 510492672 | bytes 4423680 | tf_op jit(solution)/shard_map/dot_general | solution.py:31
  175.9 3.8 %collective-permute-start.25 = (bf16[64,1152]{1,0:T(8,128)(2,1)S(1)}, bf16[64,1152]{1,0:T(8,128)(2,1)S(1)}, u32[]{:S(2)}, u32[]{:S(2)}) collective-permute-start(bf16[64,1152]{1,0:T(8,128)(2,1)S(1)} %copy-done.13), channel_id=1, source_target_pairs={{0,4},{2,6},{4,0},{6,2},{1,5},{3,7},{5,1},{7,3},{8,12},{10,14},{12... | collective-permute-start | bytes 442376 | tf_op jit(solution)/shard_map/ppermute | solution.py:18
  179.7 4.2 %collective-permute-done.23 = bf16[40,1152]{1,0:T(8,128)(2,1)S(1)} collective-permute-done((bf16[40,1152]{1,0:T(8,128)(2,1)S(1)}, bf16[40,1152]{1,0:T(8,128)(2,1)S(1)}, u32[]{:S(2)}, u32[]{:S(2)}) %collective-permute-start.23) | collective-permute-done | bytes 92192 | tf_op jit(solution)/shard_map/ppermute | solution.py:23
  186.1 3.1 %collective-permute-start.28 = (bf16[40,1152]{1,0:T(8,128)(2,1)S(1)}, bf16[40,1152]{1,0:T(8,128)(2,1)S(1)}, u32[]{:S(2)}, u32[]{:S(2)}) collective-permute-start(bf16[40,1152]{1,0:T(8,128)(2,1)S(1)} %reduce-precision_convert_fusion.7), channel_id=1, source_target_pairs={{0,24},{8,0},{16,8},{24,16},{1,25},{9,1},{17,9},{25,17},{2,26},{10... | collective-permute-start | bytes 276488 | tf_op jit(solution)/shard_map/ppermute | solution.py:23
  189.2 2.8 %collective-permute-start.27 = (bf16[40,1152]{1,0:T(8,128)(2,1)S(1)}, bf16[40,1152]{1,0:T(8,128)(2,1)S(1)}, u32[]{:S(2)}, u32[]{:S(2)}) collective-permute-start(bf16[40,1152]{1,0:T(8,128)(2,1)S(1)} %reduce-precision_convert_fusion.7), channel_id=1, source_target_pairs={{0,8},{8,16},{16,24},{24,0},{1,9},{9,17},{17,25},{25,1},{2,10},{10... | collective-permute-start | bytes 276488 | tf_op jit(solution)/shard_map/ppermute | solution.py:23
  (103 shorter events, 53.9 us)
Async XLA Ops:
  0.6 63.4 %copy-start = (bf16[1152,1152]{1,0:T(8,128)(2,1)S(1)}, bf16[1152,1152]{1,0:T(8,128)(2,1)}, u32[]{:S(2)}) copy-start(bf16[1152,1152]{1,0:T(8,128)(2,1)} %param.10) | copy-start | bytes 7962628
  0.6 49.6 %collective-permute-start = (bf16[192,1152]{1,0:T(8,128)(2,1)}, bf16[192,1152]{1,0:T(8,128)(2,1)S(1)}, u32[]{:S(2)}, u32[]{:S(2)}) collective-permute-start(bf16[192,1152]{1,0:T(8,128)(2,1)} %param.7), channel_id=1, source_target_pairs={{0,4},{2,6},{4,0},{6,2},{1,5},{3,7},{5,1},{7,3},{8,12},{10,14},{12... | collective-permute-start | bytes 1327112 | tf_op jit(solution)/shard_map/ppermute | solution.py:18
  5.0 54.9 %collective-permute-start.1 = (bf16[192,1152]{1,0:T(8,128)(2,1)}, bf16[192,1152]{1,0:T(8,128)(2,1)}, u32[]{:S(2)}, u32[]{:S(2)}) collective-permute-start(bf16[192,1152]{1,0:T(8,128)(2,1)} %param.7), channel_id=1, source_target_pairs={{0,1},{1,0},{2,3},{3,2},{4,5},{5,4},{6,7},{7,6},{8,9},{9,8},{10,11... | collective-permute-start | bytes 1327112 | tf_op jit(solution)/shard_map/ppermute | solution.py:18
  8.0 22.1 %collective-permute-start.4 = (bf16[96,1152]{1,0:T(8,128)(2,1)S(1)}, bf16[96,1152]{1,0:T(8,128)(2,1)}, u32[]{:S(2)}, u32[]{:S(2)}) collective-permute-start(bf16[96,1152]{1,0:T(8,128)(2,1)S(1)} %get-tuple-element.29), channel_id=1, source_target_pairs={{24,56},{56,88},{88,120},{120,152},{152,184},{184,216},{216,248},{... | collective-permute-start | bytes 663560 | tf_op jit(solution)/shard_map/ppermute | solution.py:155
  9.3 14.0 %collective-permute-start.2 = (bf16[96,1152]{1,0:T(8,128)(2,1)S(1)}, bf16[96,1152]{1,0:T(8,128)(2,1)}, u32[]{:S(2)}, u32[]{:S(2)}) collective-permute-start(bf16[96,1152]{1,0:T(8,128)(2,1)S(1)} %get-tuple-element.28), channel_id=1, source_target_pairs={{0,8},{8,16},{16,24},{24,0},{1,9},{9,17},{17,25},{25,1},{2,10},{10... | collective-permute-start | bytes 663560 | tf_op jit(solution)/shard_map/ppermute | solution.py:23
  14.5 39.6 %copy-start.14 = (s32[1,192]{1,0:T(1,128)S(1)}, s32[1,192]{1,0:T(1,128)}, u32[]{:S(2)}) copy-start(s32[1,192]{1,0:T(1,128)} %param.9) | copy-start | bytes 2308
  23.3 14.7 %collective-permute-start.3 = (bf16[96,1152]{1,0:T(8,128)(2,1)}, bf16[96,1152]{1,0:T(8,128)(2,1)S(1)}, u32[]{:S(2)}, u32[]{:S(2)}) collective-permute-start(bf16[96,1152]{1,0:T(8,128)(2,1)} %collective-permute-done.2), channel_id=1, source_target_pairs={{0,32},{32,64},{64,96},{96,128},{128,160},{160,192},{192,224},{224... | collective-permute-start | bytes 663560 | tf_op jit(solution)/shard_map/ppermute | solution.py:155
  30.2 9.9 %collective-permute-start.5 = (bf16[96,1152]{1,0:T(8,128)(2,1)S(1)}, bf16[96,1152]{1,0:T(8,128)(2,1)S(1)}, u32[]{:S(2)}, u32[]{:S(2)}) collective-permute-start(bf16[96,1152]{1,0:T(8,128)(2,1)S(1)} %broadcast_select_fusion), channel_id=1, source_target_pairs={{0,8},{8,16},{16,24},{24,0},{1,9},{9,17},{17,25},{25,1},{2,10},{10... | collective-permute-start | bytes 663560 | tf_op jit(solution)/shard_map/ppermute | solution.py:23
  40.1 19.7 %collective-permute-start.6 = (bf16[192,1152]{1,0:T(8,128)(2,1)S(1)}, bf16[192,1152]{1,0:T(8,128)(2,1)S(1)}, u32[]{:S(2)}, u32[]{:S(2)}) collective-permute-start(bf16[192,1152]{1,0:T(8,128)(2,1)S(1)} %pad_maximum_fusion.2), channel_id=1, source_target_pairs={{0,2},{2,0},{4,6},{6,4},{1,3},{3,1},{5,7},{7,5},{8,10},{10,8},{12,... | collective-permute-start | bytes 1327112 | tf_op jit(solution)/shard_map/ppermute | solution.py:18
  50.3 9.6 %collective-permute-start.7 = (bf16[192,1152]{1,0:T(8,128)(2,1)S(1)}, bf16[192,1152]{1,0:T(8,128)(2,1)S(1)}, u32[]{:S(2)}, u32[]{:S(2)}) collective-permute-start(bf16[192,1152]{1,0:T(8,128)(2,1)S(1)} %collective-permute-done), channel_id=1, source_target_pairs={{0,1},{1,0},{2,3},{3,2},{4,5},{5,4},{6,7},{7,6},{8,9},{9,8},{10,11... | collective-permute-start | bytes 1327112 | tf_op jit(solution)/shard_map/ppermute | solution.py:18
  73.5 8.5 %collective-permute-start.8 = (bf16[640,1152]{1,0:T(8,128)(2,1)}, bf16[640,1152]{1,0:T(8,128)(2,1)}, u32[]{:S(2)}, u32[]{:S(2)}) collective-permute-start(bf16[640,1152]{1,0:T(8,128)(2,1)} %convolution_convert_fusion), channel_id=1, source_target_pairs={{0,1},{1,0},{2,3},{3,2},{4,5},{5,4},{6,7},{7,6},{8,9},{9,8},{10,11... | collective-permute-start | bytes 4423688 | tf_op jit(solution)/shard_map/ppermute | solution.py:18
  76.2 20.5 %collective-permute-start.12 = (bf16[192,1152]{1,0:T(8,128)(2,1)}, bf16[192,1152]{1,0:T(8,128)(2,1)}, u32[]{:S(2)}, u32[]{:S(2)}) collective-permute-start(bf16[192,1152]{1,0:T(8,128)(2,1)} %slice.80), channel_id=1, source_target_pairs={{0,2},{2,0},{4,6},{6,4},{1,3},{3,1},{5,7},{7,5},{8,10},{10,8},{12,... | collective-permute-start | bytes 1327112 | tf_op jit(solution)/shard_map/ppermute | solution.py:18
  85.4 15.2 %collective-permute-start.9 = (bf16[160,1152]{1,0:T(8,128)(2,1)}, bf16[160,1152]{1,0:T(8,128)(2,1)}, u32[]{:S(2)}, u32[]{:S(2)}) collective-permute-start(bf16[160,1152]{1,0:T(8,128)(2,1)} %get-tuple-element.54), channel_id=1, source_target_pairs={{0,16},{8,24},{16,0},{24,8},{1,17},{9,25},{17,1},{25,9},{2,18},{10... | collective-permute-start | bytes 1105928 | tf_op jit(solution)/shard_map/ppermute | solution.py:23
  87.7 20.0 %collective-permute-start.10 = (bf16[160,1152]{1,0:T(8,128)(2,1)}, bf16[160,1152]{1,0:T(8,128)(2,1)}, u32[]{:S(2)}, u32[]{:S(2)}) collective-permute-start(bf16[160,1152]{1,0:T(8,128)(2,1)} %get-tuple-element.53), channel_id=1, source_target_pairs={{0,8},{8,16},{16,24},{24,0},{1,9},{9,17},{17,25},{25,1},{2,10},{10... | collective-permute-start | bytes 1105928 | tf_op jit(solution)/shard_map/ppermute | solution.py:23
  91.5 16.2 %collective-permute-start.11 = (bf16[160,1152]{1,0:T(8,128)(2,1)}, bf16[160,1152]{1,0:T(8,128)(2,1)}, u32[]{:S(2)}, u32[]{:S(2)}) collective-permute-start(bf16[160,1152]{1,0:T(8,128)(2,1)} %get-tuple-element.52), channel_id=1, source_target_pairs={{0,24},{8,0},{16,8},{24,16},{1,25},{9,1},{17,9},{25,17},{2,26},{10... | collective-permute-start | bytes 1105928 | tf_op jit(solution)/shard_map/ppermute | solution.py:23
  107.7 19.0 %collective-permute-start.16 = (bf16[384,1152]{1,0:T(8,128)(2,1)S(1)}, bf16[384,1152]{1,0:T(8,128)(2,1)S(1)}, u32[]{:S(2)}, u32[]{:S(2)}) collective-permute-start(bf16[384,1152]{1,0:T(8,128)(2,1)S(1)} %fusion.4), channel_id=1, source_target_pairs={{0,1},{1,0},{2,3},{3,2},{4,5},{5,4},{6,7},{7,6},{8,9},{9,8},{10,11... | collective-permute-start | bytes 2654216 | tf_op jit(solution)/shard_map/ppermute | solution.py:18
  113.1 10.1 %collective-permute-start.13 = (bf16[40,1152]{1,0:T(8,128)(2,1)S(1)}, bf16[40,1152]{1,0:T(8,128)(2,1)S(1)}, u32[]{:S(2)}, u32[]{:S(2)}) collective-permute-start(bf16[40,1152]{1,0:T(8,128)(2,1)S(1)} %get-tuple-element.57), channel_id=1, source_target_pairs={{0,4},{2,6},{4,0},{6,2},{1,5},{3,7},{5,1},{7,3},{8,12},{10,14},{12... | collective-permute-start | bytes 276488 | tf_op jit(solution)/shard_map/ppermute | solution.py:18
  116.0 8.8 %collective-permute-start.14 = (bf16[40,1152]{1,0:T(8,128)(2,1)S(1)}, bf16[40,1152]{1,0:T(8,128)(2,1)S(1)}, u32[]{:S(2)}, u32[]{:S(2)}) collective-permute-start(bf16[40,1152]{1,0:T(8,128)(2,1)S(1)} %get-tuple-element.56), channel_id=1, source_target_pairs={{0,6},{2,4},{4,2},{6,0},{1,7},{3,5},{5,3},{7,1},{8,14},{10,12},{12... | collective-permute-start | bytes 276488 | tf_op jit(solution)/shard_map/ppermute | solution.py:18
  119.8 6.9 %collective-permute-start.15 = (bf16[40,1152]{1,0:T(8,128)(2,1)S(1)}, bf16[40,1152]{1,0:T(8,128)(2,1)S(1)}, u32[]{:S(2)}, u32[]{:S(2)}) collective-permute-start(bf16[40,1152]{1,0:T(8,128)(2,1)S(1)} %get-tuple-element.55), channel_id=1, source_target_pairs={{0,2},{2,0},{4,6},{6,4},{1,3},{3,1},{5,7},{7,5},{8,10},{10,8},{12,... | collective-permute-start | bytes 276488 | tf_op jit(solution)/shard_map/ppermute | solution.py:18
  128.1 11.5 %collective-permute-start.17 = (bf16[40,1152]{1,0:T(8,128)(2,1)S(1)}, bf16[40,1152]{1,0:T(8,128)(2,1)S(1)}, u32[]{:S(2)}, u32[]{:S(2)}) collective-permute-start(bf16[40,1152]{1,0:T(8,128)(2,1)S(1)} %fusion.29), channel_id=1, source_target_pairs={{0,32},{32,0},{1,33},{33,1},{2,34},{34,2},{3,35},{35,3},{4,36},{36... | collective-permute-start | bytes 276488 | tf_op jit(solution)/shard_map/ppermute | solution.py:18
  141.0 17.1 %collective-permute-start.21 = (bf16[64,1152]{1,0:T(8,128)(2,1)}, bf16[64,1152]{1,0:T(8,128)(2,1)}, u32[]{:S(2)}, u32[]{:S(2)}) collective-permute-start(bf16[64,1152]{1,0:T(8,128)(2,1)} %get-tuple-element.60), channel_id=1, source_target_pairs={{0,4},{2,6},{4,0},{6,2},{1,5},{3,7},{5,1},{7,3},{8,12},{10,14},{12... | collective-permute-start | bytes 442376 | tf_op jit(solution)/shard_map/ppermute | solution.py:18
  144.6 12.6 %collective-permute-start.18 = (bf16[40,1152]{1,0:T(8,128)(2,1)}, bf16[40,1152]{1,0:T(8,128)(2,1)}, u32[]{:S(2)}, u32[]{:S(2)}) collective-permute-start(bf16[40,1152]{1,0:T(8,128)(2,1)} %reduce-precision_convert_fusion.9), channel_id=1, source_target_pairs={{0,128},{64,192},{128,0},{192,64},{256,384},{320,448},{384,256},{4... | collective-permute-start | bytes 276488 | tf_op jit(solution)/shard_map/ppermute | solution.py:18
  147.0 10.1 %collective-permute-start.19 = (bf16[40,1152]{1,0:T(8,128)(2,1)}, bf16[40,1152]{1,0:T(8,128)(2,1)}, u32[]{:S(2)}, u32[]{:S(2)}) collective-permute-start(bf16[40,1152]{1,0:T(8,128)(2,1)} %reduce-precision_convert_fusion.9), channel_id=1, source_target_pairs={{0,192},{64,128},{128,64},{192,0},{256,448},{320,384},{384,320},{4... | collective-permute-start | bytes 276488 | tf_op jit(solution)/shard_map/ppermute | solution.py:18
  151.3 6.8 %collective-permute-start.20 = (bf16[40,1152]{1,0:T(8,128)(2,1)}, bf16[40,1152]{1,0:T(8,128)(2,1)}, u32[]{:S(2)}, u32[]{:S(2)}) collective-permute-start(bf16[40,1152]{1,0:T(8,128)(2,1)} %reduce-precision_convert_fusion.9), channel_id=1, source_target_pairs={{0,64},{64,0},{128,192},{192,128},{256,320},{320,256},{384,448},{4... | collective-permute-start | bytes 276488 | tf_op jit(solution)/shard_map/ppermute | solution.py:18
  154.0 25.7 %collective-permute-start.24 = (bf16[64,1152]{1,0:T(8,128)(2,1)}, bf16[64,1152]{1,0:T(8,128)(2,1)S(1)}, u32[]{:S(2)}, u32[]{:S(2)}) collective-permute-start(bf16[64,1152]{1,0:T(8,128)(2,1)} %get-tuple-element.58), channel_id=1, source_target_pairs={{0,4},{2,6},{4,0},{6,2},{1,5},{3,7},{5,1},{7,3},{8,12},{10,14},{12... | collective-permute-start | bytes 442376 | tf_op jit(solution)/shard_map/ppermute | solution.py:18
  159.2 32.8 %copy-start.2 = (f32[384,1152]{1,0:T(8,128)S(1)}, f32[384,1152]{1,0:T(8,128)}, u32[]{:S(2)}) copy-start(f32[384,1152]{1,0:T(8,128)} %copy-done.1) | copy-start | bytes 5308420
  159.2 20.5 %collective-permute-start.22 = (bf16[40,1152]{1,0:T(8,128)(2,1)S(1)}, bf16[40,1152]{1,0:T(8,128)(2,1)S(1)}, u32[]{:S(2)}, u32[]{:S(2)}) collective-permute-start(bf16[40,1152]{1,0:T(8,128)(2,1)S(1)} %reduce-precision_convert_fusion.8), channel_id=1, source_target_pairs={{0,512},{64,576},{128,640},{192,704},{256,0},{320,64},{384,128},{4... | collective-permute-start | bytes 276488 | tf_op jit(solution)/shard_map/ppermute | solution.py:23
  171.0 12.9 %collective-permute-start.23 = (bf16[40,1152]{1,0:T(8,128)(2,1)S(1)}, bf16[40,1152]{1,0:T(8,128)(2,1)S(1)}, u32[]{:S(2)}, u32[]{:S(2)}) collective-permute-start(bf16[40,1152]{1,0:T(8,128)(2,1)S(1)} %reduce-precision_convert_fusion.8), channel_id=1, source_target_pairs={{0,256},{64,320},{128,384},{192,448},{256,512},{320,576},{384,640}... | collective-permute-start | bytes 276488 | tf_op jit(solution)/shard_map/ppermute | solution.py:23
  175.9 16.0 %collective-permute-start.25 = (bf16[64,1152]{1,0:T(8,128)(2,1)S(1)}, bf16[64,1152]{1,0:T(8,128)(2,1)S(1)}, u32[]{:S(2)}, u32[]{:S(2)}) collective-permute-start(bf16[64,1152]{1,0:T(8,128)(2,1)S(1)} %copy-done.13), channel_id=1, source_target_pairs={{0,4},{2,6},{4,0},{6,2},{1,5},{3,7},{5,1},{7,3},{8,12},{10,14},{12... | collective-permute-start | bytes 442376 | tf_op jit(solution)/shard_map/ppermute | solution.py:18
  184.0 11.3 %collective-permute-start.26 = (bf16[40,1152]{1,0:T(8,128)(2,1)S(1)}, bf16[40,1152]{1,0:T(8,128)(2,1)S(1)}, u32[]{:S(2)}, u32[]{:S(2)}) collective-permute-start(bf16[40,1152]{1,0:T(8,128)(2,1)S(1)} %reduce-precision_convert_fusion.7), channel_id=1, source_target_pairs={{0,16},{8,24},{16,0},{24,8},{1,17},{9,25},{17,1},{25,9},{2,18},{10... | collective-permute-start | bytes 276488 | tf_op jit(solution)/shard_map/ppermute | solution.py:23
  186.1 9.3 %collective-permute-start.28 = (bf16[40,1152]{1,0:T(8,128)(2,1)S(1)}, bf16[40,1152]{1,0:T(8,128)(2,1)S(1)}, u32[]{:S(2)}, u32[]{:S(2)}) collective-permute-start(bf16[40,1152]{1,0:T(8,128)(2,1)S(1)} %reduce-precision_convert_fusion.7), channel_id=1, source_target_pairs={{0,24},{8,0},{16,8},{24,16},{1,25},{9,1},{17,9},{25,17},{2,26},{10... | collective-permute-start | bytes 276488 | tf_op jit(solution)/shard_map/ppermute | solution.py:23
  189.2 7.7 %collective-permute-start.27 = (bf16[40,1152]{1,0:T(8,128)(2,1)S(1)}, bf16[40,1152]{1,0:T(8,128)(2,1)S(1)}, u32[]{:S(2)}, u32[]{:S(2)}) collective-permute-start(bf16[40,1152]{1,0:T(8,128)(2,1)S(1)} %reduce-precision_convert_fusion.7), channel_id=1, source_target_pairs={{0,8},{8,16},{16,24},{24,0},{1,9},{9,17},{17,25},{25,1},{2,10},{10... | collective-permute-start | bytes 276488 | tf_op jit(solution)/shard_map/ppermute | solution.py:23
  (13 other events, 201.0 us)

commit v6 on v4

--- a/solution.py
+++ b/solution.py
@@ -62,15 +62,13 @@
     rows = pictures.shape[0]
     z, x, y, k = (lax.axis_index(a) for a in ("z", "x", "y", "k"))
 
-    paired, moved_half = shifted(captions, x)
+    paired = turn_col(captions)
     picture = pictures.astype(f32)
     image_scale = lax.rsqrt(jnp.sum(picture * picture, -1, keepdims=True) + eps)
     image_unit = picture * image_scale
     image_low = image_unit.astype(bf16)
-    image_out, _ = tie(image_low, moved_half)
-    image_far = swap(image_out, "y", 2)
-    image_core = swap(image_out, "k", 1)
-    images = jnp.concatenate([image_low, image_far, image_core, swap(image_far, "k", 1)])
+    pair = jnp.concatenate([image_low, swap(image_low, "y", 2)])
+    images = jnp.concatenate([pair, swap(pair, "k", 1)])
     texts = jnp.concatenate([paired, swap(paired, "y", 1)])
 
     projected = dot(texts, matrix, 1, 0) + intercept
@@ -107,7 +105,7 @@
     parts = [lax.dynamic_index_in_dim(p, x, 0, keepdims=False) for p in parts] + over_x
     parts = [p.reshape(4, PAD, D) for p in parts]
     over_y = {m: swap(low(pick(parts, y ^ m)), "y", m) for m in (2, 3, 1)}
-    *over_y, image_core = tie(*over_y.values(), image_core)
+    over_y = list(over_y.values())
     total = pick(parts, y)
     for other in over_y:
         total = total + other.astype(f32)
@@ -116,12 +114,13 @@
 
     image_out = (image_kept[rows:] + image_core[rows:].astype(f32)).astype(bf16)
     head, image_out = tie(head, image_out)
-    third = rows // 3
-    far = [swap(image_out[i * third : (i + 1) * third], "y", 2) for i in range(3)]
+    far = [swap(image_out[: rows // 2], "y", 2)]
     over_z = [swap(head, "z", m) for m in (2, 3, 1)]
     *over_z, far[0] = tie(*over_z, far[0])
     over_z = [other.astype(f32) for other in over_z]
     head = low((head.astype(f32) + over_z[2]) + (over_z[0] + over_z[1]))
+    head, image_late = tie(head, image_out[rows // 2 :])
+    far.append(swap(image_late, "y", 2))
     over_z = [turn(head, "z", 8), turn(head, "z", 4)]
     *over_z, far[1] = tie(*over_z, far[1])
     ring = [head] + over_z
@@ -146,20 +145,8 @@
     return (image_grad, text_grad, head_grad, bias_grad)
 
 
-def shifted(block, x):
-    def cross(half, plane):
-        pairs = []
-        for group in range(plane, 96, 4):
-            pairs.append((group, (group + 4) % 96))
-        return lax.ppermute(half, COL, pairs)
-
-    half = block.shape[0] // 2
-    low_half, high_half = tie(block[:half], block[half:])
-    crossed = cross(high_half, 3)
-    moved = turn(low_half, "x", 1)
-    first = jnp.where(x == 0, cross(moved, 0), moved)
-    second = turn(jnp.where(x == 3, crossed, high_half), "x", 1)
-    return jnp.concatenate([first, second]), moved
+def turn_col(block):
+    return lax.ppermute(block, COL, [((i - 1) % 96, i) for i in range(96)])
 
 
 def solution(mesh):

time: 199 us -> 193 us (0.970)
  other arithmetic: 17.1 us -> 14.7 us
  waiting for transfers between devices: 48.9 us -> 46.7 us
    ppermute x10 -> x8, waiting for transfers between devices: 26.8 us -> 17.8 us  [turn(): lax.ppermute(block, axis, [(i, (i + distance) % n) for i in range(n)])]
    ppermute x2 -> x1, waiting for transfers between devices: 2.1 us -> 9.07 us  [turn_col(): return lax.ppermute(block, COL, [((i - 1) % 96, i) for i in range(96)])]
    ppermute x2 -> x1, starting transfers between devices: 6.38 us -> 3.66 us  [turn_col(): return lax.ppermute(block, COL, [((i - 1) % 96, i) for i in range(96)])]
    ppermute x10 -> x8, starting transfers between devices: 37 us -> 39.7 us  [turn(): lax.ppermute(block, axis, [(i, (i + distance) % n) for i in range(n)])]
    ppermute x17 -> x15, starting transfers between devices: 61 us -> 60.3 us  [swap(): return lax.ppermute(block, axis, [(i, i ^ mask) for i in range(n)])]
    ppermute x17 -> x15, waiting for transfers between devices: 20 us -> 19.8 us  [swap(): return lax.ppermute(block, axis, [(i, i ^ mask) for i in range(n)])]
  transfers between devices with their start and end apart: 29 -> 24, of which waited for: 11 -> 13; matrix products, arithmetic and copies ran while one was open for 14% -> 14% of each run, Pallas kernels for 0% -> 0%
where the time goes in v6:
time: 193 us; the launch traced here: 191 us
  starting transfers between devices  104 us (54%)
  waiting for transfers between devices  46.7 us (24%)
  matrix products  18.8 us (10%)
  other arithmetic  14.7 us (8%)
  local copies, waits for them, and re-layouts  4.86 us (3%)
  between operations  2.75 us (1%)
    ppermute x15, starting transfers between devices, swap(): return lax.ppermute(block, axis, [(i, i ^ mask) for i in range(n)])  60.3 us
    ppermute x8, starting transfers between devices, turn(): lax.ppermute(block, axis, [(i, (i + distance) % n) for i in range(n)])  39.7 us
    ppermute x15, waiting for transfers between devices, swap(): return lax.ppermute(block, axis, [(i, i ^ mask) for i in range(n)])  19.8 us
    dot_general x10, matrix products, dot(): lax.dot_general(a, b, (((ca,), (cb,)), ((), ())), preferred_element_type=...  18.8 us
    ppermute x8, waiting for transfers between devices, turn(): lax.ppermute(block, axis, [(i, (i + distance) % n) for i in range(n)])  17.8 us
    ppermute x1, waiting for transfers between devices, turn_col(): return lax.ppermute(block, COL, [((i - 1) % 96, i) for i in range(96)])  9.07 us
    convert_element_type x7, other arithmetic, low(): return lax.reduce_precision(values, 8, 7).astype(bf16)  5.78 us
  transfers between devices with their start and end apart: 24, of which 13 were waited for; matrix products, arithmetic and copies ran while one was open for 14% of the time, Pallas kernels for 0%

profile of v6, /device:TPU:56, one launch (start us, length us, event | category | flops | bytes accessed | tf_op | source)
XLA Modules:
  0.0 191.5 jit_solution(6228725987138274496)
XLA Ops:
  0.6 3.7 %collective-permute-start.2 = (bf16[192,1152]{1,0:T(8,128)(2,1)}, bf16[192,1152]{1,0:T(8,128)(2,1)}, u32[]{:S(2)}, u32[]{:S(2)}) collective-permute-start(bf16[192,1152]{1,0:T(8,128)(2,1)} %param.8), channel_id=1, source_target_pairs={{760,0},{0,8},{8,16},{16,24},{24,32},{32,40},{40,48},{48,56},{56,6... | collective-permute-start | bytes 1327112 | tf_op jit(solution)/shard_map/ppermute | solution.py:149
  6.7 4.0 %collective-permute-start = (bf16[192,1152]{1,0:T(8,128)(2,1)S(1)}, bf16[192,1152]{1,0:T(8,128)(2,1)S(1)}, u32[]{:S(2)}, u32[]{:S(2)}) collective-permute-start(bf16[192,1152]{1,0:T(8,128)(2,1)S(1)} %fusion.15), channel_id=1, source_target_pairs={{0,4},{2,6},{4,0},{6,2},{1,5},{3,7},{5,1},{7,3},{8,12},{10,14},{12... | collective-permute-start | bytes 1327112 | tf_op jit(solution)/shard_map/ppermute | solution.py:18
  13.3 9.1 %collective-permute-done.2 = bf16[192,1152]{1,0:T(8,128)(2,1)} collective-permute-done((bf16[192,1152]{1,0:T(8,128)(2,1)}, bf16[192,1152]{1,0:T(8,128)(2,1)}, u32[]{:S(2)}, u32[]{:S(2)}) %collective-permute-start.2) | collective-permute-done | bytes 442400 | tf_op jit(solution)/shard_map/ppermute | solution.py:149
  22.3 18.6 %collective-permute-start.3 = (bf16[192,1152]{1,0:T(8,128)(2,1)}, bf16[192,1152]{1,0:T(8,128)(2,1)S(1)}, u32[]{:S(2)}, u32[]{:S(2)}) collective-permute-start(bf16[192,1152]{1,0:T(8,128)(2,1)} %collective-permute-done.2), channel_id=1, source_target_pairs={{0,2},{2,0},{4,6},{6,4},{1,3},{3,1},{5,7},{7,5},{8,10},{10,8},{12,... | collective-permute-start | bytes 1327112 | tf_op jit(solution)/shard_map/ppermute | solution.py:18
  41.1 1.9 %collective-permute-start.1 = (bf16[384,1152]{1,0:T(8,128)(2,1)S(1)}, bf16[384,1152]{1,0:T(8,128)(2,1)S(1)}, u32[]{:S(2)}, u32[]{:S(2)}) collective-permute-start(bf16[384,1152]{1,0:T(8,128)(2,1)S(1)} %pad_maximum_fusion.1), channel_id=1, source_target_pairs={{0,1},{1,0},{2,3},{3,2},{4,5},{5,4},{6,7},{7,6},{8,9},{9,8},{10,11... | collective-permute-start | bytes 2654216 | tf_op jit(solution)/shard_map/ppermute | solution.py:18
  44.0 5.1 %collective-permute-done.3 = bf16[192,1152]{1,0:T(8,128)(2,1)S(1)} collective-permute-done((bf16[192,1152]{1,0:T(8,128)(2,1)}, bf16[192,1152]{1,0:T(8,128)(2,1)S(1)}, u32[]{:S(2)}, u32[]{:S(2)}) %collective-permute-start.3) | collective-permute-done | bytes 442400 | tf_op jit(solution)/shard_map/ppermute | solution.py:18
  54.4 2.6 %fusion.12 = bf16[768,384]{1,0:T(8,128)(2,1)S(1)} fusion(bf16[384,1152]{1,0:T(8,128)(2,1)S(1)} %multiply_convert_fusion, bf16[384,1152]{1,0:T(8,128)(2,1)S(1)} %collective-permute-done.1, bf16[192,1152]{1,0:T(8,128)(2,1)S(1)} %collective-permute-done, bf16[192,1152]{1,0:T(8,128)(2,1)S(1)} %copy-done.8, f32[]{:T(128)} %bitcast.53, f32[]{:T(128)} %bitcast.50, ...), kind=kOutput, calls=%fused_computation.28 | convolution fusion | flops 688029696 | bytes 3247112 | tf_op jit(solution)/shard_map/dot_general | solution.py:31
  58.5 2.1 %convolution_convert_fusion = bf16[640,1152]{1,0:T(8,128)(2,1)} fusion(bf16[384,640]{1,0:T(8,128)(2,1)S(1)} %fusion.8, bf16[384,1152]{1,0:T(8,128)(2,1)S(1)} %reduce-precision_convert_fusion), kind=kOutput, calls=%fused_computation | convolution fusion | flops 566968320 | bytes 2850816 | tf_op jit(solution)/shard_map/dot_general | solution.py:31
  62.7 3.8 %collective-permute-start.8 = (bf16[192,1152]{1,0:T(8,128)(2,1)S(1)}, bf16[192,1152]{1,0:T(8,128)(2,1)S(1)}, u32[]{:S(2)}, u32[]{:S(2)}) collective-permute-start(bf16[192,1152]{1,0:T(8,128)(2,1)S(1)} %slice.63), channel_id=1, source_target_pairs={{0,2},{2,0},{4,6},{6,4},{1,3},{3,1},{5,7},{7,5},{8,10},{10,8},{12,... | collective-permute-start | bytes 1327112 | tf_op jit(solution)/shard_map/ppermute | solution.py:18
  66.5 2.8 %fusion.2 = bf16[384,1152]{1,0:T(8,128)(2,1)} fusion(bf16[384,1152]{1,0:T(8,128)(2,1)} %copy-done.4, f32[]{:T(128)} %bitcast.51, bf16[768,384]{1,0:T(8,128)(2,1)} %copy-done.16), kind=kOutput, calls=%fused_computation.10 | convolution fusion | flops 340623360 | bytes 2064896 | tf_op jit(solution)/shard_map/dot_general | solution.py:31
  71.8 1.9 %collective-permute-start.5 = (bf16[160,1152]{1,0:T(8,128)(2,1)S(1)}, bf16[160,1152]{1,0:T(8,128)(2,1)S(1)}, u32[]{:S(2)}, u32[]{:S(2)}) collective-permute-start(bf16[160,1152]{1,0:T(8,128)(2,1)S(1)} %get-tuple-element.42), channel_id=1, source_target_pairs={{0,16},{8,24},{16,0},{24,8},{1,17},{9,25},{17,1},{25,9},{2,18},{10... | collective-permute-start | bytes 1105928 | tf_op jit(solution)/shard_map/ppermute | solution.py:23
  73.8 9.7 %collective-permute-start.6 = (bf16[160,1152]{1,0:T(8,128)(2,1)S(1)}, bf16[160,1152]{1,0:T(8,128)(2,1)S(1)}, u32[]{:S(2)}, u32[]{:S(2)}) collective-permute-start(bf16[160,1152]{1,0:T(8,128)(2,1)S(1)} %get-tuple-element.41), channel_id=1, source_target_pairs={{0,8},{8,16},{16,24},{24,0},{1,9},{9,17},{17,25},{25,1},{2,10},{10... | collective-permute-start | bytes 1105928 | tf_op jit(solution)/shard_map/ppermute | solution.py:23
  83.5 1.9 %collective-permute-start.7 = (bf16[160,1152]{1,0:T(8,128)(2,1)S(1)}, bf16[160,1152]{1,0:T(8,128)(2,1)S(1)}, u32[]{:S(2)}, u32[]{:S(2)}) collective-permute-start(bf16[160,1152]{1,0:T(8,128)(2,1)S(1)} %get-tuple-element.40), channel_id=1, source_target_pairs={{0,24},{8,0},{16,8},{24,16},{1,25},{9,1},{17,9},{25,17},{2,26},{10... | collective-permute-start | bytes 1105928 | tf_op jit(solution)/shard_map/ppermute | solution.py:23
  86.7 7.2 %collective-permute-done.6 = bf16[160,1152]{1,0:T(8,128)(2,1)S(1)} collective-permute-done((bf16[160,1152]{1,0:T(8,128)(2,1)S(1)}, bf16[160,1152]{1,0:T(8,128)(2,1)S(1)}, u32[]{:S(2)}, u32[]{:S(2)}) %collective-permute-start.6) | collective-permute-done | bytes 368672 | tf_op jit(solution)/shard_map/ppermute | solution.py:23
  93.9 4.6 %collective-permute-done.7 = bf16[160,1152]{1,0:T(8,128)(2,1)S(1)} collective-permute-done((bf16[160,1152]{1,0:T(8,128)(2,1)S(1)}, bf16[160,1152]{1,0:T(8,128)(2,1)S(1)}, u32[]{:S(2)}, u32[]{:S(2)}) %collective-permute-start.7) | collective-permute-done | bytes 368672 | tf_op jit(solution)/shard_map/ppermute | solution.py:23
  99.3 3.6 %collective-permute-start.12 = (bf16[40,1152]{1,0:T(8,128)(2,1)}, bf16[40,1152]{1,0:T(8,128)(2,1)}, u32[]{:S(2)}, u32[]{:S(2)}) collective-permute-start(bf16[40,1152]{1,0:T(8,128)(2,1)} %get-tuple-element.44), channel_id=1, source_target_pairs={{0,2},{2,0},{4,6},{6,4},{1,3},{3,1},{5,7},{7,5},{8,10},{10,8},{12,... | collective-permute-start | bytes 276488 | tf_op jit(solution)/shard_map/ppermute | solution.py:18
  103.0 4.3 %collective-permute-start.11 = (bf16[40,1152]{1,0:T(8,128)(2,1)}, bf16[40,1152]{1,0:T(8,128)(2,1)}, u32[]{:S(2)}, u32[]{:S(2)}) collective-permute-start(bf16[40,1152]{1,0:T(8,128)(2,1)} %get-tuple-element.45), channel_id=1, source_target_pairs={{0,6},{2,4},{4,2},{6,0},{1,7},{3,5},{5,3},{7,1},{8,14},{10,12},{12... | collective-permute-start | bytes 276488 | tf_op jit(solution)/shard_map/ppermute | solution.py:18
  107.3 1.9 %collective-permute-start.10 = (bf16[40,1152]{1,0:T(8,128)(2,1)}, bf16[40,1152]{1,0:T(8,128)(2,1)}, u32[]{:S(2)}, u32[]{:S(2)}) collective-permute-start(bf16[40,1152]{1,0:T(8,128)(2,1)} %get-tuple-element.43), channel_id=1, source_target_pairs={{0,4},{2,6},{4,0},{6,2},{1,5},{3,7},{5,1},{7,3},{8,12},{10,14},{12... | collective-permute-start | bytes 276488 | tf_op jit(solution)/shard_map/ppermute | solution.py:18
  112.6 2.9 %collective-permute-done.10 = bf16[40,1152]{1,0:T(8,128)(2,1)} collective-permute-done((bf16[40,1152]{1,0:T(8,128)(2,1)}, bf16[40,1152]{1,0:T(8,128)(2,1)}, u32[]{:S(2)}, u32[]{:S(2)}) %collective-permute-start.10) | collective-permute-done | bytes 92192 | tf_op jit(solution)/shard_map/ppermute | solution.py:18
  116.8 3.2 %collective-permute-start.13 = (bf16[40,1152]{1,0:T(8,128)(2,1)S(1)}, bf16[40,1152]{1,0:T(8,128)(2,1)S(1)}, u32[]{:S(2)}, u32[]{:S(2)}) collective-permute-start(bf16[40,1152]{1,0:T(8,128)(2,1)S(1)} %fusion.32), channel_id=1, source_target_pairs={{0,32},{32,0},{1,33},{33,1},{2,34},{34,2},{3,35},{35,3},{4,36},{36... | collective-permute-start | bytes 276488 | tf_op jit(solution)/shard_map/ppermute | solution.py:18
  121.9 5.7 %collective-permute-done.13 = bf16[40,1152]{1,0:T(8,128)(2,1)S(1)} collective-permute-done((bf16[40,1152]{1,0:T(8,128)(2,1)S(1)}, bf16[40,1152]{1,0:T(8,128)(2,1)S(1)}, u32[]{:S(2)}, u32[]{:S(2)}) %collective-permute-start.13) | collective-permute-done | bytes 92192 | tf_op jit(solution)/shard_map/ppermute | solution.py:18
  131.9 1.9 %collective-permute-start.14 = (bf16[40,1152]{1,0:T(8,128)(2,1)}, bf16[40,1152]{1,0:T(8,128)(2,1)}, u32[]{:S(2)}, u32[]{:S(2)}) collective-permute-start(bf16[40,1152]{1,0:T(8,128)(2,1)} %reduce-precision_convert_fusion.9), channel_id=1, source_target_pairs={{0,128},{64,192},{128,0},{192,64},{256,384},{320,448},{384,256},{4... | collective-permute-start | bytes 276488 | tf_op jit(solution)/shard_map/ppermute | solution.py:18
  133.8 3.3 %collective-permute-start.15 = (bf16[40,1152]{1,0:T(8,128)(2,1)}, bf16[40,1152]{1,0:T(8,128)(2,1)}, u32[]{:S(2)}, u32[]{:S(2)}) collective-permute-start(bf16[40,1152]{1,0:T(8,128)(2,1)} %reduce-precision_convert_fusion.9), channel_id=1, source_target_pairs={{0,192},{64,128},{128,64},{192,0},{256,448},{320,384},{384,320},{4... | collective-permute-start | bytes 276488 | tf_op jit(solution)/shard_map/ppermute | solution.py:18
  137.1 4.0 %collective-permute-start.16 = (bf16[40,1152]{1,0:T(8,128)(2,1)}, bf16[40,1152]{1,0:T(8,128)(2,1)}, u32[]{:S(2)}, u32[]{:S(2)}) collective-permute-start(bf16[40,1152]{1,0:T(8,128)(2,1)} %reduce-precision_convert_fusion.9), channel_id=1, source_target_pairs={{0,64},{64,0},{128,192},{192,128},{256,320},{320,256},{384,448},{4... | collective-permute-start | bytes 276488 | tf_op jit(solution)/shard_map/ppermute | solution.py:18
  145.2 13.3 %collective-permute-start.18 = (bf16[40,1152]{1,0:T(8,128)(2,1)S(1)}, bf16[40,1152]{1,0:T(8,128)(2,1)S(1)}, u32[]{:S(2)}, u32[]{:S(2)}) collective-permute-start(bf16[40,1152]{1,0:T(8,128)(2,1)S(1)} %reduce-precision_convert_fusion.8), channel_id=1, source_target_pairs={{0,512},{64,576},{128,640},{192,704},{256,0},{320,64},{384,128},{4... | collective-permute-start | bytes 276488 | tf_op jit(solution)/shard_map/ppermute | solution.py:23
  160.4 4.0 %collective-permute-start.20 = (bf16[96,1152]{1,0:T(8,128)(2,1)}, bf16[96,1152]{1,0:T(8,128)(2,1)S(1)}, u32[]{:S(2)}, u32[]{:S(2)}) collective-permute-start(bf16[96,1152]{1,0:T(8,128)(2,1)} %get-tuple-element.35), channel_id=1, source_target_pairs={{0,4},{2,6},{4,0},{6,2},{1,5},{3,7},{5,1},{7,3},{8,12},{10,14},{12... | collective-permute-start | bytes 663560 | tf_op jit(solution)/shard_map/ppermute | solution.py:18
  164.4 3.0 %fusion.22 = f32[192,1152]{1,0:T(8,128)} fusion(bf16[1152,1152]{1,0:T(8,128)(2,1)S(1)} %copy-done, bf16[192,1152]{1,0:T(8,128)(2,1)} %copy-done.12, bf16[384,1152]{1,0:T(8,128)(2,1)S(1)} %reduce-precision_convert_fusion), kind=kOutput, calls=%fused_computation.48 | convolution fusion | flops 510492672 | bytes 4423680 | tf_op jit(solution)/shard_map/dot_general | solution.py:31
  167.4 4.3 %collective-permute-done.19 = bf16[40,1152]{1,0:T(8,128)(2,1)S(1)} collective-permute-done((bf16[40,1152]{1,0:T(8,128)(2,1)S(1)}, bf16[40,1152]{1,0:T(8,128)(2,1)S(1)}, u32[]{:S(2)}, u32[]{:S(2)}) %collective-permute-start.19) | collective-permute-done | bytes 92192 | tf_op jit(solution)/shard_map/ppermute | solution.py:23
  173.7 2.9 %collective-permute-start.21 = (bf16[40,1152]{1,0:T(8,128)(2,1)S(1)}, bf16[40,1152]{1,0:T(8,128)(2,1)S(1)}, u32[]{:S(2)}, u32[]{:S(2)}) collective-permute-start(bf16[40,1152]{1,0:T(8,128)(2,1)S(1)} %reduce-precision_convert_fusion.7), channel_id=1, source_target_pairs={{0,16},{8,24},{16,0},{24,8},{1,17},{9,25},{17,1},{25,9},{2,18},{10... | collective-permute-start | bytes 276488 | tf_op jit(solution)/shard_map/ppermute | solution.py:23
  176.6 5.5 %collective-permute-start.23 = (bf16[40,1152]{1,0:T(8,128)(2,1)S(1)}, bf16[40,1152]{1,0:T(8,128)(2,1)S(1)}, u32[]{:S(2)}, u32[]{:S(2)}) collective-permute-start(bf16[40,1152]{1,0:T(8,128)(2,1)S(1)} %reduce-precision_convert_fusion.7), channel_id=1, source_target_pairs={{0,24},{8,0},{16,8},{24,16},{1,25},{9,1},{17,9},{25,17},{2,26},{10... | collective-permute-start | bytes 276488 | tf_op jit(solution)/shard_map/ppermute | solution.py:23
  182.1 2.5 %collective-permute-start.22 = (bf16[40,1152]{1,0:T(8,128)(2,1)S(1)}, bf16[40,1152]{1,0:T(8,128)(2,1)S(1)}, u32[]{:S(2)}, u32[]{:S(2)}) collective-permute-start(bf16[40,1152]{1,0:T(8,128)(2,1)S(1)} %reduce-precision_convert_fusion.7), channel_id=1, source_target_pairs={{0,8},{8,16},{16,24},{24,0},{1,9},{9,17},{17,25},{25,1},{2,10},{10... | collective-permute-start | bytes 276488 | tf_op jit(solution)/shard_map/ppermute | solution.py:23
  185.9 2.1 %fusion.18 = f32[192,1152]{1,0:T(8,128)} fusion(bf16[192,1152]{1,0:T(8,128)(2,1)S(1)} %copy-done.3, f32[192]{0:T(256)S(1)} %fusion.16, f32[192]{0:T(256)S(1)} %add_rsqrt_fusion.1, bf16[96,1152]{1,0:T(8,128)(2,1)S(1)} %collective-permute-done.20, bf16[96,1152]{1,0:T(8,128)(2,1)} %collective-permute-done.17, bf16[384,1152]{1,0:T(8,128)(2,1)S(1)} %copy-done.6, ...), kind=kLoop, calls=%fused_computation.37 | loop fusion | flops 2654208 | bytes 3098112 | tf_op jit(solution)/shard_map/mul | solution.py:144
  (97 shorter events, 41.2 us)
Async XLA Ops:
  0.6 49.5 %copy-start = (bf16[1152,1152]{1,0:T(8,128)(2,1)S(1)}, bf16[1152,1152]{1,0:T(8,128)(2,1)}, u32[]{:S(2)}) copy-start(bf16[1152,1152]{1,0:T(8,128)(2,1)} %param.10) | copy-start | bytes 7962628
  0.6 21.7 %collective-permute-start.2 = (bf16[192,1152]{1,0:T(8,128)(2,1)}, bf16[192,1152]{1,0:T(8,128)(2,1)}, u32[]{:S(2)}, u32[]{:S(2)}) collective-permute-start(bf16[192,1152]{1,0:T(8,128)(2,1)} %param.8), channel_id=1, source_target_pairs={{760,0},{0,8},{8,16},{16,24},{24,32},{32,40},{40,48},{48,56},{56,6... | collective-permute-start | bytes 1327112 | tf_op jit(solution)/shard_map/ppermute | solution.py:149
  6.7 34.4 %copy-start.7 = (bf16[192,1152]{1,0:T(8,128)(2,1)}, bf16[192,1152]{1,0:T(8,128)(2,1)S(1)}, u32[]{:S(2)}) copy-start(bf16[192,1152]{1,0:T(8,128)(2,1)S(1)} %fusion.15) | copy-start | bytes 1327108
  6.7 34.3 %collective-permute-start = (bf16[192,1152]{1,0:T(8,128)(2,1)S(1)}, bf16[192,1152]{1,0:T(8,128)(2,1)S(1)}, u32[]{:S(2)}, u32[]{:S(2)}) collective-permute-start(bf16[192,1152]{1,0:T(8,128)(2,1)S(1)} %fusion.15), channel_id=1, source_target_pairs={{0,4},{2,6},{4,0},{6,2},{1,5},{3,7},{5,1},{7,3},{8,12},{10,14},{12... | collective-permute-start | bytes 1327112 | tf_op jit(solution)/shard_map/ppermute | solution.py:18
  22.3 26.8 %collective-permute-start.3 = (bf16[192,1152]{1,0:T(8,128)(2,1)}, bf16[192,1152]{1,0:T(8,128)(2,1)S(1)}, u32[]{:S(2)}, u32[]{:S(2)}) collective-permute-start(bf16[192,1152]{1,0:T(8,128)(2,1)} %collective-permute-done.2), channel_id=1, source_target_pairs={{0,2},{2,0},{4,6},{6,4},{1,3},{3,1},{5,7},{7,5},{8,10},{10,8},{12,... | collective-permute-start | bytes 1327112 | tf_op jit(solution)/shard_map/ppermute | solution.py:18
  41.1 12.5 %collective-permute-start.1 = (bf16[384,1152]{1,0:T(8,128)(2,1)S(1)}, bf16[384,1152]{1,0:T(8,128)(2,1)S(1)}, u32[]{:S(2)}, u32[]{:S(2)}) collective-permute-start(bf16[384,1152]{1,0:T(8,128)(2,1)S(1)} %pad_maximum_fusion.1), channel_id=1, source_target_pairs={{0,1},{1,0},{2,3},{3,2},{4,5},{5,4},{6,7},{7,6},{8,9},{9,8},{10,11... | collective-permute-start | bytes 2654216 | tf_op jit(solution)/shard_map/ppermute | solution.py:18
  60.7 9.7 %collective-permute-start.4 = (bf16[640,1152]{1,0:T(8,128)(2,1)}, bf16[640,1152]{1,0:T(8,128)(2,1)}, u32[]{:S(2)}, u32[]{:S(2)}) collective-permute-start(bf16[640,1152]{1,0:T(8,128)(2,1)} %convolution_convert_fusion), channel_id=1, source_target_pairs={{0,1},{1,0},{2,3},{3,2},{4,5},{5,4},{6,7},{7,6},{8,9},{9,8},{10,11... | collective-permute-start | bytes 4423688 | tf_op jit(solution)/shard_map/ppermute | solution.py:18
  62.7 23.9 %collective-permute-start.8 = (bf16[192,1152]{1,0:T(8,128)(2,1)S(1)}, bf16[192,1152]{1,0:T(8,128)(2,1)S(1)}, u32[]{:S(2)}, u32[]{:S(2)}) collective-permute-start(bf16[192,1152]{1,0:T(8,128)(2,1)S(1)} %slice.63), channel_id=1, source_target_pairs={{0,2},{2,0},{4,6},{6,4},{1,3},{3,1},{5,7},{7,5},{8,10},{10,8},{12,... | collective-permute-start | bytes 1327112 | tf_op jit(solution)/shard_map/ppermute | solution.py:18
  71.8 14.8 %collective-permute-start.5 = (bf16[160,1152]{1,0:T(8,128)(2,1)S(1)}, bf16[160,1152]{1,0:T(8,128)(2,1)S(1)}, u32[]{:S(2)}, u32[]{:S(2)}) collective-permute-start(bf16[160,1152]{1,0:T(8,128)(2,1)S(1)} %get-tuple-element.42), channel_id=1, source_target_pairs={{0,16},{8,24},{16,0},{24,8},{1,17},{9,25},{17,1},{25,9},{2,18},{10... | collective-permute-start | bytes 1105928 | tf_op jit(solution)/shard_map/ppermute | solution.py:23
  73.8 20.1 %collective-permute-start.6 = (bf16[160,1152]{1,0:T(8,128)(2,1)S(1)}, bf16[160,1152]{1,0:T(8,128)(2,1)S(1)}, u32[]{:S(2)}, u32[]{:S(2)}) collective-permute-start(bf16[160,1152]{1,0:T(8,128)(2,1)S(1)} %get-tuple-element.41), channel_id=1, source_target_pairs={{0,8},{8,16},{16,24},{24,0},{1,9},{9,17},{17,25},{25,1},{2,10},{10... | collective-permute-start | bytes 1105928 | tf_op jit(solution)/shard_map/ppermute | solution.py:23
  83.5 14.9 %collective-permute-start.7 = (bf16[160,1152]{1,0:T(8,128)(2,1)S(1)}, bf16[160,1152]{1,0:T(8,128)(2,1)S(1)}, u32[]{:S(2)}, u32[]{:S(2)}) collective-permute-start(bf16[160,1152]{1,0:T(8,128)(2,1)S(1)} %get-tuple-element.40), channel_id=1, source_target_pairs={{0,24},{8,0},{16,8},{24,16},{1,25},{9,1},{17,9},{25,17},{2,26},{10... | collective-permute-start | bytes 1105928 | tf_op jit(solution)/shard_map/ppermute | solution.py:23
  85.5 13.0 %copy-start.9 = (bf16[1,160,1152]{2,1,0:T(8,128)(2,1)}, bf16[1,160,1152]{2,1,0:T(8,128)(2,1)S(1)}, u32[]{:S(2)}) copy-start(bf16[1,160,1152]{2,1,0:T(8,128)(2,1)S(1)} %constant_dynamic-slice_fusion.1) | copy-start | bytes 1105924
  86.6 12.7 %copy-start.10 = (bf16[1,160,1152]{2,1,0:T(8,128)(2,1)}, bf16[1,160,1152]{2,1,0:T(8,128)(2,1)S(1)}, u32[]{:S(2)}) copy-start(bf16[1,160,1152]{2,1,0:T(8,128)(2,1)S(1)} %constant_dynamic-slice_fusion) | copy-start | bytes 1105924
  86.7 16.3 %copy-start.13 = (bf16[160,1152]{1,0:T(8,128)(2,1)}, bf16[160,1152]{1,0:T(8,128)(2,1)S(1)}, u32[]{:S(2)}) copy-start(bf16[160,1152]{1,0:T(8,128)(2,1)S(1)} %collective-permute-done.5) | copy-start | bytes 1105924
  99.3 11.8 %collective-permute-start.12 = (bf16[40,1152]{1,0:T(8,128)(2,1)}, bf16[40,1152]{1,0:T(8,128)(2,1)}, u32[]{:S(2)}, u32[]{:S(2)}) collective-permute-start(bf16[40,1152]{1,0:T(8,128)(2,1)} %get-tuple-element.44), channel_id=1, source_target_pairs={{0,2},{2,0},{4,6},{6,4},{1,3},{3,1},{5,7},{7,5},{8,10},{10,8},{12,... | collective-permute-start | bytes 276488 | tf_op jit(solution)/shard_map/ppermute | solution.py:18
  103.0 9.6 %collective-permute-start.11 = (bf16[40,1152]{1,0:T(8,128)(2,1)}, bf16[40,1152]{1,0:T(8,128)(2,1)}, u32[]{:S(2)}, u32[]{:S(2)}) collective-permute-start(bf16[40,1152]{1,0:T(8,128)(2,1)} %get-tuple-element.45), channel_id=1, source_target_pairs={{0,6},{2,4},{4,2},{6,0},{1,7},{3,5},{5,3},{7,1},{8,14},{10,12},{12... | collective-permute-start | bytes 276488 | tf_op jit(solution)/shard_map/ppermute | solution.py:18
  107.3 8.2 %collective-permute-start.10 = (bf16[40,1152]{1,0:T(8,128)(2,1)}, bf16[40,1152]{1,0:T(8,128)(2,1)}, u32[]{:S(2)}, u32[]{:S(2)}) collective-permute-start(bf16[40,1152]{1,0:T(8,128)(2,1)} %get-tuple-element.43), channel_id=1, source_target_pairs={{0,4},{2,6},{4,0},{6,2},{1,5},{3,7},{5,1},{7,3},{8,12},{10,14},{12... | collective-permute-start | bytes 276488 | tf_op jit(solution)/shard_map/ppermute | solution.py:18
  109.2 19.0 %collective-permute-start.9 = (bf16[384,1152]{1,0:T(8,128)(2,1)}, bf16[384,1152]{1,0:T(8,128)(2,1)S(1)}, u32[]{:S(2)}, u32[]{:S(2)}) collective-permute-start(bf16[384,1152]{1,0:T(8,128)(2,1)} %fusion.2), channel_id=1, source_target_pairs={{0,1},{1,0},{2,3},{3,2},{4,5},{5,4},{6,7},{7,6},{8,9},{9,8},{10,11... | collective-permute-start | bytes 2654216 | tf_op jit(solution)/shard_map/ppermute | solution.py:18
  116.8 10.8 %collective-permute-start.13 = (bf16[40,1152]{1,0:T(8,128)(2,1)S(1)}, bf16[40,1152]{1,0:T(8,128)(2,1)S(1)}, u32[]{:S(2)}, u32[]{:S(2)}) collective-permute-start(bf16[40,1152]{1,0:T(8,128)(2,1)S(1)} %fusion.32), channel_id=1, source_target_pairs={{0,32},{32,0},{1,33},{33,1},{2,34},{34,2},{3,35},{35,3},{4,36},{36... | collective-permute-start | bytes 276488 | tf_op jit(solution)/shard_map/ppermute | solution.py:18
  129.9 14.2 %collective-permute-start.17 = (bf16[96,1152]{1,0:T(8,128)(2,1)}, bf16[96,1152]{1,0:T(8,128)(2,1)}, u32[]{:S(2)}, u32[]{:S(2)}) collective-permute-start(bf16[96,1152]{1,0:T(8,128)(2,1)} %get-tuple-element.47), channel_id=1, source_target_pairs={{0,4},{2,6},{4,0},{6,2},{1,5},{3,7},{5,1},{7,3},{8,12},{10,14},{12... | collective-permute-start | bytes 663560 | tf_op jit(solution)/shard_map/ppermute | solution.py:18
  131.9 9.6 %collective-permute-start.14 = (bf16[40,1152]{1,0:T(8,128)(2,1)}, bf16[40,1152]{1,0:T(8,128)(2,1)}, u32[]{:S(2)}, u32[]{:S(2)}) collective-permute-start(bf16[40,1152]{1,0:T(8,128)(2,1)} %reduce-precision_convert_fusion.9), channel_id=1, source_target_pairs={{0,128},{64,192},{128,0},{192,64},{256,384},{320,448},{384,256},{4... | collective-permute-start | bytes 276488 | tf_op jit(solution)/shard_map/ppermute | solution.py:18
  133.8 9.5 %collective-permute-start.15 = (bf16[40,1152]{1,0:T(8,128)(2,1)}, bf16[40,1152]{1,0:T(8,128)(2,1)}, u32[]{:S(2)}, u32[]{:S(2)}) collective-permute-start(bf16[40,1152]{1,0:T(8,128)(2,1)} %reduce-precision_convert_fusion.9), channel_id=1, source_target_pairs={{0,192},{64,128},{128,64},{192,0},{256,448},{320,384},{384,320},{4... | collective-permute-start | bytes 276488 | tf_op jit(solution)/shard_map/ppermute | solution.py:18
  137.1 7.0 %collective-permute-start.16 = (bf16[40,1152]{1,0:T(8,128)(2,1)}, bf16[40,1152]{1,0:T(8,128)(2,1)}, u32[]{:S(2)}, u32[]{:S(2)}) collective-permute-start(bf16[40,1152]{1,0:T(8,128)(2,1)} %reduce-precision_convert_fusion.9), channel_id=1, source_target_pairs={{0,64},{64,0},{128,192},{192,128},{256,320},{320,256},{384,448},{4... | collective-permute-start | bytes 276488 | tf_op jit(solution)/shard_map/ppermute | solution.py:18
  145.2 39.5 %copy-start.2 = (f32[384,1152]{1,0:T(8,128)S(1)}, f32[384,1152]{1,0:T(8,128)}, u32[]{:S(2)}) copy-start(f32[384,1152]{1,0:T(8,128)} %copy-done.1) | copy-start | bytes 5308420
  145.2 39.5 %copy-start.3 = (bf16[192,1152]{1,0:T(8,128)(2,1)S(1)}, bf16[192,1152]{1,0:T(8,128)(2,1)}, u32[]{:S(2)}) copy-start(bf16[192,1152]{1,0:T(8,128)(2,1)} %param.7) | copy-start | bytes 1327108
  145.2 39.5 %copy-start.6 = (bf16[384,1152]{1,0:T(8,128)(2,1)S(1)}, bf16[384,1152]{1,0:T(8,128)(2,1)}, u32[]{:S(2)}) copy-start(bf16[384,1152]{1,0:T(8,128)(2,1)} %copy-done.5) | copy-start | bytes 2654212
  145.2 22.2 %collective-permute-start.18 = (bf16[40,1152]{1,0:T(8,128)(2,1)S(1)}, bf16[40,1152]{1,0:T(8,128)(2,1)S(1)}, u32[]{:S(2)}, u32[]{:S(2)}) collective-permute-start(bf16[40,1152]{1,0:T(8,128)(2,1)S(1)} %reduce-precision_convert_fusion.8), channel_id=1, source_target_pairs={{0,512},{64,576},{128,640},{192,704},{256,0},{320,64},{384,128},{4... | collective-permute-start | bytes 276488 | tf_op jit(solution)/shard_map/ppermute | solution.py:23
  158.5 13.3 %collective-permute-start.19 = (bf16[40,1152]{1,0:T(8,128)(2,1)S(1)}, bf16[40,1152]{1,0:T(8,128)(2,1)S(1)}, u32[]{:S(2)}, u32[]{:S(2)}) collective-permute-start(bf16[40,1152]{1,0:T(8,128)(2,1)S(1)} %reduce-precision_convert_fusion.8), channel_id=1, source_target_pairs={{0,256},{64,320},{128,384},{192,448},{256,512},{320,576},{384,640}... | collective-permute-start | bytes 276488 | tf_op jit(solution)/shard_map/ppermute | solution.py:23
  160.4 13.2 %collective-permute-start.20 = (bf16[96,1152]{1,0:T(8,128)(2,1)}, bf16[96,1152]{1,0:T(8,128)(2,1)S(1)}, u32[]{:S(2)}, u32[]{:S(2)}) collective-permute-start(bf16[96,1152]{1,0:T(8,128)(2,1)} %get-tuple-element.35), channel_id=1, source_target_pairs={{0,4},{2,6},{4,0},{6,2},{1,5},{3,7},{5,1},{7,3},{8,12},{10,14},{12... | collective-permute-start | bytes 663560 | tf_op jit(solution)/shard_map/ppermute | solution.py:18
  173.7 14.3 %collective-permute-start.21 = (bf16[40,1152]{1,0:T(8,128)(2,1)S(1)}, bf16[40,1152]{1,0:T(8,128)(2,1)S(1)}, u32[]{:S(2)}, u32[]{:S(2)}) collective-permute-start(bf16[40,1152]{1,0:T(8,128)(2,1)S(1)} %reduce-precision_convert_fusion.7), channel_id=1, source_target_pairs={{0,16},{8,24},{16,0},{24,8},{1,17},{9,25},{17,1},{25,9},{2,18},{10... | collective-permute-start | bytes 276488 | tf_op jit(solution)/shard_map/ppermute | solution.py:23
  176.6 11.5 %collective-permute-start.23 = (bf16[40,1152]{1,0:T(8,128)(2,1)S(1)}, bf16[40,1152]{1,0:T(8,128)(2,1)S(1)}, u32[]{:S(2)}, u32[]{:S(2)}) collective-permute-start(bf16[40,1152]{1,0:T(8,128)(2,1)S(1)} %reduce-precision_convert_fusion.7), channel_id=1, source_target_pairs={{0,24},{8,0},{16,8},{24,16},{1,25},{9,1},{17,9},{25,17},{2,26},{10... | collective-permute-start | bytes 276488 | tf_op jit(solution)/shard_map/ppermute | solution.py:23
  182.1 7.7 %collective-permute-start.22 = (bf16[40,1152]{1,0:T(8,128)(2,1)S(1)}, bf16[40,1152]{1,0:T(8,128)(2,1)S(1)}, u32[]{:S(2)}, u32[]{:S(2)}) collective-permute-start(bf16[40,1152]{1,0:T(8,128)(2,1)S(1)} %reduce-precision_convert_fusion.7), channel_id=1, source_target_pairs={{0,8},{8,16},{16,24},{24,0},{1,9},{9,17},{17,25},{25,1},{2,10},{10... | collective-permute-start | bytes 276488 | tf_op jit(solution)/shard_map/ppermute | solution.py:23
  (11 other events, 58.8 us)
